TPU v7x, 32 devices: a whole 2x2x4 slice. The times are simulated.
32 devices in a mesh: enc: 4 (over z), lab: 8 (over y, x, core).
Axes of the slice: x: 2, y: 2, z: 4, core: 2. Of those that a mesh axis runs over, the one named last changes fastest.
Arguments:
- embeddings: bfloat16 [16384, 768], P(('enc', 'lab')), may hold values from -6 to 6
- classifier: float32 [512, 768], P('lab'), may hold values from -0.21875 to 0.21875
- label_valid: int32 [512], P('lab'), may hold values 0 or 1
- shortlist: int32 [16384, 4], P(('enc', 'lab')), may hold values from 0 to 7, all different within a row; in each aligned block of 512 rows (0 to 511, 512 to 1023, ...) at most 384 rows name the same one
- slot_live: int32 [16384, 4], P(('enc', 'lab')), may hold values 0 or 1
- positive: int32 [16384, 4], P(('enc', 'lab')), may hold values from 0 to 63
- negative: int32 [16384, 4, 8], P(('enc', 'lab')), may hold values from 0 to 63
Outputs:
- w_grad: float32 [512, 768], P('lab')
- emb_grad: float32 [16384, 768], P(('enc', 'lab'))
Inputs may be any that keep to these rules, and one draw needn't show every extreme that they name: `shortlist`: each document names 4 different clusters; among the 512 documents of one device no cluster is named by more than 384 documents.
All inputs are finite; a program needn't handle non-finite values. No bound on the sum of `label_valid` or of `slot_live` on one device may be relied on, other than what follows from the above.
Results may differ from a plain program's by a relative error of at most 0.0041.
Values may be sent and summed in bfloat16 or wider, within the bound.
No kernel may reach another device: no remote copies, remote signals or barrier semaphores. Data moves between devices by JAX's collectives and lax.ppermute only.
A program may use at most 128 MiB of HBM per device.

v0:
```python
import math

import jax
import jax.numpy as jnp
from jax import lax
from jax.sharding import PartitionSpec as P


def dense_targets(shortlist, slot_live, positive, negative, clusters, panel):
    labels = jnp.arange(panel, dtype=jnp.int32)
    pos_hot = (positive[..., None] == labels).astype(jnp.float32)
    neg_count = jnp.sum((negative[..., None] == labels).astype(jnp.float32), axis=2)
    live = slot_live.astype(jnp.float32)[..., None]
    slot_weight = live * (pos_hot + neg_count)
    cluster_hot = (shortlist[..., None] == jnp.arange(clusters, dtype=jnp.int32)).astype(
        jnp.float32
    )
    count = shortlist.shape[0]
    weight = jnp.einsum("nsc,nsj->ncj", cluster_hot, slot_weight).reshape(count, clusters * panel)
    target = jnp.einsum("nsc,nsj->ncj", cluster_hot, pos_hot).reshape(count, clusters * panel)
    return (weight.astype(jnp.bfloat16), target.astype(jnp.bfloat16))


def make_absorb(embeddings, weight_all, target_all):

    def absorb(carry, pieces, start):
        w_piece, v_piece = pieces
        weight = weight_all.astype(jnp.float32)
        weight = weight * v_piece.astype(jnp.float32)[None, :]
        target = target_all.astype(jnp.float32)
        logits = lax.dot_general(
            embeddings, w_piece, (((1,), (1,)), ((), ())), preferred_element_type=jnp.float32
        )
        dlogits = (weight * (jax.nn.sigmoid(logits) - target)).astype(jnp.bfloat16)
        grad_acc = jnp.dot(dlogits, w_piece, preferred_element_type=jnp.float32)
        return (grad_acc, dlogits)

    return absorb


def shards(embeddings, classifier, label_valid, shortlist, slot_live, positive, negative):
    lab_count = lax.axis_size("lab")
    enc_count = lax.axis_size("enc")
    docs, width = embeddings.shape
    panel = classifier.shape[0]
    slots = shortlist.shape[1]
    classifier_b = classifier.astype(jnp.bfloat16)
    weight_all, target_all = dense_targets(
        shortlist, slot_live, positive, negative, lab_count, panel
    )
    absorb = make_absorb(embeddings, weight_all, target_all)
    initial = (
        jnp.zeros((docs, width), jnp.float32),
        jnp.zeros((docs, lab_count * panel), jnp.bfloat16),
    )
    emb_grad, scored = absorb(
        initial,
        (
            lax.all_gather(classifier_b, "lab", axis=0, tiled=True),
            lax.all_gather(label_valid.astype(jnp.bfloat16), "lab", axis=0, tiled=True),
        ),
        jnp.int32(0),
    )
    partial_grad = lax.psum_scatter(
        lax.dot_general(
            scored, embeddings, (((0,), (0,)), ((), ())), preferred_element_type=jnp.float32
        ),
        "lab",
        scatter_dimension=0,
        tiled=True,
    )
    scale_factor = 1.0 / math.sqrt(docs * enc_count * slots)
    w_grad = lax.psum(partial_grad, "enc") * scale_factor
    return (w_grad, emb_grad)


def solution(mesh):
    in_specs = (
        P(("enc", "lab"), None),
        P("lab", None),
        P("lab"),
        P(("enc", "lab"), None),
        P(("enc", "lab"), None),
        P(("enc", "lab"), None),
        P(("enc", "lab"), None, None),
    )
    out_specs = (P("lab", None), P(("enc", "lab"), None))
    return jax.shard_map(shards, mesh=mesh, in_specs=in_specs, out_specs=out_specs, check_vma=False)
```

profile of v0, /device:TPU:0, one launch (start us, length us, event | category | flops | bytes accessed | tf_op | source)
XLA Modules:
  0.0 140.5 jit_solution(12652712829992859496)
XLA Ops:
  7.2 0.0 copy-start
  7.2 0.0 reduce-scatter.2.cloned.1.call-start
  7.2 0.9 copy.21
  8.1 1.4 %convert_reduce_fusion = f32[512,4,64]{0,2,1:T(8,128)S(1)} fusion(s32[512,4,8]{0,2,1:T(8,128)} %param.13), kind=kLoop, calls=%fused_computation | loop fusion | flops 3014656 | bytes 589824 | tf_op jit(solution)/shard_map/reduce_sum | solution.py:12
  9.6 0.7 convert_element_type.42
  10.3 0.8 iota_compare_fusion.4
  11.0 0.8 add_multiply_fusion
  11.8 0.3 copy.22
  12.1 2.8 %fusion = f32[512,8,64]{2,1,0:T(8,128)} fusion(bf16[512,4,64]{2,1,0:T(4,128)(2,1)S(1)} %copy.22, s32[512,4]{1,0:T(8,128)S(1)} %copy.21), kind=kOutput, calls=%fused_computation.4 | convolution fusion | flops 2375680 | bytes 1318912 | tf_op jit(solution)/shard_map/nsc,nsj->ncj/dot_general | solution.py:19
  14.9 2.2 %copy.23 = f32[512,8,64]{0,2,1:T(8,128)S(1)} copy(f32[512,8,64]{2,1,0:T(8,128)} %fusion) | data formatting | bytes 2097152 | tf_op jit(solution)/shard_map/convert_element_type | solution.py:28
  17.1 1.3 copy.24
  18.5 0.4 copy.25
  18.9 2.8 %fusion.1 = f32[512,8,64]{2,1,0:T(8,128)} fusion(pred[512,4,64]{2,1,0:T(4,128)(4,1)S(1)} %copy.25, s32[512,4]{1,0:T(8,128)S(1)} %copy.21), kind=kOutput, calls=%fused_computation.5 | convolution fusion | flops 2637824 | bytes 1187840 | tf_op jit(solution)/shard_map/nsc,nsj->ncj/dot_general | solution.py:20
  21.7 0.0 copy-start.1
  21.7 2.2 %copy.26 = f32[512,8,64]{0,2,1:T(8,128)S(1)} copy(f32[512,8,64]{2,1,0:T(8,128)} %fusion.1) | data formatting | bytes 2097152 | tf_op jit(solution)/shard_map/convert_element_type | solution.py:30
  23.9 0.0 copy-start.2
  23.9 0.0 copy-start.3
  23.9 1.3 copy.27
  25.3 0.0 copy-done.1
  25.3 11.9 %all_gather.7 = bf16[512,768]{1,0:T(8,128)(2,1)S(1)} all-gather(bf16[64,768]{1,0:T(8,128)(2,1)S(1)} %convert_element_type.50), channel_id=1, replica_groups=mesh['enc'=4,'lab'=8] {'lab'}, dimensions={0}, use_global_device_ids=true | all-gather | bytes 884736 | tf_op jit(solution)/shard_map/all_gather | solution.py:59
  37.1 0.0 copy-done.2
  37.1 0.0 copy-done.3
  37.1 0.6 dynamic-slice
  38.4 0.2 dynamic-update-slice
  38.6 13.2 %all-reduce = bf16[512]{0:T(512)(128)(2,1)S(1)} all-reduce(bf16[512]{0:T(512)(128)(2,1)S(1)} %dynamic-update-slice), channel_id=1, replica_groups=mesh['enc'=4,'lab'=8] {'lab'}, use_global_device_ids=true, to_apply=%add | all-reduce | flops 512 | bytes 2048
  51.9 0.0 copy-done
  51.9 2.3 %fusion.7 = bf16[512,512]{1,0:T(8,128)(2,1)S(1)} fusion(f32[512,512]{1,0:T(8,128)} %copy.27, bf16[512,768]{1,0:T(8,128)(2,1)S(1)} %copy-done, bf16[512,768]{1,0:T(8,128)(2,1)S(1)} %all_gather.7, f32[512,512]{1,0:T(8,128)} %copy.24, f32[512]{0:T(512)S(1)} %convert_element_type.49), kind=kOutput, calls=%fused_computation.12 | convolution fusion | flops 404488192 | bytes 4196352 | tf_op jit(solution)/shard_map/dot_general | solution.py:31
  54.2 1.7 %fusion.10 = f32[512,768]{1,0:T(8,128)} fusion(bf16[512,512]{1,0:T(8,128)(2,1)S(1)} %fusion.7, bf16[512,768]{1,0:T(8,128)(2,1)S(1)} %copy-done), kind=kOutput, calls=%fused_computation.19 | convolution fusion | flops 402653184 | bytes 2883584 | tf_op jit(solution)/shard_map/dot_general | solution.py:65
  55.9 0.0 reduce-scatter.2.cloned.1.call-update
  55.9 0.0 all-reduce.3.cloned.1.call-start
  56.0 38.9 %reduce-scatter.2.cloned.1.call-done = f32[64,768]{1,0:T(8,128)} async-done(((f32[512,768]{1,0:T(8,128)}), f32[64,768]{1,0:T(8,128)}) %reduce-scatter.2.cloned.1.call-update) | async-done | bytes 196624 | tf_op jit(solution)/shard_map/reduce_scatter | solution.py:64
  94.9 0.0 all-reduce.3.cloned.1.call-update
  94.9 1.7 %fusion.11 = f32[512,768]{1,0:T(8,128)} fusion(bf16[512,512]{1,0:T(8,128)(2,1)S(1)} %fusion.7, bf16[512,768]{1,0:T(8,128)(2,1)S(1)} %all_gather.7), kind=kOutput, calls=%fused_computation.20 | convolution fusion | flops 402653184 | bytes 2883584 | tf_op jit(solution)/shard_map/dot_general | solution.py:35
  96.6 35.4 %all-reduce.3.cloned.1.call-done = f32[64,768]{1,0:T(8,128)} async-done(((f32[64,768]{1,0:T(8,128)}), f32[64,768]{1,0:T(8,128)}) %all-reduce.3.cloned.1.call-update) | async-done | bytes 196624 | tf_op jit(solution)/shard_map/psum | solution.py:73
  132.0 1.6 %broadcast_multiply_fusion = f32[64,768]{1,0:T(8,128)} fusion(f32[64,768]{1,0:T(8,128)} %all-reduce.3.cloned.1.call-done), kind=kLoop, calls=%fused_computation.18 | loop fusion | flops 49152 | bytes 393216 | tf_op jit(solution)/shard_map/mul | solution.py:73
  (4 shorter events, 0.0 us)
Async XLA Ops:
  7.2 44.7 %copy-start = (bf16[512,768]{1,0:T(8,128)(2,1)S(1)}, bf16[512,768]{1,0:T(8,128)(2,1)}, u32[]{:S(2)}) copy-start(bf16[512,768]{1,0:T(8,128)(2,1)} %param.7) | copy-start | bytes 2359300
  7.2 87.7 %reduce-scatter.2.cloned.1.call-start = ((), (), s32[]{:S(2)}) async-start(), calls=%async_computation.1 | async-start | bytes 1769472 | tf_op jit(solution)/shard_map/reduce_scatter | solution.py:64
  21.7 3.6 %copy-start.1 = (f32[64,768]{1,0:T(8,128)S(1)}, f32[64,768]{1,0:T(8,128)}, u32[]{:S(2)}) copy-start(f32[64,768]{1,0:T(8,128)} %param.8) | copy-start | bytes 589828
  23.9 13.2 %copy-start.2 = (s32[64]{0:T(128)S(1)}, s32[64]{0:T(128)}, u32[]{:S(2)}) copy-start(s32[64]{0:T(128)} %param.9) | copy-start | bytes 772
  23.9 13.2 %copy-start.3 = (u32[32]{0:T(128)S(1)}, u32[32]{0:T(128)}, u32[]{:S(2)}) copy-start(u32[32]{0:T(128)} %constant.8) | copy-start | bytes 388
  55.9 76.1 %all-reduce.3.cloned.1.call-start = ((), (), s32[]{:S(2)}) async-start(), calls=%async_computation.2 | async-start | bytes 393216 | tf_op jit(solution)/shard_map/psum | solution.py:73
Sparse Core Ops, SparseCore 0:
  56.1 38.7 reduce-scatter.1
  97.2 34.8 all-reduce.2
where the time goes:
time: 141 us; the launch traced here: 140 us
  waiting for transfers between devices  74.3 us (53%)
  blocking collectives  25.1 us (18%)
  between operations  14.8 us (10%)
  matrix products  11.4 us (8%)
  local copies, waits for them, and re-layouts  9.52 us (7%)
  other arithmetic  5.32 us (4%)
    reduce_scatter x1, waiting for transfers between devices, shards(): lax.psum_scatter(lax.dot_general(scored, embeddings, (((0,), (0,)), ((),...  38.9 us
    psum x1, waiting for transfers between devices, shards(): w_grad = lax.psum(partial_grad, 'enc') * scale_factor  35.4 us
    unnamed x1, blocking collectives  13.2 us
    all_gather x1, blocking collectives, shards(): lax.all_gather(classifier_b, 'lab', axis=0, tiled=True)  11.9 us
    convert_element_type x2, local copies, waits for them, and re-layouts, absorb(): target = target_all.astype(jnp.float32)  3.52 us
    convert_element_type x2, local copies, waits for them, and re-layouts, absorb(): weight = weight_all.astype(jnp.float32)  3.5 us
  transfers between devices with their start and end apart: 2, of which 2 were waited for; matrix products, arithmetic and copies ran while one was open for 1% of the time, Pallas kernels for 0%

commit v1 on v0

v1 whole, which is shorter than its diff:
```python
import functools
import math

import jax
import jax.numpy as jnp
from jax import lax
from jax.experimental import pallas as pl
from jax.experimental.pallas import tpu as pltpu
from jax.sharding import PartitionSpec as P

BF16 = jnp.bfloat16
F32 = jnp.float32
LANES = 128
SUBLANES = 8
ROWS = 256
VMEM_LIMIT = 56 * 1024 * 1024


def flip(value, axis, mask):
    return lax.ppermute(value, axis, [(i, i ^ mask) for i in range(lax.axis_size(axis))])


def bit_groups(count):
    masks = [1 << b for b in range(1, count.bit_length() - 1)]
    return [tuple(masks[i : i + 2]) for i in range(0, len(masks), 2)]


def group_masks(group):
    return [group[0]] if len(group) == 1 else [group[0], group[1], group[0] | group[1]]


def targets_kernel(short_ref, live_ref, pos_ref, neg_ref, mine_ref, theirs_ref, *, panel):
    me = lax.axis_index("lab")
    slots, docs = short_ref.shape
    negatives = neg_ref.shape[1]
    groups = panel // SUBLANES
    clusters = (mine_ref.shape[0] + theirs_ref.shape[0]) // panel
    shape = (groups, SUBLANES, LANES)
    label = SUBLANES * lax.broadcasted_iota(jnp.int32, shape, 0) + lax.broadcasted_iota(jnp.int32, shape, 1)

    def chunk(i, carry):
        lanes = pl.ds(pl.multiple_of(i * LANES, LANES), LANES)

        def row(value):
            return jnp.broadcast_to(value, (SUBLANES, LANES))

        values, relative = [], []
        for s in range(slots):
            count = jnp.zeros(shape, F32)
            for k in range(negatives):
                count = count + jnp.where(row(neg_ref[s, k : k + 1, lanes])[None] == label, 1.0, 0.0)
            hot = row(pos_ref[s : s + 1, lanes])[None] == label
            live = row(live_ref[s : s + 1, lanes]).astype(F32)[None]
            values.append(jnp.where(hot, -1.0 - count, count) * live)
            relative.append(row(short_ref[s : s + 1, lanes]) ^ me)
        for r in range(clusters):
            block = jnp.zeros(shape, F32)
            for s in range(slots):
                block = jnp.where((relative[s] == r)[None], values[s], block)
            out = theirs_ref if r % 2 else mine_ref
            out[pl.ds((r // 2) * panel, panel), lanes] = block.reshape(panel, LANES).astype(BF16)
        return carry

    lax.fori_loop(0, docs // LANES, chunk, 0)


def score_kernel(*refs, pieces, parts):
    piece_refs = refs[:pieces]
    emb_refs = refs[pieces : pieces + 2]
    target_refs = refs[pieces + 2 : pieces + 4]
    part_refs = refs[pieces + 4 : pieces + 4 + parts]
    dlogit_refs = refs[pieces + 4 + parts : pieces + 6 + parts]
    classifier_ref = refs[pieces + 6 + parts]
    each = piece_refs[0].shape[0]
    for i, ref in enumerate(piece_refs):
        classifier_ref[i * each : (i + 1) * each] = ref[...]
    total = classifier_ref.shape[0]
    rows = min(ROWS, total)
    span = total // parts
    for start in range(0, total, rows):
        block = classifier_ref[start : start + rows]
        grad = None
        for emb_ref, target_ref, dlogit_ref in zip(emb_refs, target_refs, dlogit_refs):
            logits = lax.dot_general(
                block, emb_ref[...], (((1,), (1,)), ((), ())), preferred_element_type=F32
            )
            signed = target_ref[start : start + rows].astype(F32)
            dlogits = (signed * jax.nn.sigmoid(jnp.where(signed < 0, -logits, logits))).astype(BF16)
            dlogit_ref[start : start + rows] = dlogits
            term = jnp.dot(dlogits, emb_ref[...], preferred_element_type=F32)
            grad = term if grad is None else grad + term
        step = min(rows, span)
        for off in range(0, rows, step):
            part, at = divmod(start + off, span)
            ref = part_refs[part]
            ref[at : at + step] = grad[off : off + step].astype(ref.dtype)


def emb_kernel(d_own_ref, d_other_ref, c_own_ref, c_other_ref, out_ref):
    dims = (((0,), (0,)), ((), ()))
    out_ref[...] = lax.dot_general(
        d_own_ref[...], c_own_ref[...], dims, preferred_element_type=F32
    ) + lax.dot_general(d_other_ref[...], c_other_ref[...], dims, preferred_element_type=F32)


def vmem(count):
    return [pl.BlockSpec(memory_space=pltpu.VMEM)] * count


def cost(flops, nbytes):
    return pl.CostEstimate(flops=flops, bytes_accessed=nbytes, transcendentals=0)


def params():
    return pltpu.CompilerParams(vmem_limit_bytes=VMEM_LIMIT)


def shards(embeddings, classifier, label_valid, shortlist, slot_live, positive, negative):
    lab = lax.axis_size("lab")
    enc = lax.axis_size("enc")
    docs, width = embeddings.shape
    panel = classifier.shape[0]
    slots = shortlist.shape[1]
    half = lab // 2 * panel
    groups = bit_groups(lab)

    valid = label_valid.astype(F32)[:, None]
    pieces = [jnp.where(valid > 0, classifier, 0.0).astype(BF16)]
    for group in groups:
        own = pieces[0] if len(pieces) == 1 else jnp.concatenate(pieces, 0)
        pieces = [own] + [flip(own, "lab", mask) for mask in group_masks(group)]

    emb_other = flip(embeddings, "lab", 1)
    target_mine, target_theirs = pl.pallas_call(
        functools.partial(targets_kernel, panel=panel),
        out_shape=[jax.ShapeDtypeStruct((half, docs), BF16)] * 2,
        in_specs=vmem(4),
        out_specs=vmem(2),
        compiler_params=params(),
        cost_estimate=cost(docs * panel * slots * 40, docs * slots * 44 + docs * half * 4),
        name="targets",
    )(shortlist.T, slot_live.T, positive.T, negative.transpose(1, 2, 0))
    target_other = flip(target_theirs, "lab", 1)

    parts = len(group_masks(groups[-1])) + 1 if groups else 1
    outs = pl.pallas_call(
        functools.partial(score_kernel, pieces=len(pieces), parts=parts),
        out_shape=[
            jax.ShapeDtypeStruct((half // parts, width), BF16 if i else F32) for i in range(parts)
        ]
        + [jax.ShapeDtypeStruct((half, docs), BF16)] * 2
        + [jax.ShapeDtypeStruct((half, width), BF16)],
        in_specs=vmem(len(pieces) + 4),
        out_specs=vmem(parts + 3),
        compiler_params=params(),
        cost_estimate=cost(8 * docs * half * width, 4 * docs * width + 8 * half * docs + 8 * half * width),
        name="score",
    )(*pieces, embeddings, emb_other, target_mine, target_other)
    grads, (d_own, d_theirs, classifier_own) = outs[:parts], outs[parts:]

    grad = None
    for group in reversed(groups):
        masks = group_masks(group)
        if grad is not None:
            grad = grad.reshape(len(masks) + 1, -1, width)
            grads = [grad[0]] + [grad[i].astype(BF16) for i in range(1, len(masks) + 1)]
        received = [flip(g, "lab", mask) for g, mask in zip(grads[1:], masks)]
        grad = grads[0]
        for r in received:
            grad = grad + r.astype(F32)
    if grad is None:
        grad = grads[0]
    for bit in range(enc.bit_length() - 1):
        grad = grad + flip(grad.astype(BF16), "enc", 1 << bit).astype(F32)
    w_grad = grad * (valid * (1.0 / math.sqrt(docs * enc * slots)))

    emb_grad = pl.pallas_call(
        emb_kernel,
        out_shape=jax.ShapeDtypeStruct((docs, width), F32),
        in_specs=vmem(4),
        out_specs=pl.BlockSpec(memory_space=pltpu.VMEM),
        compiler_params=params(),
        cost_estimate=cost(4 * docs * half * width, 4 * docs * width + 4 * half * docs + 4 * half * width),
        name="emb_grad",
    )(d_own, flip(d_theirs, "lab", 1), classifier_own, flip(classifier_own, "lab", 1))
    return (w_grad, emb_grad)


def solution(mesh):
    in_specs = (
        P(("enc", "lab"), None),
        P("lab", None),
        P("lab"),
        P(("enc", "lab"), None),
        P(("enc", "lab"), None),
        P(("enc", "lab"), None),
        P(("enc", "lab"), None, None),
    )
    out_specs = (P("lab", None), P(("enc", "lab"), None))
    return jax.shard_map(shards, mesh=mesh, in_specs=in_specs, out_specs=out_specs, check_vma=False)
```

time: 141 us -> 44.6 us (0.32)
  waiting for transfers between devices: 74.3 us -> 15.2 us
  blocking collectives: 25.1 us -> 0 us
  between operations: 14.8 us -> 0.72 us
  starting transfers between devices: 0.08 us -> 13.8 us
  matrix products: 11.4 us -> 0 us
  Pallas kernels: 0 us -> 9.3 us
  local copies, waits for them, and re-layouts: 9.52 us -> 1.78 us
  other arithmetic: 5.32 us -> 3.42 us
    reduce_scatter x1 -> x0, waiting for transfers between devices: 38.9 us -> none  [shards(): lax.psum_scatter(lax.dot_general(scored, embeddings, (((0,), (0,)), ((),...]
    psum x1 -> x0, waiting for transfers between devices: 35.4 us -> none  [shards(): w_grad = lax.psum(partial_grad, 'enc') * scale_factor]
    ppermute x0 -> x12, waiting for transfers between devices: none -> 15.2 us  [flip(): lax.ppermute(value, axis, [(i, i ^ mask) for i in range(lax.axis_size(axi...]
    ppermute x0 -> x12, starting transfers between devices: none -> 13.8 us  [flip(): lax.ppermute(value, axis, [(i, i ^ mask) for i in range(lax.axis_size(axi...]
    unnamed x1 -> x0, blocking collectives: 13.2 us -> none
    all_gather x1 -> x0, blocking collectives: 11.9 us -> none  [shards(): lax.all_gather(classifier_b, 'lab', axis=0, tiled=True)]
    dot_general x5 -> x0, matrix products: 11.4 us -> none  [the longest x1 2.8 us: dense_targets(): jnp.einsum('nsc,nsj->ncj', cluster_hot, slot_weight)]
    pallas_call x0 -> x3, Pallas kernels: none -> 9.3 us  [the longest x1 3.82 us: shards(): pl.pallas_call(functools.partial(score_kernel, pieces=len(pieces), parts=...]
  transfers between devices with their start and end apart: 2 -> 12, of which waited for: 2 -> 8; matrix products, arithmetic and copies ran while one was open for 1% -> 6% of each run, Pallas kernels for 0% -> 6%
where the time goes in v1:
time: 44.6 us; the launch traced here: 44.3 us
  waiting for transfers between devices  15.2 us (34%)
  starting transfers between devices  13.8 us (31%)
  Pallas kernels  9.3 us (21%)
  other arithmetic  3.42 us (8%)
  local copies, waits for them, and re-layouts  1.78 us (4%)
  between operations  0.72 us (2%)
    ppermute x12, waiting for transfers between devices, flip(): lax.ppermute(value, axis, [(i, i ^ mask) for i in range(lax.axis_size(axi...  15.2 us
    ppermute x12, starting transfers between devices, flip(): lax.ppermute(value, axis, [(i, i ^ mask) for i in range(lax.axis_size(axi...  13.8 us
    pallas_call x1, Pallas kernels, shards(): pl.pallas_call(functools.partial(score_kernel, pieces=len(pieces), parts=...  3.82 us
    pallas_call x1, Pallas kernels, shards(): pl.pallas_call(emb_kernel, out_shape=jax.ShapeDtypeStruct((docs, width),...  3.01 us
    pallas_call x1, Pallas kernels, shards(): pl.pallas_call(functools.partial(targets_kernel, panel=panel), out_shape=...  2.47 us
    unnamed x18, local copies, waits for them, and re-layouts  1.78 us
    convert_element_type x1, other arithmetic, shards(): pieces = [jnp.where(valid > 0, classifier, 0.0).astype(BF16)]  1.01 us
    convert_element_type x2, other arithmetic, shards(): grad = grad + flip(grad.astype(BF16), 'enc', 1 << bit).astype(F32)  1 us
  transfers between devices with their start and end apart: 12, of which 8 were waited for; matrix products, arithmetic and copies ran while one was open for 6% of the time, Pallas kernels for 6%

profile of v1, /device:TPU:0, one launch (start us, length us, event | category | flops | bytes accessed | tf_op | source)
XLA Modules:
  0.0 44.3 jit_solution(1651112476960423136)
XLA Ops:
  0.6 0.5 %collective-permute-start.3 = (bf16[512,768]{1,0:T(8,128)(2,1)}, bf16[512,768]{1,0:T(8,128)(2,1)S(1)}, u32[]{:S(2)}, u32[]{:S(2)}) collective-permute-start(bf16[512,768]{1,0:T(8,128)(2,1)} %refs_4_.1), channel_id=1, source_target_pairs={{0,1},{1,0},{2,3},{3,2},{4,5},{5,4},{6,7},{7,6},{8,9},{9,8},{10,11... | collective-permute-start | bytes 2359304 | tf_op jit(solution)/shard_map/ppermute | solution.py:20
  1.1 2.5 %targets.1 = (bf16[256,512]{1,0:T(8,128)(2,1)}, bf16[256,512]{1,0:T(8,128)(2,1)}) custom-call(s32[4,512]{1,0:T(4,128)} %bitcast.5, s32[4,512]{1,0:T(4,128)} %bitcast.6, s32[4,512]{1,0:T(4,128)} %bitcast.7, s32[4,8,512]{2,1,0:T(8,128)} %bitcast.4), custom_call_target="tpu_custom_call" | custom-call | flops 5242880 | bytes 614400 | tf_op jit(solution)/shard_map/targets/pallas_call | solution.py:134
  3.6 0.1 collective-permute-start.4
  3.7 0.7 %convert_compare_fusion = pred[64]{0:T(512)(128)(4,1)S(1)} fusion(s32[64]{0:T(128)} %param.9), kind=kLoop, calls=%fused_computation.6 | loop fusion | flops 128 | bytes 320 | tf_op jit(solution)/shard_map/gt | solution.py:128
  4.3 1.0 %select_convert_fusion.refs_0_ = bf16[64,768]{1,0:T(8,128)(2,1)S(1)} fusion(f32[64,768]{1,0:T(8,128)} %param.8, pred[64]{0:T(512)(128)(4,1)S(1)} %convert_compare_fusion), kind=kLoop, calls=%fused_computation.3 | loop fusion | flops 49152 | bytes 294976 | tf_op jit(solution)/shard_map/convert_element_type | solution.py:128
  5.3 0.0 copy-start.2
  5.4 3.0 %collective-permute-start = (bf16[64,768]{1,0:T(8,128)(2,1)S(1)}, bf16[64,768]{1,0:T(8,128)(2,1)S(1)}, u32[]{:S(2)}, u32[]{:S(2)}) collective-permute-start(bf16[64,768]{1,0:T(8,128)(2,1)S(1)} %select_convert_fusion.refs_0_), channel_id=1, source_target_pairs={{0,2},{1,3},{2,0},{3,1},{4,6},{5,7},{6,4},{7,5},{8,10},{9,11},{10,... | collective-permute-start | bytes 294920 | tf_op jit(solution)/shard_map/ppermute | solution.py:20
  8.4 1.5 %collective-permute-start.1 = (bf16[64,768]{1,0:T(8,128)(2,1)S(1)}, bf16[64,768]{1,0:T(8,128)(2,1)S(1)}, u32[]{:S(2)}, u32[]{:S(2)}) collective-permute-start(bf16[64,768]{1,0:T(8,128)(2,1)S(1)} %select_convert_fusion.refs_0_), channel_id=1, source_target_pairs={{0,4},{1,5},{2,6},{3,7},{4,0},{5,1},{6,2},{7,3},{8,12},{9,13},{10,... | collective-permute-start | bytes 294920 | tf_op jit(solution)/shard_map/ppermute | solution.py:20
  9.9 0.0 collective-permute-start.2
  9.9 1.5 %collective-permute-done.refs_1_ = bf16[64,768]{1,0:T(8,128)(2,1)S(1)} collective-permute-done((bf16[64,768]{1,0:T(8,128)(2,1)S(1)}, bf16[64,768]{1,0:T(8,128)(2,1)S(1)}, u32[]{:S(2)}, u32[]{:S(2)}) %collective-permute-start) | collective-permute-done | bytes 98336 | tf_op jit(solution)/shard_map/ppermute | solution.py:20
  11.4 0.0 copy-start.5
  11.4 2.6 %collective-permute-done.1.refs_2_ = bf16[64,768]{1,0:T(8,128)(2,1)S(1)} collective-permute-done((bf16[64,768]{1,0:T(8,128)(2,1)S(1)}, bf16[64,768]{1,0:T(8,128)(2,1)S(1)}, u32[]{:S(2)}, u32[]{:S(2)}) %collective-permute-start.1) | collective-permute-done | bytes 98336 | tf_op jit(solution)/shard_map/ppermute | solution.py:20
  14.0 0.0 copy-start.6
  14.1 1.3 %collective-permute-done.2.refs_3_ = bf16[64,768]{1,0:T(8,128)(2,1)S(1)} collective-permute-done((bf16[64,768]{1,0:T(8,128)(2,1)S(1)}, bf16[64,768]{1,0:T(8,128)(2,1)S(1)}, u32[]{:S(2)}, u32[]{:S(2)}) %collective-permute-start.2) | collective-permute-done | bytes 98336 | tf_op jit(solution)/shard_map/ppermute | solution.py:20
  15.4 0.0 copy-start.7
  15.4 0.0 collective-permute-done.4.refs_7_
  15.4 0.0 copy-start.4
  15.4 0.0 collective-permute-done.3.refs_5_
  15.4 0.0 copy-start.3
  15.4 0.0 copy-done.2
  15.4 0.0 copy-done.5
  15.4 0.0 copy-done.6
  15.5 0.6 %copy-done.7 = bf16[64,768]{1,0:T(8,128)(2,1)} copy-done((bf16[64,768]{1,0:T(8,128)(2,1)}, bf16[64,768]{1,0:T(8,128)(2,1)S(1)}, u32[]{:S(2)}) %copy-start.7) | copy-done | bytes 98328
  16.0 0.1 copy-done.4
  16.1 0.2 copy-done.3
  16.4 0.0 copy-start.8
  16.4 3.8 %score.1 = (f32[64,768]{1,0:T(8,128)}, bf16[64,768]{1,0:T(8,128)(2,1)}, bf16[64,768]{1,0:T(8,128)(2,1)}, bf16[64,768]{1,0:T(8,128)(2,1)}, bf16[256,512]{1,0:T(8,...) custom-call(bf16[64,768]{1,0:T(8,128)(2,1)} %copy-done.2, bf16[64,768]{1,0:T(8,128)(2,1)} %copy-done.5, ...), custom_call_target="tpu_custom_call" | custom-call | flops 805306368 | bytes 4194304 | tf_op jit(solution)/shard_map/score/pallas_call | solution.py:146
  20.2 1.1 %collective-permute-start.7 = (bf16[64,768]{1,0:T(8,128)(2,1)}, bf16[64,768]{1,0:T(8,128)(2,1)S(1)}, u32[]{:S(2)}, u32[]{:S(2)}) collective-permute-start(bf16[64,768]{1,0:T(8,128)(2,1)} %get-tuple-element.16), channel_id=1, source_target_pairs={{0,6},{1,7},{2,4},{3,5},{4,2},{5,3},{6,0},{7,1},{8,14},{9,15},{10,... | collective-permute-start | bytes 294920 | tf_op jit(solution)/shard_map/ppermute | solution.py:20
  21.3 1.1 %collective-permute-start.6 = (bf16[64,768]{1,0:T(8,128)(2,1)}, bf16[64,768]{1,0:T(8,128)(2,1)S(1)}, u32[]{:S(2)}, u32[]{:S(2)}) collective-permute-start(bf16[64,768]{1,0:T(8,128)(2,1)} %get-tuple-element.15), channel_id=1, source_target_pairs={{0,4},{1,5},{2,6},{3,7},{4,0},{5,1},{6,2},{7,3},{8,12},{9,13},{10,... | collective-permute-start | bytes 294920 | tf_op jit(solution)/shard_map/ppermute | solution.py:20
  22.4 1.3 %collective-permute-start.5 = (bf16[64,768]{1,0:T(8,128)(2,1)}, bf16[64,768]{1,0:T(8,128)(2,1)S(1)}, u32[]{:S(2)}, u32[]{:S(2)}) collective-permute-start(bf16[64,768]{1,0:T(8,128)(2,1)} %get-tuple-element.14), channel_id=1, source_target_pairs={{0,2},{1,3},{2,0},{3,1},{4,6},{5,7},{6,4},{7,5},{8,10},{9,11},{10,... | collective-permute-start | bytes 294920 | tf_op jit(solution)/shard_map/ppermute | solution.py:20
  23.7 2.4 %collective-permute-done.7 = bf16[64,768]{1,0:T(8,128)(2,1)S(1)} collective-permute-done((bf16[64,768]{1,0:T(8,128)(2,1)}, bf16[64,768]{1,0:T(8,128)(2,1)S(1)}, u32[]{:S(2)}, u32[]{:S(2)}) %collective-permute-start.7) | collective-permute-done | bytes 98336 | tf_op jit(solution)/shard_map/ppermute | solution.py:20
  26.1 1.0 %collective-permute-done.6 = bf16[64,768]{1,0:T(8,128)(2,1)S(1)} collective-permute-done((bf16[64,768]{1,0:T(8,128)(2,1)}, bf16[64,768]{1,0:T(8,128)(2,1)S(1)}, u32[]{:S(2)}, u32[]{:S(2)}) %collective-permute-start.6) | collective-permute-done | bytes 98336 | tf_op jit(solution)/shard_map/ppermute | solution.py:20
  27.0 0.2 collective-permute-done.5
  27.3 1.0 %fusion.1 = (bf16[64,768]{1,0:T(8,128)(2,1)S(1)}, f32[64,768]{1,0:T(8,128)S(1)}) fusion(bf16[64,768]{1,0:T(8,128)(2,1)S(1)} %collective-permute-done.7, bf16[64,768]{1,0:T(8,128)(2,1)S(1)} %collective-permute-done.6, f32[64,768]{1,0:T(8,128)} %get-tuple-element.13, bf16[64,768]{1,0:T(8,128)(2,1)S(1)} %collective-permute-done.5), kind=kLoop, calls=%fused_computation.7 | loop fusion | flops 344064 | bytes 786432 | tf_op jit(solution)/shard_map/convert_element_type | solution.py:174
  28.2 1.6 %collective-permute-start.8 = (bf16[64,768]{1,0:T(8,128)(2,1)S(1)}, bf16[64,768]{1,0:T(8,128)(2,1)S(1)}, u32[]{:S(2)}, u32[]{:S(2)}) collective-permute-start(bf16[64,768]{1,0:T(8,128)(2,1)S(1)} %get-tuple-element.20), channel_id=1, source_target_pairs={{0,8},{8,0},{16,24},{24,16},{1,9},{9,1},{17,25},{25,17},{2,10},{10... | collective-permute-start | bytes 294920 | tf_op jit(solution)/shard_map/ppermute | solution.py:20
  29.9 0.0 collective-permute-start.10
  29.9 0.5 %collective-permute-start.11 = (bf16[256,768]{1,0:T(8,128)(2,1)}, bf16[256,768]{1,0:T(8,128)(2,1)S(1)}, u32[]{:S(2)}, u32[]{:S(2)}) collective-permute-start(bf16[256,768]{1,0:T(8,128)(2,1)} %get-tuple-element.19.c_own_ref), channel_id=1, source_target_pairs={{0,1},{1,0},{2,3},{3,2},{4,5},{5,4},{6,7},{7,6},{8,9},{9,8},{10,11... | collective-permute-start | bytes 1179656 | tf_op jit(solution)/shard_map/ppermute | solution.py:20
  30.4 2.5 %collective-permute-done.8 = bf16[64,768]{1,0:T(8,128)(2,1)S(1)} collective-permute-done((bf16[64,768]{1,0:T(8,128)(2,1)S(1)}, bf16[64,768]{1,0:T(8,128)(2,1)S(1)}, u32[]{:S(2)}, u32[]{:S(2)}) %collective-permute-start.8) | collective-permute-done | bytes 98336 | tf_op jit(solution)/shard_map/ppermute | solution.py:20
  32.9 3.1 %collective-permute-start.9 = (bf16[64,768]{1,0:T(8,128)(2,1)S(1)}, bf16[64,768]{1,0:T(8,128)(2,1)S(1)}, u32[]{:S(2)}, u32[]{:S(2)}) collective-permute-start(bf16[64,768]{1,0:T(8,128)(2,1)S(1)} %fusion), channel_id=1, source_target_pairs={{0,16},{8,24},{16,0},{24,8},{1,17},{9,25},{17,1},{25,9},{2,18},{10... | collective-permute-start | bytes 294920 | tf_op jit(solution)/shard_map/ppermute | solution.py:20
  36.0 0.0 copy-done.8
  36.0 3.6 %collective-permute-done.9 = bf16[64,768]{1,0:T(8,128)(2,1)S(1)} collective-permute-done((bf16[64,768]{1,0:T(8,128)(2,1)S(1)}, bf16[64,768]{1,0:T(8,128)(2,1)S(1)}, u32[]{:S(2)}, u32[]{:S(2)}) %collective-permute-start.9) | collective-permute-done | bytes 98336 | tf_op jit(solution)/shard_map/ppermute | solution.py:20
  39.7 0.8 %add_multiply_fusion = f32[64,768]{1,0:T(8,128)} fusion(bf16[64,768]{1,0:T(8,128)(2,1)S(1)} %collective-permute-done.9, f32[64,768]{1,0:T(8,128)S(1)} %get-tuple-element.21, bf16[64,768]{1,0:T(8,128)(2,1)S(1)} %collective-permute-done.8, f32[64]{0:T(128)S(1)} %convert_multiply_fusion), kind=kLoop, calls=%fused_computation | loop fusion | flops 245760 | bytes 590080 | tf_op jit(solution)/shard_map/mul | solution.py:175
  40.4 0.0 collective-permute-done.10.d_other_ref
  40.4 0.0 copy-start.1
  40.4 0.0 collective-permute-done.11.c_other_ref
  40.4 0.0 copy-start
  40.5 0.7 %copy-done.1 = bf16[256,512]{1,0:T(8,128)(2,1)} copy-done((bf16[256,512]{1,0:T(8,128)(2,1)}, bf16[256,512]{1,0:T(8,128)(2,1)S(1)}, u32[]{:S(2)}) %copy-start.1) | copy-done | bytes 262168
  41.1 0.1 copy-done
  41.3 3.0 %emb_grad.1 = f32[512,768]{1,0:T(8,128)} custom-call(bf16[256,512]{1,0:T(8,128)(2,1)} %get-tuple-element.17.d_own_ref, bf16[256,512]{1,0:T(8,128)(2,1)} %copy-done.1, bf16[256,768]{1,0:T(8,128)(2,1)} %get-tuple-element.19.c_own_ref, bf16[256,768]{1,0:T(8,128)(2,1)} %copy-done), custom_call_target="tpu_custom_call" | custom-call | flops 402653184 | bytes 2883584 | tf_op jit(solution)/shard_map/emb_grad/pallas_call | solution.py:177
  (2 shorter events, 0.0 us)
Async XLA Ops:
  0.6 14.8 %collective-permute-start.3 = (bf16[512,768]{1,0:T(8,128)(2,1)}, bf16[512,768]{1,0:T(8,128)(2,1)S(1)}, u32[]{:S(2)}, u32[]{:S(2)}) collective-permute-start(bf16[512,768]{1,0:T(8,128)(2,1)} %refs_4_.1), channel_id=1, source_target_pairs={{0,1},{1,0},{2,3},{3,2},{4,5},{5,4},{6,7},{7,6},{8,9},{9,8},{10,11... | collective-permute-start | bytes 2359304 | tf_op jit(solution)/shard_map/ppermute | solution.py:20
  3.6 11.8 %collective-permute-start.4 = (bf16[256,512]{1,0:T(8,128)(2,1)}, bf16[256,512]{1,0:T(8,128)(2,1)S(1)}, u32[]{:S(2)}, u32[]{:S(2)}) collective-permute-start(bf16[256,512]{1,0:T(8,128)(2,1)} %get-tuple-element.12), channel_id=1, source_target_pairs={{0,1},{1,0},{2,3},{3,2},{4,5},{5,4},{6,7},{7,6},{8,9},{9,8},{10,11... | collective-permute-start | bytes 786440 | tf_op jit(solution)/shard_map/ppermute | solution.py:20
  5.3 10.1 %copy-start.2 = (bf16[64,768]{1,0:T(8,128)(2,1)}, bf16[64,768]{1,0:T(8,128)(2,1)S(1)}, u32[]{:S(2)}) copy-start(bf16[64,768]{1,0:T(8,128)(2,1)S(1)} %select_convert_fusion.refs_0_) | copy-start | bytes 294916
  5.4 6.1 %collective-permute-start = (bf16[64,768]{1,0:T(8,128)(2,1)S(1)}, bf16[64,768]{1,0:T(8,128)(2,1)S(1)}, u32[]{:S(2)}, u32[]{:S(2)}) collective-permute-start(bf16[64,768]{1,0:T(8,128)(2,1)S(1)} %select_convert_fusion.refs_0_), channel_id=1, source_target_pairs={{0,2},{1,3},{2,0},{3,1},{4,6},{5,7},{6,4},{7,5},{8,10},{9,11},{10,... | collective-permute-start | bytes 294920 | tf_op jit(solution)/shard_map/ppermute | solution.py:20
  8.4 5.7 %collective-permute-start.1 = (bf16[64,768]{1,0:T(8,128)(2,1)S(1)}, bf16[64,768]{1,0:T(8,128)(2,1)S(1)}, u32[]{:S(2)}, u32[]{:S(2)}) collective-permute-start(bf16[64,768]{1,0:T(8,128)(2,1)S(1)} %select_convert_fusion.refs_0_), channel_id=1, source_target_pairs={{0,4},{1,5},{2,6},{3,7},{4,0},{5,1},{6,2},{7,3},{8,12},{9,13},{10,... | collective-permute-start | bytes 294920 | tf_op jit(solution)/shard_map/ppermute | solution.py:20
  9.9 5.5 %collective-permute-start.2 = (bf16[64,768]{1,0:T(8,128)(2,1)S(1)}, bf16[64,768]{1,0:T(8,128)(2,1)S(1)}, u32[]{:S(2)}, u32[]{:S(2)}) collective-permute-start(bf16[64,768]{1,0:T(8,128)(2,1)S(1)} %select_convert_fusion.refs_0_), channel_id=1, source_target_pairs={{0,6},{1,7},{2,4},{3,5},{4,2},{5,3},{6,0},{7,1},{8,14},{9,15},{10,... | collective-permute-start | bytes 294920 | tf_op jit(solution)/shard_map/ppermute | solution.py:20
  11.4 4.0 %copy-start.5 = (bf16[64,768]{1,0:T(8,128)(2,1)}, bf16[64,768]{1,0:T(8,128)(2,1)S(1)}, u32[]{:S(2)}) copy-start(bf16[64,768]{1,0:T(8,128)(2,1)S(1)} %collective-permute-done.refs_1_) | copy-start | bytes 294916
  14.0 1.4 %copy-start.6 = (bf16[64,768]{1,0:T(8,128)(2,1)}, bf16[64,768]{1,0:T(8,128)(2,1)S(1)}, u32[]{:S(2)}) copy-start(bf16[64,768]{1,0:T(8,128)(2,1)S(1)} %collective-permute-done.1.refs_2_) | copy-start | bytes 294916
  15.4 0.6 %copy-start.7 = (bf16[64,768]{1,0:T(8,128)(2,1)}, bf16[64,768]{1,0:T(8,128)(2,1)S(1)}, u32[]{:S(2)}) copy-start(bf16[64,768]{1,0:T(8,128)(2,1)S(1)} %collective-permute-done.2.refs_3_) | copy-start | bytes 294916
  15.4 0.7 %copy-start.4 = (bf16[256,512]{1,0:T(8,128)(2,1)}, bf16[256,512]{1,0:T(8,128)(2,1)S(1)}, u32[]{:S(2)}) copy-start(bf16[256,512]{1,0:T(8,128)(2,1)S(1)} %collective-permute-done.4.refs_7_) | copy-start | bytes 786436
  15.4 1.0 %copy-start.3 = (bf16[512,768]{1,0:T(8,128)(2,1)}, bf16[512,768]{1,0:T(8,128)(2,1)S(1)}, u32[]{:S(2)}) copy-start(bf16[512,768]{1,0:T(8,128)(2,1)S(1)} %collective-permute-done.3.refs_5_) | copy-start | bytes 2359300
  16.4 19.6 %copy-start.8 = (s32[64]{0:T(128)S(1)}, s32[64]{0:T(128)}, u32[]{:S(2)}) copy-start(s32[64]{0:T(128)} %param.9) | copy-start | bytes 772
  20.2 5.9 %collective-permute-start.7 = (bf16[64,768]{1,0:T(8,128)(2,1)}, bf16[64,768]{1,0:T(8,128)(2,1)S(1)}, u32[]{:S(2)}, u32[]{:S(2)}) collective-permute-start(bf16[64,768]{1,0:T(8,128)(2,1)} %get-tuple-element.16), channel_id=1, source_target_pairs={{0,6},{1,7},{2,4},{3,5},{4,2},{5,3},{6,0},{7,1},{8,14},{9,15},{10,... | collective-permute-start | bytes 294920 | tf_op jit(solution)/shard_map/ppermute | solution.py:20
  21.3 5.7 %collective-permute-start.6 = (bf16[64,768]{1,0:T(8,128)(2,1)}, bf16[64,768]{1,0:T(8,128)(2,1)S(1)}, u32[]{:S(2)}, u32[]{:S(2)}) collective-permute-start(bf16[64,768]{1,0:T(8,128)(2,1)} %get-tuple-element.15), channel_id=1, source_target_pairs={{0,4},{1,5},{2,6},{3,7},{4,0},{5,1},{6,2},{7,3},{8,12},{9,13},{10,... | collective-permute-start | bytes 294920 | tf_op jit(solution)/shard_map/ppermute | solution.py:20
  22.4 4.8 %collective-permute-start.5 = (bf16[64,768]{1,0:T(8,128)(2,1)}, bf16[64,768]{1,0:T(8,128)(2,1)S(1)}, u32[]{:S(2)}, u32[]{:S(2)}) collective-permute-start(bf16[64,768]{1,0:T(8,128)(2,1)} %get-tuple-element.14), channel_id=1, source_target_pairs={{0,2},{1,3},{2,0},{3,1},{4,6},{5,7},{6,4},{7,5},{8,10},{9,11},{10,... | collective-permute-start | bytes 294920 | tf_op jit(solution)/shard_map/ppermute | solution.py:20
  28.2 4.7 %collective-permute-start.8 = (bf16[64,768]{1,0:T(8,128)(2,1)S(1)}, bf16[64,768]{1,0:T(8,128)(2,1)S(1)}, u32[]{:S(2)}, u32[]{:S(2)}) collective-permute-start(bf16[64,768]{1,0:T(8,128)(2,1)S(1)} %get-tuple-element.20), channel_id=1, source_target_pairs={{0,8},{8,0},{16,24},{24,16},{1,9},{9,1},{17,25},{25,17},{2,10},{10... | collective-permute-start | bytes 294920 | tf_op jit(solution)/shard_map/ppermute | solution.py:20
  29.9 10.6 %collective-permute-start.10 = (bf16[256,512]{1,0:T(8,128)(2,1)}, bf16[256,512]{1,0:T(8,128)(2,1)S(1)}, u32[]{:S(2)}, u32[]{:S(2)}) collective-permute-start(bf16[256,512]{1,0:T(8,128)(2,1)} %get-tuple-element.18), channel_id=1, source_target_pairs={{0,1},{1,0},{2,3},{3,2},{4,5},{5,4},{6,7},{7,6},{8,9},{9,8},{10,11... | collective-permute-start | bytes 786440 | tf_op jit(solution)/shard_map/ppermute | solution.py:20
  29.9 10.6 %collective-permute-start.11 = (bf16[256,768]{1,0:T(8,128)(2,1)}, bf16[256,768]{1,0:T(8,128)(2,1)S(1)}, u32[]{:S(2)}, u32[]{:S(2)}) collective-permute-start(bf16[256,768]{1,0:T(8,128)(2,1)} %get-tuple-element.19.c_own_ref), channel_id=1, source_target_pairs={{0,1},{1,0},{2,3},{3,2},{4,5},{5,4},{6,7},{7,6},{8,9},{9,8},{10,11... | collective-permute-start | bytes 1179656 | tf_op jit(solution)/shard_map/ppermute | solution.py:20
  32.9 6.7 %collective-permute-start.9 = (bf16[64,768]{1,0:T(8,128)(2,1)S(1)}, bf16[64,768]{1,0:T(8,128)(2,1)S(1)}, u32[]{:S(2)}, u32[]{:S(2)}) collective-permute-start(bf16[64,768]{1,0:T(8,128)(2,1)S(1)} %fusion), channel_id=1, source_target_pairs={{0,16},{8,24},{16,0},{24,8},{1,17},{9,25},{17,1},{25,9},{2,18},{10... | collective-permute-start | bytes 294920 | tf_op jit(solution)/shard_map/ppermute | solution.py:20
  40.4 0.7 %copy-start.1 = (bf16[256,512]{1,0:T(8,128)(2,1)}, bf16[256,512]{1,0:T(8,128)(2,1)S(1)}, u32[]{:S(2)}) copy-start(bf16[256,512]{1,0:T(8,128)(2,1)S(1)} %collective-permute-done.10.d_other_ref) | copy-start | bytes 786436
  40.4 0.8 %copy-start = (bf16[256,768]{1,0:T(8,128)(2,1)}, bf16[256,768]{1,0:T(8,128)(2,1)S(1)}, u32[]{:S(2)}) copy-start(bf16[256,768]{1,0:T(8,128)(2,1)S(1)} %collective-permute-done.11.c_other_ref) | copy-start | bytes 1179652

commit v2 on v1

--- a/solution.py
+++ b/solution.py
@@ -13,7 +13,7 @@
 LANES = 128
 SUBLANES = 8
 ROWS = 256
-VMEM_LIMIT = 56 * 1024 * 1024
+MIB = 1024 * 1024
 
 
 def flip(value, axis, mask):
@@ -62,6 +62,16 @@
         return carry
 
     lax.fori_loop(0, docs // LANES, chunk, 0)
+
+
+def pack_kernel(classifier_ref, valid_ref, out_ref):
+    panel = classifier_ref.shape[0]
+    diagonal = lax.broadcasted_iota(jnp.int32, (panel, panel), 0) == lax.broadcasted_iota(
+        jnp.int32, (panel, panel), 1
+    )
+    flags = jnp.broadcast_to(valid_ref[...].astype(F32), (panel, panel))
+    column = jnp.sum(jnp.where(diagonal, flags, 0.0), axis=1, keepdims=True)
+    out_ref[...] = (classifier_ref[...] * column).astype(BF16)
 
 
 def score_kernel(*refs, pieces, parts):
@@ -111,8 +121,8 @@
     return pl.CostEstimate(flops=flops, bytes_accessed=nbytes, transcendentals=0)
 
 
-def params():
-    return pltpu.CompilerParams(vmem_limit_bytes=VMEM_LIMIT)
+def params(*sizes):
+    return pltpu.CompilerParams(vmem_limit_bytes=(2 * sum(sizes) // MIB + 4) * MIB)
 
 
 def shards(embeddings, classifier, label_valid, shortlist, slot_live, positive, negative):
@@ -124,8 +134,17 @@
     half = lab // 2 * panel
     groups = bit_groups(lab)
 
-    valid = label_valid.astype(F32)[:, None]
-    pieces = [jnp.where(valid > 0, classifier, 0.0).astype(BF16)]
+    pieces = [
+        pl.pallas_call(
+            pack_kernel,
+            out_shape=jax.ShapeDtypeStruct((panel, width), BF16),
+            in_specs=vmem(2),
+            out_specs=pl.BlockSpec(memory_space=pltpu.VMEM),
+            compiler_params=params(panel * width * 6),
+            cost_estimate=cost(panel * width, panel * width * 6),
+            name="pack",
+        )(classifier, label_valid.reshape(1, panel))
+    ]
     for group in groups:
         own = pieces[0] if len(pieces) == 1 else jnp.concatenate(pieces, 0)
         pieces = [own] + [flip(own, "lab", mask) for mask in group_masks(group)]
@@ -136,7 +155,7 @@
         out_shape=[jax.ShapeDtypeStruct((half, docs), BF16)] * 2,
         in_specs=vmem(4),
         out_specs=vmem(2),
-        compiler_params=params(),
+        compiler_params=params(docs * slots * 44, docs * half * 4),
         cost_estimate=cost(docs * panel * slots * 40, docs * slots * 44 + docs * half * 4),
         name="targets",
     )(shortlist.T, slot_live.T, positive.T, negative.transpose(1, 2, 0))
@@ -152,7 +171,7 @@
         + [jax.ShapeDtypeStruct((half, width), BF16)],
         in_specs=vmem(len(pieces) + 4),
         out_specs=vmem(parts + 3),
-        compiler_params=params(),
+        compiler_params=params(4 * docs * width, 16 * half * docs, 12 * half * width),
         cost_estimate=cost(8 * docs * half * width, 4 * docs * width + 8 * half * docs + 8 * half * width),
         name="score",
     )(*pieces, embeddings, emb_other, target_mine, target_other)
@@ -172,14 +191,14 @@
         grad = grads[0]
     for bit in range(enc.bit_length() - 1):
         grad = grad + flip(grad.astype(BF16), "enc", 1 << bit).astype(F32)
-    w_grad = grad * (valid * (1.0 / math.sqrt(docs * enc * slots)))
+    w_grad = grad * (label_valid.astype(F32) * (1.0 / math.sqrt(docs * enc * slots)))[:, None]
 
     emb_grad = pl.pallas_call(
         emb_kernel,
         out_shape=jax.ShapeDtypeStruct((docs, width), F32),
         in_specs=vmem(4),
         out_specs=pl.BlockSpec(memory_space=pltpu.VMEM),
-        compiler_params=params(),
+        compiler_params=params(8 * docs * width, 4 * half * docs, 4 * half * width),
         cost_estimate=cost(4 * docs * half * width, 4 * docs * width + 4 * half * docs + 4 * half * width),
         name="emb_grad",
     )(d_own, flip(d_theirs, "lab", 1), classifier_own, flip(classifier_own, "lab", 1))

time: 44.6 us -> 40.4 us (0.906)
  Pallas kernels: 9.3 us -> 3.95 us
  local copies, waits for them, and re-layouts: 1.78 us -> 5.65 us
  other arithmetic: 3.42 us -> 0.83 us
    unnamed x18 -> x16, local copies, waits for them, and re-layouts: 1.78 us -> 5.65 us
    pallas_call x1, Pallas kernels: 3.82 us -> 1.33 us  [shards(): pl.pallas_call(functools.partial(score_kernel, pieces=len(pieces), parts=...]
    pallas_call x1, Pallas kernels: 2.47 us -> 0.79 us  [shards(): pl.pallas_call(functools.partial(targets_kernel, panel=panel), out_shape=...]
    pallas_call x1, Pallas kernels: 3.01 us -> 1.74 us  [shards(): pl.pallas_call(emb_kernel, out_shape=jax.ShapeDtypeStruct((docs, width),...]
    convert_element_type x1 -> x0, other arithmetic: 1.01 us -> none  [shards(): pieces = [jnp.where(valid > 0, classifier, 0.0).astype(BF16)]]
    convert_element_type x2, other arithmetic: 1 us -> 0.07 us  [shards(): grad = grad + flip(grad.astype(BF16), 'enc', 1 << bit).astype(F32)]
    gt x1 -> x0, other arithmetic: 0.66 us -> none  [shards(): pieces = [jnp.where(valid > 0, classifier, 0.0).astype(BF16)]]
  transfers between devices with their start and end apart: 12 -> 12, of which waited for: 8 -> 8; matrix products, arithmetic and copies ran while one was open for 6% -> 2% of each run, Pallas kernels for 6% -> 2%
where the time goes in v2:
time: 40.4 us; the launch traced here: 40.1 us
  waiting for transfers between devices  15 us (37%)
  starting transfers between devices  14 us (35%)
  local copies, waits for them, and re-layouts  5.65 us (14%)
  Pallas kernels  3.95 us (10%)
  other arithmetic  0.83 us (2%)
  between operations  0.68 us (2%)
    ppermute x12, waiting for transfers between devices, flip(): lax.ppermute(value, axis, [(i, i ^ mask) for i in range(lax.axis_size(axi...  15 us
    ppermute x12, starting transfers between devices, flip(): lax.ppermute(value, axis, [(i, i ^ mask) for i in range(lax.axis_size(axi...  14 us
    unnamed x16, local copies, waits for them, and re-layouts  5.65 us
    pallas_call x1, Pallas kernels, shards(): pl.pallas_call(emb_kernel, out_shape=jax.ShapeDtypeStruct((docs, width),...  1.74 us
    pallas_call x1, Pallas kernels, shards(): pl.pallas_call(functools.partial(score_kernel, pieces=len(pieces), parts=...  1.33 us
  transfers between devices with their start and end apart: 12, of which 8 were waited for; matrix products, arithmetic and copies ran while one was open for 2% of the time, Pallas kernels for 2%

profile of v2, /device:TPU:0, one launch (start us, length us, event | category | flops | bytes accessed | tf_op | source)
XLA Modules:
  0.0 40.1 jit_solution(3170918680408193316)
XLA Ops:
  0.6 0.5 %collective-permute-start.3 = (bf16[512,768]{1,0:T(8,128)(2,1)}, bf16[512,768]{1,0:T(8,128)(2,1)S(1)}, u32[]{:S(2)}, u32[]{:S(2)}) collective-permute-start(bf16[512,768]{1,0:T(8,128)(2,1)} %refs_4_.1), channel_id=1, source_target_pairs={{0,1},{1,0},{2,3},{3,2},{4,5},{5,4},{6,7},{7,6},{8,9},{9,8},{10,11... | collective-permute-start | bytes 2359304 | tf_op jit(solution)/shard_map/ppermute | solution.py:20
  1.1 0.0 copy-start.1
  1.2 0.8 %copy-done.1 = s32[512,4,8]{0,2,1:T(8,128)S(1)} copy-done((s32[512,4,8]{0,2,1:T(8,128)S(1)}, s32[512,4,8]{0,2,1:T(8,128)}, u32[]{:S(2)}) %copy-start.1) | copy-done | bytes 65560
  2.0 0.0 copy-start.2
  2.0 0.7 %copy-done.2 = s32[512,4]{0,1:T(4,128)S(1)} copy-done((s32[512,4]{0,1:T(4,128)S(1)}, s32[512,4]{0,1:T(4,128)}, u32[]{:S(2)}) %copy-start.2) | copy-done | bytes 8216
  2.7 0.0 copy-start.3
  2.7 0.7 %copy-done.3 = s32[512,4]{0,1:T(4,128)S(1)} copy-done((s32[512,4]{0,1:T(4,128)S(1)}, s32[512,4]{0,1:T(4,128)}, u32[]{:S(2)}) %copy-start.3) | copy-done | bytes 8216
  3.4 0.0 copy-start.4
  3.4 0.7 %copy-done.4 = s32[512,4]{0,1:T(4,128)S(1)} copy-done((s32[512,4]{0,1:T(4,128)S(1)}, s32[512,4]{0,1:T(4,128)}, u32[]{:S(2)}) %copy-start.4) | copy-done | bytes 8216
  4.1 0.8 %targets.1 = (bf16[256,512]{1,0:T(8,128)(2,1)S(1)}, bf16[256,512]{1,0:T(8,128)(2,1)S(1)}) custom-call(s32[4,512]{1,0:T(4,128)S(1)} %bitcast.6, s32[4,512]{1,0:T(4,128)S(1)} %bitcast.7, s32[4,512]{1,0:T(4,128)S(1)} %bitcast.8, s32[4,8,512]{2,1,0:T(8,128)S(1)} %bitcast.5), custom_call_target="tpu_custom_call" | custom-call | flops 5242880 | bytes 614400 | tf_op jit(solution)/shard_map/targets/pallas_call | solution.py:153
  4.9 0.1 collective-permute-start.4
  5.0 0.0 copy-start
  5.0 0.9 %copy-done = f32[64,768]{1,0:T(8,128)S(1)} copy-done((f32[64,768]{1,0:T(8,128)S(1)}, f32[64,768]{1,0:T(8,128)}, u32[]{:S(2)}) %copy-start) | copy-done | bytes 196632
  5.9 0.0 copy-start.5
  5.9 0.7 %copy-done.5 = s32[64]{0:T(128)S(1)} copy-done((s32[64]{0:T(128)S(1)}, s32[64]{0:T(128)}, u32[]{:S(2)}) %copy-start.5) | copy-done | bytes 280
  6.6 0.1 pack.1.refs_0_
  6.7 3.0 %collective-permute-start = (bf16[64,768]{1,0:T(8,128)(2,1)S(1)}, bf16[64,768]{1,0:T(8,128)(2,1)S(1)}, u32[]{:S(2)}, u32[]{:S(2)}) collective-permute-start(bf16[64,768]{1,0:T(8,128)(2,1)S(1)} %pack.1.refs_0_), channel_id=1, source_target_pairs={{0,2},{1,3},{2,0},{3,1},{4,6},{5,7},{6,4},{7,5},{8,10},{9,11},{10,... | collective-permute-start | bytes 294920 | tf_op jit(solution)/shard_map/ppermute | solution.py:20
  9.7 1.5 %collective-permute-start.1 = (bf16[64,768]{1,0:T(8,128)(2,1)S(1)}, bf16[64,768]{1,0:T(8,128)(2,1)S(1)}, u32[]{:S(2)}, u32[]{:S(2)}) collective-permute-start(bf16[64,768]{1,0:T(8,128)(2,1)S(1)} %pack.1.refs_0_), channel_id=1, source_target_pairs={{0,4},{1,5},{2,6},{3,7},{4,0},{5,1},{6,2},{7,3},{8,12},{9,13},{10,... | collective-permute-start | bytes 294920 | tf_op jit(solution)/shard_map/ppermute | solution.py:20
  11.2 0.0 collective-permute-start.2
  11.2 1.5 %collective-permute-done.refs_1_ = bf16[64,768]{1,0:T(8,128)(2,1)S(1)} collective-permute-done((bf16[64,768]{1,0:T(8,128)(2,1)S(1)}, bf16[64,768]{1,0:T(8,128)(2,1)S(1)}, u32[]{:S(2)}, u32[]{:S(2)}) %collective-permute-start) | collective-permute-done | bytes 98336 | tf_op jit(solution)/shard_map/ppermute | solution.py:20
  12.8 2.6 %collective-permute-done.1.refs_2_ = bf16[64,768]{1,0:T(8,128)(2,1)S(1)} collective-permute-done((bf16[64,768]{1,0:T(8,128)(2,1)S(1)}, bf16[64,768]{1,0:T(8,128)(2,1)S(1)}, u32[]{:S(2)}, u32[]{:S(2)}) %collective-permute-start.1) | collective-permute-done | bytes 98336 | tf_op jit(solution)/shard_map/ppermute | solution.py:20
  15.4 1.3 %collective-permute-done.2.refs_3_ = bf16[64,768]{1,0:T(8,128)(2,1)S(1)} collective-permute-done((bf16[64,768]{1,0:T(8,128)(2,1)S(1)}, bf16[64,768]{1,0:T(8,128)(2,1)S(1)}, u32[]{:S(2)}, u32[]{:S(2)}) %collective-permute-start.2) | collective-permute-done | bytes 98336 | tf_op jit(solution)/shard_map/ppermute | solution.py:20
  16.7 0.0 collective-permute-done.4.refs_7_
  16.7 0.0 collective-permute-done.3.refs_5_
  16.7 0.0 copy-start.7
  16.7 1.1 %copy-done.7 = bf16[512,768]{1,0:T(8,128)(2,1)S(1)} copy-done((bf16[512,768]{1,0:T(8,128)(2,1)S(1)}, bf16[512,768]{1,0:T(8,128)(2,1)}, u32[]{:S(2)}) %copy-start.7) | copy-done | bytes 786456
  17.9 0.0 copy-start.6
  17.9 1.3 %score.1 = (f32[64,768]{1,0:T(8,128)S(1)}, bf16[64,768]{1,0:T(8,128)(2,1)S(1)}, bf16[64,768]{1,0:T(8,128)(2,1)S(1)}, bf16[64,768]{1,0:T(8,128)(2,1)S(1)}, bf16[2...) custom-call(bf16[64,768]{1,0:T(8,128)(2,1)S(1)} %pack.1.refs_0_, ...), custom_call_target="tpu_custom_call" | custom-call | flops 805306368 | bytes 4194304 | tf_op jit(solution)/shard_map/score/pallas_call | solution.py:165
  19.2 1.1 %collective-permute-start.7 = (bf16[64,768]{1,0:T(8,128)(2,1)S(1)}, bf16[64,768]{1,0:T(8,128)(2,1)S(1)}, u32[]{:S(2)}, u32[]{:S(2)}) collective-permute-start(bf16[64,768]{1,0:T(8,128)(2,1)S(1)} %get-tuple-element.16), channel_id=1, source_target_pairs={{0,6},{1,7},{2,4},{3,5},{4,2},{5,3},{6,0},{7,1},{8,14},{9,15},{10,... | collective-permute-start | bytes 294920 | tf_op jit(solution)/shard_map/ppermute | solution.py:20
  20.3 1.2 %collective-permute-start.6 = (bf16[64,768]{1,0:T(8,128)(2,1)S(1)}, bf16[64,768]{1,0:T(8,128)(2,1)S(1)}, u32[]{:S(2)}, u32[]{:S(2)}) collective-permute-start(bf16[64,768]{1,0:T(8,128)(2,1)S(1)} %get-tuple-element.15), channel_id=1, source_target_pairs={{0,4},{1,5},{2,6},{3,7},{4,0},{5,1},{6,2},{7,3},{8,12},{9,13},{10,... | collective-permute-start | bytes 294920 | tf_op jit(solution)/shard_map/ppermute | solution.py:20
  21.5 1.3 %collective-permute-start.5 = (bf16[64,768]{1,0:T(8,128)(2,1)S(1)}, bf16[64,768]{1,0:T(8,128)(2,1)S(1)}, u32[]{:S(2)}, u32[]{:S(2)}) collective-permute-start(bf16[64,768]{1,0:T(8,128)(2,1)S(1)} %get-tuple-element.14), channel_id=1, source_target_pairs={{0,2},{1,3},{2,0},{3,1},{4,6},{5,7},{6,4},{7,5},{8,10},{9,11},{10,... | collective-permute-start | bytes 294920 | tf_op jit(solution)/shard_map/ppermute | solution.py:20
  22.8 2.2 %collective-permute-done.7 = bf16[64,768]{1,0:T(8,128)(2,1)S(1)} collective-permute-done((bf16[64,768]{1,0:T(8,128)(2,1)S(1)}, bf16[64,768]{1,0:T(8,128)(2,1)S(1)}, u32[]{:S(2)}, u32[]{:S(2)}) %collective-permute-start.7) | collective-permute-done | bytes 98336 | tf_op jit(solution)/shard_map/ppermute | solution.py:20
  24.9 1.0 %collective-permute-done.6 = bf16[64,768]{1,0:T(8,128)(2,1)S(1)} collective-permute-done((bf16[64,768]{1,0:T(8,128)(2,1)S(1)}, bf16[64,768]{1,0:T(8,128)(2,1)S(1)}, u32[]{:S(2)}, u32[]{:S(2)}) %collective-permute-start.6) | collective-permute-done | bytes 98336 | tf_op jit(solution)/shard_map/ppermute | solution.py:20
  25.9 0.2 collective-permute-done.5
  26.1 0.1 fusion.1
  26.1 1.6 %collective-permute-start.8 = (bf16[64,768]{1,0:T(8,128)(2,1)S(1)}, bf16[64,768]{1,0:T(8,128)(2,1)S(1)}, u32[]{:S(2)}, u32[]{:S(2)}) collective-permute-start(bf16[64,768]{1,0:T(8,128)(2,1)S(1)} %get-tuple-element.20), channel_id=1, source_target_pairs={{0,8},{8,0},{16,24},{24,16},{1,9},{9,1},{17,25},{25,17},{2,10},{10... | collective-permute-start | bytes 294920 | tf_op jit(solution)/shard_map/ppermute | solution.py:20
  27.8 0.0 collective-permute-start.10
  27.8 0.5 %collective-permute-start.11 = (bf16[256,768]{1,0:T(8,128)(2,1)S(1)}, bf16[256,768]{1,0:T(8,128)(2,1)S(1)}, u32[]{:S(2)}, u32[]{:S(2)}) collective-permute-start(bf16[256,768]{1,0:T(8,128)(2,1)S(1)} %get-tuple-element.19.c_own_ref), channel_id=1, source_target_pairs={{0,1},{1,0},{2,3},{3,2},{4,5},{5,4},{6,7},{7,6},{8,9},{9,8},{10,11... | collective-permute-start | bytes 1179656 | tf_op jit(solution)/shard_map/ppermute | solution.py:20
  28.3 2.5 %collective-permute-done.8 = bf16[64,768]{1,0:T(8,128)(2,1)S(1)} collective-permute-done((bf16[64,768]{1,0:T(8,128)(2,1)S(1)}, bf16[64,768]{1,0:T(8,128)(2,1)S(1)}, u32[]{:S(2)}, u32[]{:S(2)}) %collective-permute-start.8) | collective-permute-done | bytes 98336 | tf_op jit(solution)/shard_map/ppermute | solution.py:20
  30.8 3.1 %collective-permute-start.9 = (bf16[64,768]{1,0:T(8,128)(2,1)S(1)}, bf16[64,768]{1,0:T(8,128)(2,1)S(1)}, u32[]{:S(2)}, u32[]{:S(2)}) collective-permute-start(bf16[64,768]{1,0:T(8,128)(2,1)S(1)} %fusion), channel_id=1, source_target_pairs={{0,16},{8,24},{16,0},{24,8},{1,17},{9,25},{17,1},{25,9},{2,18},{10... | collective-permute-start | bytes 294920 | tf_op jit(solution)/shard_map/ppermute | solution.py:20
  33.9 0.0 copy-done.6
  33.9 3.6 %collective-permute-done.9 = bf16[64,768]{1,0:T(8,128)(2,1)S(1)} collective-permute-done((bf16[64,768]{1,0:T(8,128)(2,1)S(1)}, bf16[64,768]{1,0:T(8,128)(2,1)S(1)}, u32[]{:S(2)}, u32[]{:S(2)}) %collective-permute-start.9) | collective-permute-done | bytes 98336 | tf_op jit(solution)/shard_map/ppermute | solution.py:20
  37.6 0.8 %add_multiply_fusion = f32[64,768]{1,0:T(8,128)} fusion(bf16[64,768]{1,0:T(8,128)(2,1)S(1)} %collective-permute-done.9, f32[64,768]{1,0:T(8,128)S(1)} %get-tuple-element.21, bf16[64,768]{1,0:T(8,128)(2,1)S(1)} %collective-permute-done.8, f32[64]{0:T(128)S(1)} %convert_multiply_fusion), kind=kLoop, calls=%fused_computation | loop fusion | flops 245760 | bytes 590080 | tf_op jit(solution)/shard_map/mul | solution.py:194
  38.3 0.0 collective-permute-done.10.d_other_ref
  38.3 0.0 collective-permute-done.11.c_other_ref
  38.3 1.7 %emb_grad.1 = f32[512,768]{1,0:T(8,128)} custom-call(bf16[256,512]{1,0:T(8,128)(2,1)S(1)} %get-tuple-element.17.d_own_ref, bf16[256,512]{1,0:T(8,128)(2,1)S(1)} %collective-permute-done.10.d_other_ref, bf16[256,768]{1,0:T(8,128)(2,1)S(1)} %get-tuple-element.19.c_own_ref, bf16[256,768]{1,0:T(8,128)(2,1)S(1)} %collective-permute-done.11.c_other_ref), custom_call_target="tpu_custom_call" | custom-call | flops 402653184 | bytes 2883584 | tf_op jit(solution)/shard_map/emb_grad/pallas_call | solution.py:196
  (2 shorter events, 0.0 us)
Async XLA Ops:
  0.6 16.1 %collective-permute-start.3 = (bf16[512,768]{1,0:T(8,128)(2,1)}, bf16[512,768]{1,0:T(8,128)(2,1)S(1)}, u32[]{:S(2)}, u32[]{:S(2)}) collective-permute-start(bf16[512,768]{1,0:T(8,128)(2,1)} %refs_4_.1), channel_id=1, source_target_pairs={{0,1},{1,0},{2,3},{3,2},{4,5},{5,4},{6,7},{7,6},{8,9},{9,8},{10,11... | collective-permute-start | bytes 2359304 | tf_op jit(solution)/shard_map/ppermute | solution.py:20
  1.1 0.8 %copy-start.1 = (s32[512,4,8]{0,2,1:T(8,128)S(1)}, s32[512,4,8]{0,2,1:T(8,128)}, u32[]{:S(2)}) copy-start(s32[512,4,8]{0,2,1:T(8,128)} %param.13) | copy-start | bytes 196612
  2.0 0.7 %copy-start.2 = (s32[512,4]{0,1:T(4,128)S(1)}, s32[512,4]{0,1:T(4,128)}, u32[]{:S(2)}) copy-start(s32[512,4]{0,1:T(4,128)} %param.10) | copy-start | bytes 24580
  2.7 0.7 %copy-start.3 = (s32[512,4]{0,1:T(4,128)S(1)}, s32[512,4]{0,1:T(4,128)}, u32[]{:S(2)}) copy-start(s32[512,4]{0,1:T(4,128)} %param.11) | copy-start | bytes 24580
  3.4 0.7 %copy-start.4 = (s32[512,4]{0,1:T(4,128)S(1)}, s32[512,4]{0,1:T(4,128)}, u32[]{:S(2)}) copy-start(s32[512,4]{0,1:T(4,128)} %param.12) | copy-start | bytes 24580
  4.9 11.8 %collective-permute-start.4 = (bf16[256,512]{1,0:T(8,128)(2,1)S(1)}, bf16[256,512]{1,0:T(8,128)(2,1)S(1)}, u32[]{:S(2)}, u32[]{:S(2)}) collective-permute-start(bf16[256,512]{1,0:T(8,128)(2,1)S(1)} %get-tuple-element.12), channel_id=1, source_target_pairs={{0,1},{1,0},{2,3},{3,2},{4,5},{5,4},{6,7},{7,6},{8,9},{9,8},{10,11... | collective-permute-start | bytes 786440 | tf_op jit(solution)/shard_map/ppermute | solution.py:20
  5.0 0.9 %copy-start = (f32[64,768]{1,0:T(8,128)S(1)}, f32[64,768]{1,0:T(8,128)}, u32[]{:S(2)}) copy-start(f32[64,768]{1,0:T(8,128)} %classifier_ref.1) | copy-start | bytes 589828
  5.9 0.7 %copy-start.5 = (s32[64]{0:T(128)S(1)}, s32[64]{0:T(128)}, u32[]{:S(2)}) copy-start(s32[64]{0:T(128)} %param.9) | copy-start | bytes 772
  6.7 6.1 %collective-permute-start = (bf16[64,768]{1,0:T(8,128)(2,1)S(1)}, bf16[64,768]{1,0:T(8,128)(2,1)S(1)}, u32[]{:S(2)}, u32[]{:S(2)}) collective-permute-start(bf16[64,768]{1,0:T(8,128)(2,1)S(1)} %pack.1.refs_0_), channel_id=1, source_target_pairs={{0,2},{1,3},{2,0},{3,1},{4,6},{5,7},{6,4},{7,5},{8,10},{9,11},{10,... | collective-permute-start | bytes 294920 | tf_op jit(solution)/shard_map/ppermute | solution.py:20
  9.7 5.7 %collective-permute-start.1 = (bf16[64,768]{1,0:T(8,128)(2,1)S(1)}, bf16[64,768]{1,0:T(8,128)(2,1)S(1)}, u32[]{:S(2)}, u32[]{:S(2)}) collective-permute-start(bf16[64,768]{1,0:T(8,128)(2,1)S(1)} %pack.1.refs_0_), channel_id=1, source_target_pairs={{0,4},{1,5},{2,6},{3,7},{4,0},{5,1},{6,2},{7,3},{8,12},{9,13},{10,... | collective-permute-start | bytes 294920 | tf_op jit(solution)/shard_map/ppermute | solution.py:20
  11.2 5.5 %collective-permute-start.2 = (bf16[64,768]{1,0:T(8,128)(2,1)S(1)}, bf16[64,768]{1,0:T(8,128)(2,1)S(1)}, u32[]{:S(2)}, u32[]{:S(2)}) collective-permute-start(bf16[64,768]{1,0:T(8,128)(2,1)S(1)} %pack.1.refs_0_), channel_id=1, source_target_pairs={{0,6},{1,7},{2,4},{3,5},{4,2},{5,3},{6,0},{7,1},{8,14},{9,15},{10,... | collective-permute-start | bytes 294920 | tf_op jit(solution)/shard_map/ppermute | solution.py:20
  16.7 1.1 %copy-start.7 = (bf16[512,768]{1,0:T(8,128)(2,1)S(1)}, bf16[512,768]{1,0:T(8,128)(2,1)}, u32[]{:S(2)}) copy-start(bf16[512,768]{1,0:T(8,128)(2,1)} %refs_4_.1) | copy-start | bytes 2359300
  17.9 16.0 %copy-start.6 = (s32[64]{0:T(128)S(1)}, s32[64]{0:T(128)}, u32[]{:S(2)}) copy-start(s32[64]{0:T(128)} %param.9) | copy-start | bytes 772
  19.2 5.7 %collective-permute-start.7 = (bf16[64,768]{1,0:T(8,128)(2,1)S(1)}, bf16[64,768]{1,0:T(8,128)(2,1)S(1)}, u32[]{:S(2)}, u32[]{:S(2)}) collective-permute-start(bf16[64,768]{1,0:T(8,128)(2,1)S(1)} %get-tuple-element.16), channel_id=1, source_target_pairs={{0,6},{1,7},{2,4},{3,5},{4,2},{5,3},{6,0},{7,1},{8,14},{9,15},{10,... | collective-permute-start | bytes 294920 | tf_op jit(solution)/shard_map/ppermute | solution.py:20
  20.3 5.6 %collective-permute-start.6 = (bf16[64,768]{1,0:T(8,128)(2,1)S(1)}, bf16[64,768]{1,0:T(8,128)(2,1)S(1)}, u32[]{:S(2)}, u32[]{:S(2)}) collective-permute-start(bf16[64,768]{1,0:T(8,128)(2,1)S(1)} %get-tuple-element.15), channel_id=1, source_target_pairs={{0,4},{1,5},{2,6},{3,7},{4,0},{5,1},{6,2},{7,3},{8,12},{9,13},{10,... | collective-permute-start | bytes 294920 | tf_op jit(solution)/shard_map/ppermute | solution.py:20
  21.5 4.6 %collective-permute-start.5 = (bf16[64,768]{1,0:T(8,128)(2,1)S(1)}, bf16[64,768]{1,0:T(8,128)(2,1)S(1)}, u32[]{:S(2)}, u32[]{:S(2)}) collective-permute-start(bf16[64,768]{1,0:T(8,128)(2,1)S(1)} %get-tuple-element.14), channel_id=1, source_target_pairs={{0,2},{1,3},{2,0},{3,1},{4,6},{5,7},{6,4},{7,5},{8,10},{9,11},{10,... | collective-permute-start | bytes 294920 | tf_op jit(solution)/shard_map/ppermute | solution.py:20
  26.1 4.7 %collective-permute-start.8 = (bf16[64,768]{1,0:T(8,128)(2,1)S(1)}, bf16[64,768]{1,0:T(8,128)(2,1)S(1)}, u32[]{:S(2)}, u32[]{:S(2)}) collective-permute-start(bf16[64,768]{1,0:T(8,128)(2,1)S(1)} %get-tuple-element.20), channel_id=1, source_target_pairs={{0,8},{8,0},{16,24},{24,16},{1,9},{9,1},{17,25},{25,17},{2,10},{10... | collective-permute-start | bytes 294920 | tf_op jit(solution)/shard_map/ppermute | solution.py:20
  27.8 10.5 %collective-permute-start.10 = (bf16[256,512]{1,0:T(8,128)(2,1)S(1)}, bf16[256,512]{1,0:T(8,128)(2,1)S(1)}, u32[]{:S(2)}, u32[]{:S(2)}) collective-permute-start(bf16[256,512]{1,0:T(8,128)(2,1)S(1)} %get-tuple-element.18), channel_id=1, source_target_pairs={{0,1},{1,0},{2,3},{3,2},{4,5},{5,4},{6,7},{7,6},{8,9},{9,8},{10,11... | collective-permute-start | bytes 786440 | tf_op jit(solution)/shard_map/ppermute | solution.py:20
  27.8 10.5 %collective-permute-start.11 = (bf16[256,768]{1,0:T(8,128)(2,1)S(1)}, bf16[256,768]{1,0:T(8,128)(2,1)S(1)}, u32[]{:S(2)}, u32[]{:S(2)}) collective-permute-start(bf16[256,768]{1,0:T(8,128)(2,1)S(1)} %get-tuple-element.19.c_own_ref), channel_id=1, source_target_pairs={{0,1},{1,0},{2,3},{3,2},{4,5},{5,4},{6,7},{7,6},{8,9},{9,8},{10,11... | collective-permute-start | bytes 1179656 | tf_op jit(solution)/shard_map/ppermute | solution.py:20
  30.8 6.7 %collective-permute-start.9 = (bf16[64,768]{1,0:T(8,128)(2,1)S(1)}, bf16[64,768]{1,0:T(8,128)(2,1)S(1)}, u32[]{:S(2)}, u32[]{:S(2)}) collective-permute-start(bf16[64,768]{1,0:T(8,128)(2,1)S(1)} %fusion), channel_id=1, source_target_pairs={{0,16},{8,24},{16,0},{24,8},{1,17},{9,25},{17,1},{25,9},{2,18},{10... | collective-permute-start | bytes 294920 | tf_op jit(solution)/shard_map/ppermute | solution.py:20

commit v3 on v1

--- a/solution.py
+++ b/solution.py
@@ -13,7 +13,7 @@
 LANES = 128
 SUBLANES = 8
 ROWS = 256
-VMEM_LIMIT = 56 * 1024 * 1024
+MIB = 1024 * 1024
 
 
 def flip(value, axis, mask):
@@ -29,7 +29,35 @@
     return [group[0]] if len(group) == 1 else [group[0], group[1], group[0] | group[1]]
 
 
-def targets_kernel(short_ref, live_ref, pos_ref, neg_ref, mine_ref, theirs_ref, *, panel):
+def fetch(sources, targets, sem):
+    copies = [pltpu.make_async_copy(x, y, sem.at[i]) for i, (x, y) in enumerate(zip(sources, targets))]
+    for copy in copies:
+        copy.start()
+    for copy in copies:
+        copy.wait()
+
+
+def flag_column(flags):
+    panel = flags.shape[1]
+    diagonal = lax.broadcasted_iota(jnp.int32, (panel, panel), 0) == lax.broadcasted_iota(
+        jnp.int32, (panel, panel), 1
+    )
+    spread = jnp.broadcast_to(flags.astype(F32), (panel, panel))
+    return jnp.sum(jnp.where(diagonal, spread, 0.0), axis=1, keepdims=True)
+
+
+def pack_kernel(classifier_hbm, valid_hbm, out_ref, classifier_ref, valid_ref, sem):
+    fetch((classifier_hbm, valid_hbm), (classifier_ref, valid_ref), sem)
+    out_ref[...] = (classifier_ref[...] * flag_column(valid_ref[...])).astype(BF16)
+
+
+def targets_kernel(
+    short_hbm, live_hbm, pos_hbm, neg_hbm, emb_hbm, after_ref, mine_ref, theirs_ref, emb_ref,
+    short_ref, live_ref, pos_ref, neg_ref, sem, emb_sem, *, panel
+):
+    emb_copy = pltpu.make_async_copy(emb_hbm, emb_ref, emb_sem)
+    emb_copy.start()
+    fetch((short_hbm, live_hbm, pos_hbm, neg_hbm), (short_ref, live_ref, pos_ref, neg_ref), sem)
     me = lax.axis_index("lab")
     slots, docs = short_ref.shape
     negatives = neg_ref.shape[1]
@@ -62,6 +90,7 @@
         return carry
 
     lax.fori_loop(0, docs // LANES, chunk, 0)
+    emb_copy.wait()
 
 
 def score_kernel(*refs, pieces, parts):
@@ -96,23 +125,37 @@
             ref[at : at + step] = grad[off : off + step].astype(ref.dtype)
 
 
-def emb_kernel(d_own_ref, d_other_ref, c_own_ref, c_other_ref, out_ref):
+def emb_kernel(d_own_ref, d_other_ref, c_own_ref, c_other_ref, after_ref, out_ref):
     dims = (((0,), (0,)), ((), ()))
     out_ref[...] = lax.dot_general(
         d_own_ref[...], c_own_ref[...], dims, preferred_element_type=F32
     ) + lax.dot_general(d_other_ref[...], c_other_ref[...], dims, preferred_element_type=F32)
 
 
+def finish_kernel(grad_ref, received_ref, valid_hbm, after_hbm, out_ref, valid_ref, sem, *, scale):
+    fetch((valid_hbm,), (valid_ref,), sem)
+    column = flag_column(valid_ref[...]) * scale
+    out_ref[...] = (grad_ref[...] + received_ref[...].astype(F32)) * column
+
+
+def hbm(count):
+    return [pl.BlockSpec(memory_space=pltpu.HBM)] * count
+
+
 def vmem(count):
     return [pl.BlockSpec(memory_space=pltpu.VMEM)] * count
 
 
+def keep(*arrays):
+    return [pltpu.with_memory_space_constraint(x, pltpu.HBM) for x in arrays]
+
+
 def cost(flops, nbytes):
     return pl.CostEstimate(flops=flops, bytes_accessed=nbytes, transcendentals=0)
 
 
-def params():
-    return pltpu.CompilerParams(vmem_limit_bytes=VMEM_LIMIT)
+def params(*sizes):
+    return pltpu.CompilerParams(vmem_limit_bytes=(2 * sum(sizes) // MIB + 4) * MIB)
 
 
 def shards(embeddings, classifier, label_valid, shortlist, slot_live, positive, negative):
@@ -124,22 +167,43 @@
     half = lab // 2 * panel
     groups = bit_groups(lab)
 
-    valid = label_valid.astype(F32)[:, None]
-    pieces = [jnp.where(valid > 0, classifier, 0.0).astype(BF16)]
+    valid = label_valid.reshape(1, panel)
+    packed = pl.pallas_call(
+        pack_kernel,
+        out_shape=jax.ShapeDtypeStruct((panel, width), BF16),
+        in_specs=hbm(2),
+        out_specs=pl.BlockSpec(memory_space=pltpu.VMEM),
+        scratch_shapes=[
+            pltpu.VMEM((panel, width), F32),
+            pltpu.VMEM((1, panel), jnp.int32),
+            pltpu.SemaphoreType.DMA((2,)),
+        ],
+        compiler_params=params(panel * width * 6),
+        cost_estimate=cost(panel * width, panel * width * 6),
+        name="pack",
+    )(*keep(classifier, valid))
+    pieces = [packed]
     for group in groups:
         own = pieces[0] if len(pieces) == 1 else jnp.concatenate(pieces, 0)
         pieces = [own] + [flip(own, "lab", mask) for mask in group_masks(group)]
 
     emb_other = flip(embeddings, "lab", 1)
-    target_mine, target_theirs = pl.pallas_call(
+    target_mine, target_theirs, emb_own = pl.pallas_call(
         functools.partial(targets_kernel, panel=panel),
-        out_shape=[jax.ShapeDtypeStruct((half, docs), BF16)] * 2,
-        in_specs=vmem(4),
-        out_specs=vmem(2),
-        compiler_params=params(),
+        out_shape=[jax.ShapeDtypeStruct((half, docs), BF16)] * 2
+        + [jax.ShapeDtypeStruct((docs, width), BF16)],
+        in_specs=hbm(5) + vmem(1),
+        out_specs=vmem(3),
+        scratch_shapes=[pltpu.VMEM((slots, docs), jnp.int32)] * 3
+        + [
+            pltpu.VMEM((slots, negative.shape[2], docs), jnp.int32),
+            pltpu.SemaphoreType.DMA((4,)),
+            pltpu.SemaphoreType.DMA,
+        ],
+        compiler_params=params(docs * slots * 44, docs * half * 4, docs * width * 2),
         cost_estimate=cost(docs * panel * slots * 40, docs * slots * 44 + docs * half * 4),
         name="targets",
-    )(shortlist.T, slot_live.T, positive.T, negative.transpose(1, 2, 0))
+    )(*keep(shortlist.T, slot_live.T, positive.T, negative.transpose(1, 2, 0), embeddings), packed)
     target_other = flip(target_theirs, "lab", 1)
 
     parts = len(group_masks(groups[-1])) + 1 if groups else 1
@@ -152,10 +216,10 @@
         + [jax.ShapeDtypeStruct((half, width), BF16)],
         in_specs=vmem(len(pieces) + 4),
         out_specs=vmem(parts + 3),
-        compiler_params=params(),
+        compiler_params=params(4 * docs * width, 16 * half * docs, 12 * half * width),
         cost_estimate=cost(8 * docs * half * width, 4 * docs * width + 8 * half * docs + 8 * half * width),
         name="score",
-    )(*pieces, embeddings, emb_other, target_mine, target_other)
+    )(*pieces, emb_own, emb_other, target_mine, target_other)
     grads, (d_own, d_theirs, classifier_own) = outs[:parts], outs[parts:]
 
     grad = None
@@ -170,19 +234,32 @@
             grad = grad + r.astype(F32)
     if grad is None:
         grad = grads[0]
-    for bit in range(enc.bit_length() - 1):
-        grad = grad + flip(grad.astype(BF16), "enc", 1 << bit).astype(F32)
-    w_grad = grad * (valid * (1.0 / math.sqrt(docs * enc * slots)))
+    d_other, classifier_other = flip(d_theirs, "lab", 1), flip(classifier_own, "lab", 1)
+    bits = [1 << bit for bit in range(enc.bit_length() - 1)]
+    for bit in bits[:-1]:
+        grad = grad + flip(grad.astype(BF16), "enc", bit).astype(F32)
+    received = flip(grad.astype(BF16), "enc", bits[-1])
 
     emb_grad = pl.pallas_call(
         emb_kernel,
         out_shape=jax.ShapeDtypeStruct((docs, width), F32),
-        in_specs=vmem(4),
+        in_specs=vmem(5),
         out_specs=pl.BlockSpec(memory_space=pltpu.VMEM),
-        compiler_params=params(),
+        compiler_params=params(8 * docs * width, 4 * half * docs, 4 * half * width),
         cost_estimate=cost(4 * docs * half * width, 4 * docs * width + 4 * half * docs + 4 * half * width),
         name="emb_grad",
-    )(d_own, flip(d_theirs, "lab", 1), classifier_own, flip(classifier_own, "lab", 1))
+    )(d_own, d_other, classifier_own, classifier_other, grad)
+
+    w_grad = pl.pallas_call(
+        functools.partial(finish_kernel, scale=1.0 / math.sqrt(docs * enc * slots)),
+        out_shape=jax.ShapeDtypeStruct((panel, width), F32),
+        in_specs=vmem(2) + hbm(2),
+        out_specs=pl.BlockSpec(memory_space=pltpu.VMEM),
+        scratch_shapes=[pltpu.VMEM((1, panel), jnp.int32), pltpu.SemaphoreType.DMA((1,))],
+        compiler_params=params(panel * width * 10),
+        cost_estimate=cost(panel * width, panel * width * 10),
+        name="finish",
+    )(grad, received, *keep(valid, emb_grad))
     return (w_grad, emb_grad)
 
 

time: 44.6 us -> 35.1 us (0.79)
  other arithmetic: 3.42 us -> 0.12 us
  waiting for transfers between devices: 15.2 us -> 13.1 us
  Pallas kernels: 9.3 us -> 7.51 us
  local copies, waits for them, and re-layouts: 1.78 us -> 0 us
    pallas_call x1, Pallas kernels: 3.82 us -> 1.33 us  [shards(): pl.pallas_call(functools.partial(score_kernel, pieces=len(pieces), parts=...]
    pallas_call x0 -> x2, Pallas kernels: none -> 2.47 us  [the longest x1 1.43 us: shards(): pl.pallas_call(functools.partial(finish_kernel, scale=1.0 / math.sqrt(doc...]
    ppermute x12, waiting for transfers between devices: 15.2 us -> 13.1 us  [flip(): lax.ppermute(value, axis, [(i, i ^ mask) for i in range(lax.axis_size(axi...]
    convert_element_type x3 -> x2, other arithmetic: 2 us -> 0.12 us  [the longest x1 0.06 us: shards(): received = flip(grad.astype(BF16), 'enc', bits[-1])]
    unnamed x18 -> x0, local copies, waits for them, and re-layouts: 1.78 us -> none
    pallas_call x1, Pallas kernels: 3.01 us -> 1.75 us  [shards(): pl.pallas_call(emb_kernel, out_shape=jax.ShapeDtypeStruct((docs, width),...]
    mul x2 -> x0, other arithmetic: 0.76 us -> none  [shards(): w_grad = grad * (valid * (1.0 / math.sqrt(docs * enc * slots)))]
    gt x1 -> x0, other arithmetic: 0.66 us -> none  [shards(): pieces = [jnp.where(valid > 0, classifier, 0.0).astype(BF16)]]
  transfers between devices with their start and end apart: 12 -> 12, of which waited for: 8 -> 7; matrix products, arithmetic and copies ran while one was open for 6% -> 0% of each run, Pallas kernels for 6% -> 14%
where the time goes in v3:
time: 35.1 us; the launch traced here: 34.9 us
  starting transfers between devices  13.5 us (38%)
  waiting for transfers between devices  13.1 us (37%)
  Pallas kernels  7.51 us (21%)
  between operations  0.67 us (2%)
    ppermute x12, starting transfers between devices, flip(): lax.ppermute(value, axis, [(i, i ^ mask) for i in range(lax.axis_size(axi...  13.5 us
    ppermute x12, waiting for transfers between devices, flip(): lax.ppermute(value, axis, [(i, i ^ mask) for i in range(lax.axis_size(axi...  13.1 us
    pallas_call x1, Pallas kernels, shards(): pl.pallas_call(functools.partial(targets_kernel, panel=panel), out_shape=...  1.97 us
    pallas_call x1, Pallas kernels, shards(): pl.pallas_call(emb_kernel, out_shape=jax.ShapeDtypeStruct((docs, width),...  1.75 us
    pallas_call x1, Pallas kernels, shards(): pl.pallas_call(functools.partial(finish_kernel, scale=1.0 / math.sqrt(doc...  1.43 us
    pallas_call x1, Pallas kernels, shards(): pl.pallas_call(functools.partial(score_kernel, pieces=len(pieces), parts=...  1.33 us
    pallas_call x1, Pallas kernels, shards(): pl.pallas_call(pack_kernel, out_shape=jax.ShapeDtypeStruct((panel, width)...  1.04 us
  transfers between devices with their start and end apart: 12, of which 7 were waited for; matrix products, arithmetic and copies ran while one was open for 0% of the time, Pallas kernels for 14%

profile of v3, /device:TPU:0, one launch (start us, length us, event | category | flops | bytes accessed | tf_op | source)
XLA Modules:
  0.0 34.9 jit_solution(14393160842709011554)
XLA Ops:
  0.6 0.5 %collective-permute-start.3 = (bf16[512,768]{1,0:T(8,128)(2,1)}, bf16[512,768]{1,0:T(8,128)(2,1)S(1)}, u32[]{:S(2)}, u32[]{:S(2)}) collective-permute-start(bf16[512,768]{1,0:T(8,128)(2,1)} %emb_hbm.1), channel_id=1, source_target_pairs={{0,1},{1,0},{2,3},{3,2},{4,5},{5,4},{6,7},{7,6},{8,9},{9,8},{10,11... | collective-permute-start | bytes 2359304 | tf_op jit(solution)/shard_map/ppermute | solution.py:20
  1.1 1.0 %pack.1.after_ref.refs_0_ = bf16[64,768]{1,0:T(8,128)(2,1)S(1)} custom-call(f32[64,768]{1,0:T(8,128)} %classifier_hbm.1, s32[1,64]{1,0:T(1,128)} %bitcast.9), custom_call_target="tpu_custom_call" | custom-call | flops 49152 | bytes 294912 | tf_op jit(solution)/shard_map/pack/pallas_call | solution.py:171
  2.2 2.0 %targets.1 = (bf16[256,512]{1,0:T(8,128)(2,1)S(1)}, bf16[256,512]{1,0:T(8,128)(2,1)S(1)}, bf16[512,768]{1,0:T(8,128)(2,1)S(1)}) custom-call(s32[4,512]{1,0:T(4,128)} %bitcast.6, s32[4,512]{1,0:T(4,128)} %bitcast.7, s32[4,512]{1,0:T(4,128)} %bitcast.8, s32[4,8,512]{2,1,0:T(8,128)} %bitcast.5, bf16[512,768]{1,0:T(8,128)(2,1)} %emb_hbm.1, ...), custom_call_target="tpu_custom_call" | custom-call | flops 5242880 | bytes 614400 | tf_op jit(solution)/shard_map/targets/pallas_call | solution.py:191
  4.2 0.1 collective-permute-start.4
  4.3 3.9 %collective-permute-start.2 = (bf16[64,768]{1,0:T(8,128)(2,1)S(1)}, bf16[64,768]{1,0:T(8,128)(2,1)S(1)}, u32[]{:S(2)}, u32[]{:S(2)}) collective-permute-start(bf16[64,768]{1,0:T(8,128)(2,1)S(1)} %pack.1.after_ref.refs_0_), channel_id=1, source_target_pairs={{0,6},{1,7},{2,4},{3,5},{4,2},{5,3},{6,0},{7,1},{8,14},{9,15},{10,... | collective-permute-start | bytes 294920 | tf_op jit(solution)/shard_map/ppermute | solution.py:20
  8.2 0.5 %collective-permute-start.1 = (bf16[64,768]{1,0:T(8,128)(2,1)S(1)}, bf16[64,768]{1,0:T(8,128)(2,1)S(1)}, u32[]{:S(2)}, u32[]{:S(2)}) collective-permute-start(bf16[64,768]{1,0:T(8,128)(2,1)S(1)} %pack.1.after_ref.refs_0_), channel_id=1, source_target_pairs={{0,4},{1,5},{2,6},{3,7},{4,0},{5,1},{6,2},{7,3},{8,12},{9,13},{10,... | collective-permute-start | bytes 294920 | tf_op jit(solution)/shard_map/ppermute | solution.py:20
  8.7 0.1 collective-permute-start
  8.8 2.6 %collective-permute-done.2.refs_3_ = bf16[64,768]{1,0:T(8,128)(2,1)S(1)} collective-permute-done((bf16[64,768]{1,0:T(8,128)(2,1)S(1)}, bf16[64,768]{1,0:T(8,128)(2,1)S(1)}, u32[]{:S(2)}, u32[]{:S(2)}) %collective-permute-start.2) | collective-permute-done | bytes 98336 | tf_op jit(solution)/shard_map/ppermute | solution.py:20
  11.4 1.9 %collective-permute-done.1.refs_2_ = bf16[64,768]{1,0:T(8,128)(2,1)S(1)} collective-permute-done((bf16[64,768]{1,0:T(8,128)(2,1)S(1)}, bf16[64,768]{1,0:T(8,128)(2,1)S(1)}, u32[]{:S(2)}, u32[]{:S(2)}) %collective-permute-start.1) | collective-permute-done | bytes 98336 | tf_op jit(solution)/shard_map/ppermute | solution.py:20
  13.3 0.2 collective-permute-done.refs_1_
  13.6 0.0 collective-permute-done.4.refs_7_
  13.6 0.0 collective-permute-done.3.refs_5_
  13.6 1.3 %score.1 = (f32[64,768]{1,0:T(8,128)S(1)}, bf16[64,768]{1,0:T(8,128)(2,1)S(1)}, bf16[64,768]{1,0:T(8,128)(2,1)S(1)}, bf16[64,768]{1,0:T(8,128)(2,1)S(1)}, bf16[2...) custom-call(bf16[64,768]{1,0:T(8,128)(2,1)S(1)} %pack.1.after_ref.refs_0_, ...), custom_call_target="tpu_custom_call" | custom-call | flops 805306368 | bytes 4194304 | tf_op jit(solution)/shard_map/score/pallas_call | solution.py:210
  14.9 1.6 %collective-permute-start.5 = (bf16[64,768]{1,0:T(8,128)(2,1)S(1)}, bf16[64,768]{1,0:T(8,128)(2,1)S(1)}, u32[]{:S(2)}, u32[]{:S(2)}) collective-permute-start(bf16[64,768]{1,0:T(8,128)(2,1)S(1)} %get-tuple-element.16), channel_id=1, source_target_pairs={{0,2},{1,3},{2,0},{3,1},{4,6},{5,7},{6,4},{7,5},{8,10},{9,11},{10,... | collective-permute-start | bytes 294920 | tf_op jit(solution)/shard_map/ppermute | solution.py:20
  16.5 0.6 %collective-permute-start.6 = (bf16[64,768]{1,0:T(8,128)(2,1)S(1)}, bf16[64,768]{1,0:T(8,128)(2,1)S(1)}, u32[]{:S(2)}, u32[]{:S(2)}) collective-permute-start(bf16[64,768]{1,0:T(8,128)(2,1)S(1)} %get-tuple-element.17), channel_id=1, source_target_pairs={{0,4},{1,5},{2,6},{3,7},{4,0},{5,1},{6,2},{7,3},{8,12},{9,13},{10,... | collective-permute-start | bytes 294920 | tf_op jit(solution)/shard_map/ppermute | solution.py:20
  17.1 1.3 %collective-permute-start.7 = (bf16[64,768]{1,0:T(8,128)(2,1)S(1)}, bf16[64,768]{1,0:T(8,128)(2,1)S(1)}, u32[]{:S(2)}, u32[]{:S(2)}) collective-permute-start(bf16[64,768]{1,0:T(8,128)(2,1)S(1)} %get-tuple-element.18), channel_id=1, source_target_pairs={{0,6},{1,7},{2,4},{3,5},{4,2},{5,3},{6,0},{7,1},{8,14},{9,15},{10,... | collective-permute-start | bytes 294920 | tf_op jit(solution)/shard_map/ppermute | solution.py:20
  18.5 1.1 %collective-permute-done.5 = bf16[64,768]{1,0:T(8,128)(2,1)S(1)} collective-permute-done((bf16[64,768]{1,0:T(8,128)(2,1)S(1)}, bf16[64,768]{1,0:T(8,128)(2,1)S(1)}, u32[]{:S(2)}, u32[]{:S(2)}) %collective-permute-start.5) | collective-permute-done | bytes 98336 | tf_op jit(solution)/shard_map/ppermute | solution.py:20
  19.6 3.5 %collective-permute-done.6 = bf16[64,768]{1,0:T(8,128)(2,1)S(1)} collective-permute-done((bf16[64,768]{1,0:T(8,128)(2,1)S(1)}, bf16[64,768]{1,0:T(8,128)(2,1)S(1)}, u32[]{:S(2)}, u32[]{:S(2)}) %collective-permute-start.6) | collective-permute-done | bytes 98336 | tf_op jit(solution)/shard_map/ppermute | solution.py:20
  23.1 0.0 collective-permute-done.7
  23.1 0.1 fusion
  23.1 1.6 %collective-permute-start.8 = (bf16[64,768]{1,0:T(8,128)(2,1)S(1)}, bf16[64,768]{1,0:T(8,128)(2,1)S(1)}, u32[]{:S(2)}, u32[]{:S(2)}) collective-permute-start(bf16[64,768]{1,0:T(8,128)(2,1)S(1)} %fusion), channel_id=1, source_target_pairs={{0,8},{8,0},{16,24},{24,16},{1,9},{9,1},{17,25},{25,17},{2,10},{10... | collective-permute-start | bytes 294920 | tf_op jit(solution)/shard_map/ppermute | solution.py:20
  24.8 0.0 collective-permute-start.11
  24.8 0.5 %collective-permute-start.10 = (bf16[256,512]{1,0:T(8,128)(2,1)S(1)}, bf16[256,512]{1,0:T(8,128)(2,1)S(1)}, u32[]{:S(2)}, u32[]{:S(2)}) collective-permute-start(bf16[256,512]{1,0:T(8,128)(2,1)S(1)} %get-tuple-element.20), channel_id=1, source_target_pairs={{0,1},{1,0},{2,3},{3,2},{4,5},{5,4},{6,7},{7,6},{8,9},{9,8},{10,11... | collective-permute-start | bytes 786440 | tf_op jit(solution)/shard_map/ppermute | solution.py:20
  25.3 2.5 %collective-permute-done.8 = bf16[64,768]{1,0:T(8,128)(2,1)S(1)} collective-permute-done((bf16[64,768]{1,0:T(8,128)(2,1)S(1)}, bf16[64,768]{1,0:T(8,128)(2,1)S(1)}, u32[]{:S(2)}, u32[]{:S(2)}) %collective-permute-start.8) | collective-permute-done | bytes 98336 | tf_op jit(solution)/shard_map/ppermute | solution.py:20
  27.8 0.1 fusion.1
  27.9 2.7 %collective-permute-start.9 = (bf16[64,768]{1,0:T(8,128)(2,1)S(1)}, bf16[64,768]{1,0:T(8,128)(2,1)S(1)}, u32[]{:S(2)}, u32[]{:S(2)}) collective-permute-start(bf16[64,768]{1,0:T(8,128)(2,1)S(1)} %get-tuple-element.22), channel_id=1, source_target_pairs={{0,16},{8,24},{16,0},{24,8},{1,17},{9,25},{17,1},{25,9},{2,18},{10... | collective-permute-start | bytes 294920 | tf_op jit(solution)/shard_map/ppermute | solution.py:20
  30.6 0.0 collective-permute-done.10.d_other_ref
  30.6 0.0 collective-permute-done.11.c_other_ref
  30.6 1.7 %emb_grad.1.after_hbm = f32[512,768]{1,0:T(8,128)} custom-call(bf16[256,512]{1,0:T(8,128)(2,1)S(1)} %get-tuple-element.19.d_own_ref, bf16[256,512]{1,0:T(8,128)(2,1)S(1)} %collective-permute-done.10.d_other_ref, bf16[256,768]{1,0:T(8,128)(2,1)S(1)} %get-tuple-element.21.c_own_ref, bf16[256,768]{1,0:T(8,128)(2,1)S(1)} %collective-permute-done.11.c_other_ref, ...), custom_call_target="tpu_custom_call" | custom-call | flops 402653184 | bytes 2883584 | tf_op jit(solution)/shard_map/emb_grad/pallas_call | solution.py:243
  32.3 1.1 %collective-permute-done.9.received_ref = bf16[64,768]{1,0:T(8,128)(2,1)S(1)} collective-permute-done((bf16[64,768]{1,0:T(8,128)(2,1)S(1)}, bf16[64,768]{1,0:T(8,128)(2,1)S(1)}, u32[]{:S(2)}, u32[]{:S(2)}) %collective-permute-start.9) | collective-permute-done | bytes 98336 | tf_op jit(solution)/shard_map/ppermute | solution.py:20
  33.5 1.4 %finish.1 = f32[64,768]{1,0:T(8,128)} custom-call(f32[64,768]{1,0:T(8,128)S(1)} %get-tuple-element.23.after_ref.grad_ref, bf16[64,768]{1,0:T(8,128)(2,1)S(1)} %collective-permute-done.9.received_ref, s32[1,64]{1,0:T(1,128)} %bitcast.10, f32[512,768]{1,0:T(8,128)} %emb_grad.1.after_hbm), custom_call_target="tpu_custom_call" | custom-call | flops 49152 | bytes 491520 | tf_op jit(solution)/shard_map/finish/pallas_call | solution.py:253
Async XLA Ops:
  0.6 13.0 %collective-permute-start.3 = (bf16[512,768]{1,0:T(8,128)(2,1)}, bf16[512,768]{1,0:T(8,128)(2,1)S(1)}, u32[]{:S(2)}, u32[]{:S(2)}) collective-permute-start(bf16[512,768]{1,0:T(8,128)(2,1)} %emb_hbm.1), channel_id=1, source_target_pairs={{0,1},{1,0},{2,3},{3,2},{4,5},{5,4},{6,7},{7,6},{8,9},{9,8},{10,11... | collective-permute-start | bytes 2359304 | tf_op jit(solution)/shard_map/ppermute | solution.py:20
  4.2 9.4 %collective-permute-start.4 = (bf16[256,512]{1,0:T(8,128)(2,1)S(1)}, bf16[256,512]{1,0:T(8,128)(2,1)S(1)}, u32[]{:S(2)}, u32[]{:S(2)}) collective-permute-start(bf16[256,512]{1,0:T(8,128)(2,1)S(1)} %get-tuple-element.14), channel_id=1, source_target_pairs={{0,1},{1,0},{2,3},{3,2},{4,5},{5,4},{6,7},{7,6},{8,9},{9,8},{10,11... | collective-permute-start | bytes 786440 | tf_op jit(solution)/shard_map/ppermute | solution.py:20
  4.3 7.1 %collective-permute-start.2 = (bf16[64,768]{1,0:T(8,128)(2,1)S(1)}, bf16[64,768]{1,0:T(8,128)(2,1)S(1)}, u32[]{:S(2)}, u32[]{:S(2)}) collective-permute-start(bf16[64,768]{1,0:T(8,128)(2,1)S(1)} %pack.1.after_ref.refs_0_), channel_id=1, source_target_pairs={{0,6},{1,7},{2,4},{3,5},{4,2},{5,3},{6,0},{7,1},{8,14},{9,15},{10,... | collective-permute-start | bytes 294920 | tf_op jit(solution)/shard_map/ppermute | solution.py:20
  8.2 5.1 %collective-permute-start.1 = (bf16[64,768]{1,0:T(8,128)(2,1)S(1)}, bf16[64,768]{1,0:T(8,128)(2,1)S(1)}, u32[]{:S(2)}, u32[]{:S(2)}) collective-permute-start(bf16[64,768]{1,0:T(8,128)(2,1)S(1)} %pack.1.after_ref.refs_0_), channel_id=1, source_target_pairs={{0,4},{1,5},{2,6},{3,7},{4,0},{5,1},{6,2},{7,3},{8,12},{9,13},{10,... | collective-permute-start | bytes 294920 | tf_op jit(solution)/shard_map/ppermute | solution.py:20
  8.7 4.9 %collective-permute-start = (bf16[64,768]{1,0:T(8,128)(2,1)S(1)}, bf16[64,768]{1,0:T(8,128)(2,1)S(1)}, u32[]{:S(2)}, u32[]{:S(2)}) collective-permute-start(bf16[64,768]{1,0:T(8,128)(2,1)S(1)} %pack.1.after_ref.refs_0_), channel_id=1, source_target_pairs={{0,2},{1,3},{2,0},{3,1},{4,6},{5,7},{6,4},{7,5},{8,10},{9,11},{10,... | collective-permute-start | bytes 294920 | tf_op jit(solution)/shard_map/ppermute | solution.py:20
  14.9 4.7 %collective-permute-start.5 = (bf16[64,768]{1,0:T(8,128)(2,1)S(1)}, bf16[64,768]{1,0:T(8,128)(2,1)S(1)}, u32[]{:S(2)}, u32[]{:S(2)}) collective-permute-start(bf16[64,768]{1,0:T(8,128)(2,1)S(1)} %get-tuple-element.16), channel_id=1, source_target_pairs={{0,2},{1,3},{2,0},{3,1},{4,6},{5,7},{6,4},{7,5},{8,10},{9,11},{10,... | collective-permute-start | bytes 294920 | tf_op jit(solution)/shard_map/ppermute | solution.py:20
  16.5 6.6 %collective-permute-start.6 = (bf16[64,768]{1,0:T(8,128)(2,1)S(1)}, bf16[64,768]{1,0:T(8,128)(2,1)S(1)}, u32[]{:S(2)}, u32[]{:S(2)}) collective-permute-start(bf16[64,768]{1,0:T(8,128)(2,1)S(1)} %get-tuple-element.17), channel_id=1, source_target_pairs={{0,4},{1,5},{2,6},{3,7},{4,0},{5,1},{6,2},{7,3},{8,12},{9,13},{10,... | collective-permute-start | bytes 294920 | tf_op jit(solution)/shard_map/ppermute | solution.py:20
  17.1 6.0 %collective-permute-start.7 = (bf16[64,768]{1,0:T(8,128)(2,1)S(1)}, bf16[64,768]{1,0:T(8,128)(2,1)S(1)}, u32[]{:S(2)}, u32[]{:S(2)}) collective-permute-start(bf16[64,768]{1,0:T(8,128)(2,1)S(1)} %get-tuple-element.18), channel_id=1, source_target_pairs={{0,6},{1,7},{2,4},{3,5},{4,2},{5,3},{6,0},{7,1},{8,14},{9,15},{10,... | collective-permute-start | bytes 294920 | tf_op jit(solution)/shard_map/ppermute | solution.py:20
  23.1 4.7 %collective-permute-start.8 = (bf16[64,768]{1,0:T(8,128)(2,1)S(1)}, bf16[64,768]{1,0:T(8,128)(2,1)S(1)}, u32[]{:S(2)}, u32[]{:S(2)}) collective-permute-start(bf16[64,768]{1,0:T(8,128)(2,1)S(1)} %fusion), channel_id=1, source_target_pairs={{0,8},{8,0},{16,24},{24,16},{1,9},{9,1},{17,25},{25,17},{2,10},{10... | collective-permute-start | bytes 294920 | tf_op jit(solution)/shard_map/ppermute | solution.py:20
  24.8 5.8 %collective-permute-start.11 = (bf16[256,768]{1,0:T(8,128)(2,1)S(1)}, bf16[256,768]{1,0:T(8,128)(2,1)S(1)}, u32[]{:S(2)}, u32[]{:S(2)}) collective-permute-start(bf16[256,768]{1,0:T(8,128)(2,1)S(1)} %get-tuple-element.21.c_own_ref), channel_id=1, source_target_pairs={{0,1},{1,0},{2,3},{3,2},{4,5},{5,4},{6,7},{7,6},{8,9},{9,8},{10,11... | collective-permute-start | bytes 1179656 | tf_op jit(solution)/shard_map/ppermute | solution.py:20
  24.8 5.8 %collective-permute-start.10 = (bf16[256,512]{1,0:T(8,128)(2,1)S(1)}, bf16[256,512]{1,0:T(8,128)(2,1)S(1)}, u32[]{:S(2)}, u32[]{:S(2)}) collective-permute-start(bf16[256,512]{1,0:T(8,128)(2,1)S(1)} %get-tuple-element.20), channel_id=1, source_target_pairs={{0,1},{1,0},{2,3},{3,2},{4,5},{5,4},{6,7},{7,6},{8,9},{9,8},{10,11... | collective-permute-start | bytes 786440 | tf_op jit(solution)/shard_map/ppermute | solution.py:20
  27.9 5.6 %collective-permute-start.9 = (bf16[64,768]{1,0:T(8,128)(2,1)S(1)}, bf16[64,768]{1,0:T(8,128)(2,1)S(1)}, u32[]{:S(2)}, u32[]{:S(2)}) collective-permute-start(bf16[64,768]{1,0:T(8,128)(2,1)S(1)} %get-tuple-element.22), channel_id=1, source_target_pairs={{0,16},{8,24},{16,0},{24,8},{1,17},{9,25},{17,1},{25,9},{2,18},{10... | collective-permute-start | bytes 294920 | tf_op jit(solution)/shard_map/ppermute | solution.py:20

commit v4 on v3

--- a/solution.py
+++ b/solution.py
@@ -46,47 +46,60 @@
     return jnp.sum(jnp.where(diagonal, spread, 0.0), axis=1, keepdims=True)
 
 
-def pack_kernel(classifier_hbm, valid_hbm, out_ref, classifier_ref, valid_ref, sem):
-    fetch((classifier_hbm, valid_hbm), (classifier_ref, valid_ref), sem)
-    out_ref[...] = (classifier_ref[...] * flag_column(valid_ref[...])).astype(BF16)
+def pack_kernel(
+    classifier_hbm, valid_hbm, short_hbm, live_hbm, pos_hbm, neg_hbm, rows_ref, column_ref, index_ref,
+    classifier_ref, valid_ref, short_ref, live_ref, pos_ref, sem, *, scale
+):
+    slots, negatives, docs = neg_hbm.shape
+    fetch(
+        (classifier_hbm, valid_hbm, short_hbm, live_hbm, pos_hbm)
+        + tuple(neg_hbm.at[s] for s in range(slots)),
+        (classifier_ref, valid_ref, short_ref, live_ref, pos_ref)
+        + tuple(index_ref.at[pl.ds(s * negatives, negatives)] for s in range(slots)),
+        sem,
+    )
+    column = flag_column(valid_ref[...])
+    rows_ref[...] = (classifier_ref[...] * column).astype(BF16)
+    column_ref[...] = jnp.broadcast_to(column * scale, column_ref.shape)
+    index_ref[slots * negatives : slots * (negatives + 2)] = jnp.concatenate(
+        [pos_ref[...], jnp.where(live_ref[...] > 0, short_ref[...], -1)], 0
+    )
 
 
 def targets_kernel(
-    short_hbm, live_hbm, pos_hbm, neg_hbm, emb_hbm, after_ref, mine_ref, theirs_ref, emb_ref,
-    short_ref, live_ref, pos_ref, neg_ref, sem, emb_sem, *, panel
+    index_own_ref, index_other_ref, emb_hbm, target_own_ref, target_other_ref, emb_ref, emb_sem, *, panel, slots
 ):
     emb_copy = pltpu.make_async_copy(emb_hbm, emb_ref, emb_sem)
     emb_copy.start()
-    fetch((short_hbm, live_hbm, pos_hbm, neg_hbm), (short_ref, live_ref, pos_ref, neg_ref), sem)
     me = lax.axis_index("lab")
-    slots, docs = short_ref.shape
-    negatives = neg_ref.shape[1]
+    docs = index_own_ref.shape[1]
+    negatives = index_own_ref.shape[0] // slots - 2
     groups = panel // SUBLANES
-    clusters = (mine_ref.shape[0] + theirs_ref.shape[0]) // panel
     shape = (groups, SUBLANES, LANES)
     label = SUBLANES * lax.broadcasted_iota(jnp.int32, shape, 0) + lax.broadcasted_iota(jnp.int32, shape, 1)
 
-    def chunk(i, carry):
-        lanes = pl.ds(pl.multiple_of(i * LANES, LANES), LANES)
-
-        def row(value):
-            return jnp.broadcast_to(value, (SUBLANES, LANES))
+    def fill(index_ref, out_ref, lanes):
+        def row(at):
+            return jnp.broadcast_to(index_ref[at : at + 1, lanes], (SUBLANES, LANES))
 
         values, relative = [], []
         for s in range(slots):
             count = jnp.zeros(shape, F32)
             for k in range(negatives):
-                count = count + jnp.where(row(neg_ref[s, k : k + 1, lanes])[None] == label, 1.0, 0.0)
-            hot = row(pos_ref[s : s + 1, lanes])[None] == label
-            live = row(live_ref[s : s + 1, lanes]).astype(F32)[None]
-            values.append(jnp.where(hot, -1.0 - count, count) * live)
-            relative.append(row(short_ref[s : s + 1, lanes]) ^ me)
-        for r in range(clusters):
+                count = count + jnp.where(row(s * negatives + k)[None] == label, 1.0, 0.0)
+            hot = row(slots * negatives + s)[None] == label
+            values.append(jnp.where(hot, -1.0 - count, count))
+            relative.append(row(slots * (negatives + 1) + s) ^ me)
+        for j in range(out_ref.shape[0] // panel):
             block = jnp.zeros(shape, F32)
             for s in range(slots):
-                block = jnp.where((relative[s] == r)[None], values[s], block)
-            out = theirs_ref if r % 2 else mine_ref
-            out[pl.ds((r // 2) * panel, panel), lanes] = block.reshape(panel, LANES).astype(BF16)
+                block = jnp.where((relative[s] == 2 * j)[None], values[s], block)
+            out_ref[pl.ds(j * panel, panel), lanes] = block.reshape(panel, LANES).astype(BF16)
+
+    def chunk(i, carry):
+        lanes = pl.ds(pl.multiple_of(i * LANES, LANES), LANES)
+        fill(index_own_ref, target_own_ref, lanes)
+        fill(index_other_ref, target_other_ref, lanes)
         return carry
 
     lax.fori_loop(0, docs // LANES, chunk, 0)
@@ -132,10 +145,8 @@
     ) + lax.dot_general(d_other_ref[...], c_other_ref[...], dims, preferred_element_type=F32)
 
 
-def finish_kernel(grad_ref, received_ref, valid_hbm, after_hbm, out_ref, valid_ref, sem, *, scale):
-    fetch((valid_hbm,), (valid_ref,), sem)
-    column = flag_column(valid_ref[...]) * scale
-    out_ref[...] = (grad_ref[...] + received_ref[...].astype(F32)) * column
+def finish_kernel(grad_ref, received_ref, column_ref, after_hbm, out_ref):
+    out_ref[...] = (grad_ref[...] + received_ref[...].astype(F32)) * column_ref[:, :1]
 
 
 def hbm(count):
@@ -167,45 +178,47 @@
     half = lab // 2 * panel
     groups = bit_groups(lab)
 
-    valid = label_valid.reshape(1, panel)
-    packed = pl.pallas_call(
-        pack_kernel,
-        out_shape=jax.ShapeDtypeStruct((panel, width), BF16),
-        in_specs=hbm(2),
-        out_specs=pl.BlockSpec(memory_space=pltpu.VMEM),
-        scratch_shapes=[
-            pltpu.VMEM((panel, width), F32),
-            pltpu.VMEM((1, panel), jnp.int32),
-            pltpu.SemaphoreType.DMA((2,)),
+    negatives = negative.shape[2]
+    height = slots * (negatives + 2)
+    packed, column, index_own = pl.pallas_call(
+        functools.partial(pack_kernel, scale=1.0 / math.sqrt(docs * enc * slots)),
+        out_shape=[
+            jax.ShapeDtypeStruct((panel, width), BF16),
+            jax.ShapeDtypeStruct((panel, LANES), F32),
+            jax.ShapeDtypeStruct((height, docs), jnp.int32),
         ],
-        compiler_params=params(panel * width * 6),
-        cost_estimate=cost(panel * width, panel * width * 6),
+        in_specs=hbm(6),
+        out_specs=vmem(3),
+        scratch_shapes=[pltpu.VMEM((panel, width), F32), pltpu.VMEM((1, panel), jnp.int32)]
+        + [pltpu.VMEM((slots, docs), jnp.int32)] * 3
+        + [pltpu.SemaphoreType.DMA((5 + slots,))],
+        compiler_params=params(panel * width * 6, height * docs * 4),
+        cost_estimate=cost(panel * width, panel * width * 6 + height * docs * 4),
         name="pack",
-    )(*keep(classifier, valid))
+    )(
+        *keep(
+            classifier, label_valid.reshape(1, panel), shortlist.T, slot_live.T, positive.T,
+            negative.transpose(1, 2, 0),
+        )
+    )
     pieces = [packed]
     for group in groups:
         own = pieces[0] if len(pieces) == 1 else jnp.concatenate(pieces, 0)
         pieces = [own] + [flip(own, "lab", mask) for mask in group_masks(group)]
 
     emb_other = flip(embeddings, "lab", 1)
-    target_mine, target_theirs, emb_own = pl.pallas_call(
-        functools.partial(targets_kernel, panel=panel),
+    index_other = flip(index_own, "lab", 1)
+    target_own, target_other, emb_own = pl.pallas_call(
+        functools.partial(targets_kernel, panel=panel, slots=slots),
         out_shape=[jax.ShapeDtypeStruct((half, docs), BF16)] * 2
         + [jax.ShapeDtypeStruct((docs, width), BF16)],
-        in_specs=hbm(5) + vmem(1),
+        in_specs=vmem(2) + hbm(1),
         out_specs=vmem(3),
-        scratch_shapes=[pltpu.VMEM((slots, docs), jnp.int32)] * 3
-        + [
-            pltpu.VMEM((slots, negative.shape[2], docs), jnp.int32),
-            pltpu.SemaphoreType.DMA((4,)),
-            pltpu.SemaphoreType.DMA,
-        ],
-        compiler_params=params(docs * slots * 44, docs * half * 4, docs * width * 2),
-        cost_estimate=cost(docs * panel * slots * 40, docs * slots * 44 + docs * half * 4),
+        scratch_shapes=[pltpu.SemaphoreType.DMA],
+        compiler_params=params(height * docs * 8, docs * half * 4, docs * width * 2),
+        cost_estimate=cost(docs * panel * slots * 80, height * docs * 8 + docs * half * 4),
         name="targets",
-    )(*keep(shortlist.T, slot_live.T, positive.T, negative.transpose(1, 2, 0), embeddings), packed)
-    target_other = flip(target_theirs, "lab", 1)
-
+    )(index_own, index_other, *keep(embeddings))
     parts = len(group_masks(groups[-1])) + 1 if groups else 1
     outs = pl.pallas_call(
         functools.partial(score_kernel, pieces=len(pieces), parts=parts),
@@ -219,7 +232,7 @@
         compiler_params=params(4 * docs * width, 16 * half * docs, 12 * half * width),
         cost_estimate=cost(8 * docs * half * width, 4 * docs * width + 8 * half * docs + 8 * half * width),
         name="score",
-    )(*pieces, emb_own, emb_other, target_mine, target_other)
+    )(*pieces, emb_own, emb_other, target_own, target_other)
     grads, (d_own, d_theirs, classifier_own) = outs[:parts], outs[parts:]
 
     grad = None
@@ -251,15 +264,14 @@
     )(d_own, d_other, classifier_own, classifier_other, grad)
 
     w_grad = pl.pallas_call(
-        functools.partial(finish_kernel, scale=1.0 / math.sqrt(docs * enc * slots)),
+        finish_kernel,
         out_shape=jax.ShapeDtypeStruct((panel, width), F32),
-        in_specs=vmem(2) + hbm(2),
+        in_specs=vmem(3) + hbm(1),
         out_specs=pl.BlockSpec(memory_space=pltpu.VMEM),
-        scratch_shapes=[pltpu.VMEM((1, panel), jnp.int32), pltpu.SemaphoreType.DMA((1,))],
         compiler_params=params(panel * width * 10),
         cost_estimate=cost(panel * width, panel * width * 10),
         name="finish",
-    )(grad, received, *keep(valid, emb_grad))
+    )(grad, received, column, *keep(emb_grad))
     return (w_grad, emb_grad)
 
 

time: 35.1 us -> 32.5 us (0.926)
  Pallas kernels: 7.51 us -> 6.28 us
  waiting for transfers between devices: 13.1 us -> 12.1 us
  starting transfers between devices: 13.5 us -> 13.1 us
    pallas_call x3, Pallas kernels: 4.44 us -> 3.22 us  [the longest x1 1.35 us: shards(): pl.pallas_call(functools.partial(targets_kernel, panel=panel, slots=slots...]
    ppermute x12, waiting for transfers between devices: 13.1 us -> 12.1 us  [flip(): lax.ppermute(value, axis, [(i, i ^ mask) for i in range(lax.axis_size(axi...]
    ppermute x12, starting transfers between devices: 13.5 us -> 13.1 us  [flip(): lax.ppermute(value, axis, [(i, i ^ mask) for i in range(lax.axis_size(axi...]
  transfers between devices with their start and end apart: 12 -> 12, of which waited for: 7 -> 8; matrix products, arithmetic and copies ran while one was open for 0% -> 0% of each run, Pallas kernels for 14% -> 13%
where the time goes in v4:
time: 32.5 us; the launch traced here: 32.3 us
  starting transfers between devices  13.1 us (40%)
  waiting for transfers between devices  12.1 us (37%)
  Pallas kernels  6.28 us (19%)
  between operations  0.68 us (2%)
    ppermute x12, starting transfers between devices, flip(): lax.ppermute(value, axis, [(i, i ^ mask) for i in range(lax.axis_size(axi...  13.1 us
    ppermute x12, waiting for transfers between devices, flip(): lax.ppermute(value, axis, [(i, i ^ mask) for i in range(lax.axis_size(axi...  12.1 us
    pallas_call x1, Pallas kernels, shards(): pl.pallas_call(emb_kernel, out_shape=jax.ShapeDtypeStruct((docs, width),...  1.74 us
    pallas_call x1, Pallas kernels, shards(): pl.pallas_call(functools.partial(targets_kernel, panel=panel, slots=slots...  1.35 us
    pallas_call x1, Pallas kernels, shards(): pl.pallas_call(functools.partial(score_kernel, pieces=len(pieces), parts=...  1.32 us
    pallas_call x1, Pallas kernels, shards(): pl.pallas_call(functools.partial(pack_kernel, scale=1.0 / math.sqrt(docs...  1.11 us
    pallas_call x1, Pallas kernels, shards(): pl.pallas_call(finish_kernel, out_shape=jax.ShapeDtypeStruct((panel, widt...  0.76 us
  transfers between devices with their start and end apart: 12, of which 8 were waited for; matrix products, arithmetic and copies ran while one was open for 0% of the time, Pallas kernels for 13%

profile of v4, /device:TPU:0, one launch (start us, length us, event | category | flops | bytes accessed | tf_op | source)
XLA Modules:
  0.0 32.3 jit_solution(9188713494103192542)
XLA Ops:
  0.6 0.5 %collective-permute-start.4 = (bf16[512,768]{1,0:T(8,128)(2,1)}, bf16[512,768]{1,0:T(8,128)(2,1)S(1)}, u32[]{:S(2)}, u32[]{:S(2)}) collective-permute-start(bf16[512,768]{1,0:T(8,128)(2,1)} %emb_hbm.1), channel_id=1, source_target_pairs={{0,1},{1,0},{2,3},{3,2},{4,5},{5,4},{6,7},{7,6},{8,9},{9,8},{10,11... | collective-permute-start | bytes 2359304 | tf_op jit(solution)/shard_map/ppermute | solution.py:20
  1.1 1.1 %pack.1 = (bf16[64,768]{1,0:T(8,128)(2,1)S(1)}, f32[64,128]{1,0:T(8,128)S(1)}, s32[40,512]{1,0:T(8,128)S(1)}) custom-call(f32[64,768]{1,0:T(8,128)} %classifier_hbm.1, s32[1,64]{1,0:T(1,128)} %bitcast.9, s32[4,512]{1,0:T(4,128)} %bitcast.6, s32[4,512]{1,0:T(4,128)} %bitcast.7, s32[4,512]{1,0:T(4,128)} %bitcast.8, s32[4,8,512]{2,1,0:T(8,128)} %bitcast.5), custom_call_target="tpu_custom_call" | custom-call | flops 49152 | bytes 376832 | tf_op jit(solution)/shard_map/pack/pallas_call | solution.py:183
  2.3 3.5 %collective-permute-start.2 = (bf16[64,768]{1,0:T(8,128)(2,1)S(1)}, bf16[64,768]{1,0:T(8,128)(2,1)S(1)}, u32[]{:S(2)}, u32[]{:S(2)}) collective-permute-start(bf16[64,768]{1,0:T(8,128)(2,1)S(1)} %get-tuple-element.15.refs_0_), channel_id=1, source_target_pairs={{0,6},{1,7},{2,4},{3,5},{4,2},{5,3},{6,0},{7,1},{8,14},{9,15},{10,... | collective-permute-start | bytes 294920 | tf_op jit(solution)/shard_map/ppermute | solution.py:20
  5.8 0.5 %collective-permute-start.1 = (bf16[64,768]{1,0:T(8,128)(2,1)S(1)}, bf16[64,768]{1,0:T(8,128)(2,1)S(1)}, u32[]{:S(2)}, u32[]{:S(2)}) collective-permute-start(bf16[64,768]{1,0:T(8,128)(2,1)S(1)} %get-tuple-element.15.refs_0_), channel_id=1, source_target_pairs={{0,4},{1,5},{2,6},{3,7},{4,0},{5,1},{6,2},{7,3},{8,12},{9,13},{10,... | collective-permute-start | bytes 294920 | tf_op jit(solution)/shard_map/ppermute | solution.py:20
  6.3 0.1 collective-permute-start
  6.4 0.0 collective-permute-start.3
  6.4 1.3 %collective-permute-done.3.index_other_ref = s32[40,512]{1,0:T(8,128)S(1)} collective-permute-done((s32[40,512]{1,0:T(8,128)S(1)}, s32[40,512]{1,0:T(8,128)S(1)}, u32[]{:S(2)}, u32[]{:S(2)}) %collective-permute-start.3) | collective-permute-done | bytes 81952 | tf_op jit(solution)/shard_map/ppermute | solution.py:20
  7.7 1.3 %targets.1 = (bf16[256,512]{1,0:T(8,128)(2,1)S(1)}, bf16[256,512]{1,0:T(8,128)(2,1)S(1)}, bf16[512,768]{1,0:T(8,128)(2,1)S(1)}) custom-call(s32[40,512]{1,0:T(8,128)S(1)} %get-tuple-element.16.index_own_ref, s32[40,512]{1,0:T(8,128)S(1)} %collective-permute-done.3.index_other_ref, bf16[512,768]{1,0:T(8,128)(2,1)} %emb_hbm.1), custom_call_target="tpu_custom_call" | custom-call | flops 10485760 | bytes 688128 | tf_op jit(solution)/shard_map/targets/pallas_call | solution.py:211
  9.1 0.2 collective-permute-done.2.refs_3_
  9.3 2.0 %collective-permute-done.1.refs_2_ = bf16[64,768]{1,0:T(8,128)(2,1)S(1)} collective-permute-done((bf16[64,768]{1,0:T(8,128)(2,1)S(1)}, bf16[64,768]{1,0:T(8,128)(2,1)S(1)}, u32[]{:S(2)}, u32[]{:S(2)}) %collective-permute-start.1) | collective-permute-done | bytes 98336 | tf_op jit(solution)/shard_map/ppermute | solution.py:20
  11.4 0.2 collective-permute-done.refs_1_
  11.6 0.0 collective-permute-done.4.refs_5_
  11.6 1.3 %score.1 = (f32[64,768]{1,0:T(8,128)S(1)}, bf16[64,768]{1,0:T(8,128)(2,1)S(1)}, bf16[64,768]{1,0:T(8,128)(2,1)S(1)}, bf16[64,768]{1,0:T(8,128)(2,1)S(1)}, bf16[2...) custom-call(bf16[64,768]{1,0:T(8,128)(2,1)S(1)} %get-tuple-element.15.refs_0_, ...), custom_call_target="tpu_custom_call" | custom-call | flops 805306368 | bytes 4194304 | tf_op jit(solution)/shard_map/score/pallas_call | solution.py:223
  12.9 1.6 %collective-permute-start.5 = (bf16[64,768]{1,0:T(8,128)(2,1)S(1)}, bf16[64,768]{1,0:T(8,128)(2,1)S(1)}, u32[]{:S(2)}, u32[]{:S(2)}) collective-permute-start(bf16[64,768]{1,0:T(8,128)(2,1)S(1)} %get-tuple-element.21), channel_id=1, source_target_pairs={{0,2},{1,3},{2,0},{3,1},{4,6},{5,7},{6,4},{7,5},{8,10},{9,11},{10,... | collective-permute-start | bytes 294920 | tf_op jit(solution)/shard_map/ppermute | solution.py:20
  14.5 0.6 %collective-permute-start.6 = (bf16[64,768]{1,0:T(8,128)(2,1)S(1)}, bf16[64,768]{1,0:T(8,128)(2,1)S(1)}, u32[]{:S(2)}, u32[]{:S(2)}) collective-permute-start(bf16[64,768]{1,0:T(8,128)(2,1)S(1)} %get-tuple-element.22), channel_id=1, source_target_pairs={{0,4},{1,5},{2,6},{3,7},{4,0},{5,1},{6,2},{7,3},{8,12},{9,13},{10,... | collective-permute-start | bytes 294920 | tf_op jit(solution)/shard_map/ppermute | solution.py:20
  15.1 1.4 %collective-permute-start.7 = (bf16[64,768]{1,0:T(8,128)(2,1)S(1)}, bf16[64,768]{1,0:T(8,128)(2,1)S(1)}, u32[]{:S(2)}, u32[]{:S(2)}) collective-permute-start(bf16[64,768]{1,0:T(8,128)(2,1)S(1)} %get-tuple-element.23), channel_id=1, source_target_pairs={{0,6},{1,7},{2,4},{3,5},{4,2},{5,3},{6,0},{7,1},{8,14},{9,15},{10,... | collective-permute-start | bytes 294920 | tf_op jit(solution)/shard_map/ppermute | solution.py:20
  16.5 1.1 %collective-permute-done.5 = bf16[64,768]{1,0:T(8,128)(2,1)S(1)} collective-permute-done((bf16[64,768]{1,0:T(8,128)(2,1)S(1)}, bf16[64,768]{1,0:T(8,128)(2,1)S(1)}, u32[]{:S(2)}, u32[]{:S(2)}) %collective-permute-start.5) | collective-permute-done | bytes 98336 | tf_op jit(solution)/shard_map/ppermute | solution.py:20
  17.6 3.5 %collective-permute-done.6 = bf16[64,768]{1,0:T(8,128)(2,1)S(1)} collective-permute-done((bf16[64,768]{1,0:T(8,128)(2,1)S(1)}, bf16[64,768]{1,0:T(8,128)(2,1)S(1)}, u32[]{:S(2)}, u32[]{:S(2)}) %collective-permute-start.6) | collective-permute-done | bytes 98336 | tf_op jit(solution)/shard_map/ppermute | solution.py:20
  21.1 0.0 collective-permute-done.7
  21.1 0.1 fusion
  21.2 1.6 %collective-permute-start.8 = (bf16[64,768]{1,0:T(8,128)(2,1)S(1)}, bf16[64,768]{1,0:T(8,128)(2,1)S(1)}, u32[]{:S(2)}, u32[]{:S(2)}) collective-permute-start(bf16[64,768]{1,0:T(8,128)(2,1)S(1)} %fusion), channel_id=1, source_target_pairs={{0,8},{8,0},{16,24},{24,16},{1,9},{9,1},{17,25},{25,17},{2,10},{10... | collective-permute-start | bytes 294920 | tf_op jit(solution)/shard_map/ppermute | solution.py:20
  22.8 0.0 collective-permute-start.11
  22.8 0.5 %collective-permute-start.10 = (bf16[256,512]{1,0:T(8,128)(2,1)S(1)}, bf16[256,512]{1,0:T(8,128)(2,1)S(1)}, u32[]{:S(2)}, u32[]{:S(2)}) collective-permute-start(bf16[256,512]{1,0:T(8,128)(2,1)S(1)} %get-tuple-element.26), channel_id=1, source_target_pairs={{0,1},{1,0},{2,3},{3,2},{4,5},{5,4},{6,7},{7,6},{8,9},{9,8},{10,11... | collective-permute-start | bytes 786440 | tf_op jit(solution)/shard_map/ppermute | solution.py:20
  23.3 2.5 %collective-permute-done.8 = bf16[64,768]{1,0:T(8,128)(2,1)S(1)} collective-permute-done((bf16[64,768]{1,0:T(8,128)(2,1)S(1)}, bf16[64,768]{1,0:T(8,128)(2,1)S(1)}, u32[]{:S(2)}, u32[]{:S(2)}) %collective-permute-start.8) | collective-permute-done | bytes 98336 | tf_op jit(solution)/shard_map/ppermute | solution.py:20
  25.9 0.1 fusion.1
  25.9 2.7 %collective-permute-start.9 = (bf16[64,768]{1,0:T(8,128)(2,1)S(1)}, bf16[64,768]{1,0:T(8,128)(2,1)S(1)}, u32[]{:S(2)}, u32[]{:S(2)}) collective-permute-start(bf16[64,768]{1,0:T(8,128)(2,1)S(1)} %get-tuple-element.28), channel_id=1, source_target_pairs={{0,16},{8,24},{16,0},{24,8},{1,17},{9,25},{17,1},{25,9},{2,18},{10... | collective-permute-start | bytes 294920 | tf_op jit(solution)/shard_map/ppermute | solution.py:20
  28.6 0.0 collective-permute-done.10.d_other_ref
  28.6 0.0 collective-permute-done.11.c_other_ref
  28.6 1.7 %emb_grad.1.after_hbm = f32[512,768]{1,0:T(8,128)} custom-call(bf16[256,512]{1,0:T(8,128)(2,1)S(1)} %get-tuple-element.25.d_own_ref, bf16[256,512]{1,0:T(8,128)(2,1)S(1)} %collective-permute-done.10.d_other_ref, bf16[256,768]{1,0:T(8,128)(2,1)S(1)} %get-tuple-element.27.c_own_ref, bf16[256,768]{1,0:T(8,128)(2,1)S(1)} %collective-permute-done.11.c_other_ref, ...), custom_call_target="tpu_custom_call" | custom-call | flops 402653184 | bytes 2883584 | tf_op jit(solution)/shard_map/emb_grad/pallas_call | solution.py:256
  30.4 1.2 %collective-permute-done.9.received_ref = bf16[64,768]{1,0:T(8,128)(2,1)S(1)} collective-permute-done((bf16[64,768]{1,0:T(8,128)(2,1)S(1)}, bf16[64,768]{1,0:T(8,128)(2,1)S(1)}, u32[]{:S(2)}, u32[]{:S(2)}) %collective-permute-start.9) | collective-permute-done | bytes 98336 | tf_op jit(solution)/shard_map/ppermute | solution.py:20
  31.5 0.8 %finish.1 = f32[64,768]{1,0:T(8,128)} custom-call(f32[64,768]{1,0:T(8,128)S(1)} %get-tuple-element.29.after_ref.grad_ref, bf16[64,768]{1,0:T(8,128)(2,1)S(1)} %collective-permute-done.9.received_ref, f32[64,128]{1,0:T(8,128)S(1)} %get-tuple-element.24.column_ref, f32[512,768]{1,0:T(8,128)} %emb_grad.1.after_hbm), custom_call_target="tpu_custom_call" | custom-call | flops 49152 | bytes 491520 | tf_op jit(solution)/shard_map/finish/pallas_call | solution.py:266
Async XLA Ops:
  0.6 11.0 %collective-permute-start.4 = (bf16[512,768]{1,0:T(8,128)(2,1)}, bf16[512,768]{1,0:T(8,128)(2,1)S(1)}, u32[]{:S(2)}, u32[]{:S(2)}) collective-permute-start(bf16[512,768]{1,0:T(8,128)(2,1)} %emb_hbm.1), channel_id=1, source_target_pairs={{0,1},{1,0},{2,3},{3,2},{4,5},{5,4},{6,7},{7,6},{8,9},{9,8},{10,11... | collective-permute-start | bytes 2359304 | tf_op jit(solution)/shard_map/ppermute | solution.py:20
  2.3 7.0 %collective-permute-start.2 = (bf16[64,768]{1,0:T(8,128)(2,1)S(1)}, bf16[64,768]{1,0:T(8,128)(2,1)S(1)}, u32[]{:S(2)}, u32[]{:S(2)}) collective-permute-start(bf16[64,768]{1,0:T(8,128)(2,1)S(1)} %get-tuple-element.15.refs_0_), channel_id=1, source_target_pairs={{0,6},{1,7},{2,4},{3,5},{4,2},{5,3},{6,0},{7,1},{8,14},{9,15},{10,... | collective-permute-start | bytes 294920 | tf_op jit(solution)/shard_map/ppermute | solution.py:20
  5.8 5.6 %collective-permute-start.1 = (bf16[64,768]{1,0:T(8,128)(2,1)S(1)}, bf16[64,768]{1,0:T(8,128)(2,1)S(1)}, u32[]{:S(2)}, u32[]{:S(2)}) collective-permute-start(bf16[64,768]{1,0:T(8,128)(2,1)S(1)} %get-tuple-element.15.refs_0_), channel_id=1, source_target_pairs={{0,4},{1,5},{2,6},{3,7},{4,0},{5,1},{6,2},{7,3},{8,12},{9,13},{10,... | collective-permute-start | bytes 294920 | tf_op jit(solution)/shard_map/ppermute | solution.py:20
  6.3 5.3 %collective-permute-start = (bf16[64,768]{1,0:T(8,128)(2,1)S(1)}, bf16[64,768]{1,0:T(8,128)(2,1)S(1)}, u32[]{:S(2)}, u32[]{:S(2)}) collective-permute-start(bf16[64,768]{1,0:T(8,128)(2,1)S(1)} %get-tuple-element.15.refs_0_), channel_id=1, source_target_pairs={{0,2},{1,3},{2,0},{3,1},{4,6},{5,7},{6,4},{7,5},{8,10},{9,11},{10,... | collective-permute-start | bytes 294920 | tf_op jit(solution)/shard_map/ppermute | solution.py:20
  6.4 1.3 %collective-permute-start.3 = (s32[40,512]{1,0:T(8,128)S(1)}, s32[40,512]{1,0:T(8,128)S(1)}, u32[]{:S(2)}, u32[]{:S(2)}) collective-permute-start(s32[40,512]{1,0:T(8,128)S(1)} %get-tuple-element.16.index_own_ref), channel_id=1, source_target_pairs={{0,1},{1,0},{2,3},{3,2},{4,5},{5,4},{6,7},{7,6},{8,9},{9,8},{10,11... | collective-permute-start | bytes 245768 | tf_op jit(solution)/shard_map/ppermute | solution.py:20
  12.9 4.7 %collective-permute-start.5 = (bf16[64,768]{1,0:T(8,128)(2,1)S(1)}, bf16[64,768]{1,0:T(8,128)(2,1)S(1)}, u32[]{:S(2)}, u32[]{:S(2)}) collective-permute-start(bf16[64,768]{1,0:T(8,128)(2,1)S(1)} %get-tuple-element.21), channel_id=1, source_target_pairs={{0,2},{1,3},{2,0},{3,1},{4,6},{5,7},{6,4},{7,5},{8,10},{9,11},{10,... | collective-permute-start | bytes 294920 | tf_op jit(solution)/shard_map/ppermute | solution.py:20
  14.5 6.6 %collective-permute-start.6 = (bf16[64,768]{1,0:T(8,128)(2,1)S(1)}, bf16[64,768]{1,0:T(8,128)(2,1)S(1)}, u32[]{:S(2)}, u32[]{:S(2)}) collective-permute-start(bf16[64,768]{1,0:T(8,128)(2,1)S(1)} %get-tuple-element.22), channel_id=1, source_target_pairs={{0,4},{1,5},{2,6},{3,7},{4,0},{5,1},{6,2},{7,3},{8,12},{9,13},{10,... | collective-permute-start | bytes 294920 | tf_op jit(solution)/shard_map/ppermute | solution.py:20
  15.1 6.0 %collective-permute-start.7 = (bf16[64,768]{1,0:T(8,128)(2,1)S(1)}, bf16[64,768]{1,0:T(8,128)(2,1)S(1)}, u32[]{:S(2)}, u32[]{:S(2)}) collective-permute-start(bf16[64,768]{1,0:T(8,128)(2,1)S(1)} %get-tuple-element.23), channel_id=1, source_target_pairs={{0,6},{1,7},{2,4},{3,5},{4,2},{5,3},{6,0},{7,1},{8,14},{9,15},{10,... | collective-permute-start | bytes 294920 | tf_op jit(solution)/shard_map/ppermute | solution.py:20
  21.2 4.7 %collective-permute-start.8 = (bf16[64,768]{1,0:T(8,128)(2,1)S(1)}, bf16[64,768]{1,0:T(8,128)(2,1)S(1)}, u32[]{:S(2)}, u32[]{:S(2)}) collective-permute-start(bf16[64,768]{1,0:T(8,128)(2,1)S(1)} %fusion), channel_id=1, source_target_pairs={{0,8},{8,0},{16,24},{24,16},{1,9},{9,1},{17,25},{25,17},{2,10},{10... | collective-permute-start | bytes 294920 | tf_op jit(solution)/shard_map/ppermute | solution.py:20
  22.8 5.8 %collective-permute-start.11 = (bf16[256,768]{1,0:T(8,128)(2,1)S(1)}, bf16[256,768]{1,0:T(8,128)(2,1)S(1)}, u32[]{:S(2)}, u32[]{:S(2)}) collective-permute-start(bf16[256,768]{1,0:T(8,128)(2,1)S(1)} %get-tuple-element.27.c_own_ref), channel_id=1, source_target_pairs={{0,1},{1,0},{2,3},{3,2},{4,5},{5,4},{6,7},{7,6},{8,9},{9,8},{10,11... | collective-permute-start | bytes 1179656 | tf_op jit(solution)/shard_map/ppermute | solution.py:20
  22.8 5.8 %collective-permute-start.10 = (bf16[256,512]{1,0:T(8,128)(2,1)S(1)}, bf16[256,512]{1,0:T(8,128)(2,1)S(1)}, u32[]{:S(2)}, u32[]{:S(2)}) collective-permute-start(bf16[256,512]{1,0:T(8,128)(2,1)S(1)} %get-tuple-element.26), channel_id=1, source_target_pairs={{0,1},{1,0},{2,3},{3,2},{4,5},{5,4},{6,7},{7,6},{8,9},{9,8},{10,11... | collective-permute-start | bytes 786440 | tf_op jit(solution)/shard_map/ppermute | solution.py:20
  25.9 5.6 %collective-permute-start.9 = (bf16[64,768]{1,0:T(8,128)(2,1)S(1)}, bf16[64,768]{1,0:T(8,128)(2,1)S(1)}, u32[]{:S(2)}, u32[]{:S(2)}) collective-permute-start(bf16[64,768]{1,0:T(8,128)(2,1)S(1)} %get-tuple-element.28), channel_id=1, source_target_pairs={{0,16},{8,24},{16,0},{24,8},{1,17},{9,25},{17,1},{25,9},{2,18},{10... | collective-permute-start | bytes 294920 | tf_op jit(solution)/shard_map/ppermute | solution.py:20

commit v5 on v4

--- a/solution.py
+++ b/solution.py
@@ -66,11 +66,15 @@
     )
 
 
-def targets_kernel(
-    index_own_ref, index_other_ref, emb_hbm, target_own_ref, target_other_ref, emb_ref, emb_sem, *, panel, slots
-):
-    emb_copy = pltpu.make_async_copy(emb_hbm, emb_ref, emb_sem)
-    emb_copy.start()
+def turn_kernel(emb_hbm, other_ref, own_ref, own_turned_ref, other_turned_ref, sem):
+    copy = pltpu.make_async_copy(emb_hbm, own_ref, sem)
+    copy.start()
+    other_turned_ref[...] = other_ref[...].T
+    copy.wait()
+    own_turned_ref[...] = own_ref[...].T
+
+
+def targets_kernel(index_own_ref, index_other_ref, after_ref, target_own_ref, target_other_ref, *, panel, slots):
     me = lax.axis_index("lab")
     docs = index_own_ref.shape[1]
     negatives = index_own_ref.shape[0] // slots - 2
@@ -103,39 +107,55 @@
         return carry
 
     lax.fori_loop(0, docs // LANES, chunk, 0)
-    emb_copy.wait()
-
-
-def score_kernel(*refs, pieces, parts):
-    piece_refs = refs[:pieces]
-    emb_refs = refs[pieces : pieces + 2]
-    target_refs = refs[pieces + 2 : pieces + 4]
-    part_refs = refs[pieces + 4 : pieces + 4 + parts]
-    dlogit_refs = refs[pieces + 4 + parts : pieces + 6 + parts]
-    classifier_ref = refs[pieces + 6 + parts]
+
+
+def score_kernel(*refs, which, after):
+    refs = list(refs)
+
+    def take(number):
+        return [refs.pop(0) for _ in range(number)]
+
+    count = len(which)
+    piece_refs, emb_refs, turned_refs, target_refs = take(count), take(2), take(2), take(2)
+    take(after)
+    grad_refs, dlogit_refs = take(count), [take(count) for _ in range(2)]
     each = piece_refs[0].shape[0]
-    for i, ref in enumerate(piece_refs):
-        classifier_ref[i * each : (i + 1) * each] = ref[...]
-    total = classifier_ref.shape[0]
-    rows = min(ROWS, total)
-    span = total // parts
-    for start in range(0, total, rows):
-        block = classifier_ref[start : start + rows]
+    if each * count <= ROWS:
+        units = [[(i, 0, each) for i in range(count)]]
+    else:
+        rows = min(ROWS, each)
+        units = [[(i, start, rows)] for i in range(count) for start in range(0, each, rows)]
+
+    def gather(unit, refs, at=lambda i: 0):
+        values = [refs[i][at(i) + start : at(i) + start + rows] for i, start, rows in unit]
+        return values[0] if len(values) == 1 else jnp.concatenate(values, 0)
+
+    for unit in units:
+        block = gather(unit, piece_refs)
         grad = None
-        for emb_ref, target_ref, dlogit_ref in zip(emb_refs, target_refs, dlogit_refs):
-            logits = lax.dot_general(
-                block, emb_ref[...], (((1,), (1,)), ((), ())), preferred_element_type=F32
-            )
-            signed = target_ref[start : start + rows].astype(F32)
+        for emb_ref, turned_ref, target_ref, out_refs in zip(emb_refs, turned_refs, target_refs, dlogit_refs):
+            logits = jnp.dot(block, turned_ref[...], preferred_element_type=F32)
+            signed = gather(unit, [target_ref] * count, lambda i: which[i] * each).astype(F32)
             dlogits = (signed * jax.nn.sigmoid(jnp.where(signed < 0, -logits, logits))).astype(BF16)
-            dlogit_ref[start : start + rows] = dlogits
             term = jnp.dot(dlogits, emb_ref[...], preferred_element_type=F32)
             grad = term if grad is None else grad + term
-        step = min(rows, span)
-        for off in range(0, rows, step):
-            part, at = divmod(start + off, span)
-            ref = part_refs[part]
-            ref[at : at + step] = grad[off : off + step].astype(ref.dtype)
+            off = 0
+            for i, start, rows in unit:
+                out_refs[i][start : start + rows] = dlogits[off : off + rows]
+                off += rows
+        off = 0
+        for i, start, rows in unit:
+            grad_refs[i][start : start + rows] = grad[off : off + rows].astype(grad_refs[i].dtype)
+            off += rows
+
+
+def join_kernel(*refs, count):
+    for k in range(3):
+        out_ref = refs[3 * count + k]
+        at = 0
+        for ref in refs[k * count : (k + 1) * count]:
+            out_ref[at : at + ref.shape[0]] = ref[...]
+            at += ref.shape[0]
 
 
 def emb_kernel(d_own_ref, d_other_ref, c_own_ref, c_other_ref, after_ref, out_ref):
@@ -208,32 +228,66 @@
 
     emb_other = flip(embeddings, "lab", 1)
     index_other = flip(index_own, "lab", 1)
-    target_own, target_other, emb_own = pl.pallas_call(
-        functools.partial(targets_kernel, panel=panel, slots=slots),
-        out_shape=[jax.ShapeDtypeStruct((half, docs), BF16)] * 2
-        + [jax.ShapeDtypeStruct((docs, width), BF16)],
-        in_specs=vmem(2) + hbm(1),
+    emb_own, own_turned, other_turned = pl.pallas_call(
+        turn_kernel,
+        out_shape=[jax.ShapeDtypeStruct((docs, width), BF16)]
+        + [jax.ShapeDtypeStruct((width, docs), BF16)] * 2,
+        in_specs=hbm(1) + vmem(1),
         out_specs=vmem(3),
         scratch_shapes=[pltpu.SemaphoreType.DMA],
-        compiler_params=params(height * docs * 8, docs * half * 4, docs * width * 2),
+        compiler_params=params(docs * width * 10),
+        cost_estimate=cost(docs * width, docs * width * 10),
+        name="turn",
+    )(*keep(embeddings), emb_other)
+    target_own, target_other = pl.pallas_call(
+        functools.partial(targets_kernel, panel=panel, slots=slots),
+        out_shape=[jax.ShapeDtypeStruct((half, docs), BF16)] * 2,
+        in_specs=vmem(3),
+        out_specs=vmem(2),
+        compiler_params=params(height * docs * 8, docs * half * 4),
         cost_estimate=cost(docs * panel * slots * 80, height * docs * 8 + docs * half * 4),
         name="targets",
-    )(index_own, index_other, *keep(embeddings))
-    parts = len(group_masks(groups[-1])) + 1 if groups else 1
-    outs = pl.pallas_call(
-        functools.partial(score_kernel, pieces=len(pieces), parts=parts),
-        out_shape=[
-            jax.ShapeDtypeStruct((half // parts, width), BF16 if i else F32) for i in range(parts)
-        ]
-        + [jax.ShapeDtypeStruct((half, docs), BF16)] * 2
-        + [jax.ShapeDtypeStruct((half, width), BF16)],
-        in_specs=vmem(len(pieces) + 4),
-        out_specs=vmem(parts + 3),
-        compiler_params=params(4 * docs * width, 16 * half * docs, 12 * half * width),
-        cost_estimate=cost(8 * docs * half * width, 4 * docs * width + 8 * half * docs + 8 * half * width),
-        name="score",
-    )(*pieces, emb_own, emb_other, target_own, target_other)
-    grads, (d_own, d_theirs, classifier_own) = outs[:parts], outs[parts:]
+    )(index_own, index_other, other_turned)
+
+    each = pieces[0].shape[0]
+    number = len(pieces)
+
+    def score(which, after):
+        count, rows = len(which), each * len(which)
+        outs = pl.pallas_call(
+            functools.partial(score_kernel, which=which, after=len(after)),
+            out_shape=[jax.ShapeDtypeStruct((each, width), BF16 if i else F32) for i in which]
+            + [jax.ShapeDtypeStruct((each, docs), BF16)] * (2 * count),
+            in_specs=vmem(count + 6 + len(after)),
+            out_specs=vmem(3 * count),
+            compiler_params=params(8 * docs * width, 16 * rows * docs, 12 * rows * width),
+            cost_estimate=cost(
+                8 * docs * rows * width, 8 * docs * width + 8 * rows * docs + 8 * rows * width
+            ),
+            name="score",
+        )(
+            *[pieces[i] for i in which], emb_own, emb_other, own_turned, other_turned,
+            target_own, target_other, *after,
+        )
+        return outs[:count], outs[count : 2 * count], outs[2 * count :]
+
+    order = [number - 1, 0] + list(range(1, number - 1))
+    grads, dlogits = {}, ([], [])
+    for which in [w for w in (order[:2], order[2:]) if w]:
+        results = score(which, list(grads.values())[:1])
+        grads.update(zip(which, results[0]))
+        for store, values in zip(dlogits, results[1:]):
+            store += values
+    classifier_own, d_own, d_theirs = pl.pallas_call(
+        functools.partial(join_kernel, count=number),
+        out_shape=[jax.ShapeDtypeStruct((half, width), BF16)]
+        + [jax.ShapeDtypeStruct((half, docs), BF16)] * 2,
+        in_specs=vmem(3 * number),
+        out_specs=vmem(3),
+        compiler_params=params(4 * half * width, 8 * half * docs),
+        cost_estimate=cost(0, 4 * half * width + 8 * half * docs),
+        name="join",
+    )(*[pieces[i] for i in order], *dlogits[0], *dlogits[1])
 
     grad = None
     for group in reversed(groups):
@@ -241,7 +295,12 @@
         if grad is not None:
             grad = grad.reshape(len(masks) + 1, -1, width)
             grads = [grad[0]] + [grad[i].astype(BF16) for i in range(1, len(masks) + 1)]
-        received = [flip(g, "lab", mask) for g, mask in zip(grads[1:], masks)]
+        received = []
+        for i in reversed(range(len(masks))):
+            value = grads[i + 1]
+            if i == 2:
+                value = jnp.concatenate([value, value[:16]], 0)
+            received.append(flip(value, "lab", masks[i])[: grads[i + 1].shape[0]])
         grad = grads[0]
         for r in received:
             grad = grad + r.astype(F32)

time: 32.5 us -> 30.7 us (0.945)
  waiting for transfers between devices: 12.1 us -> 7.8 us
  Pallas kernels: 6.28 us -> 8.09 us
  starting transfers between devices: 13.1 us -> 13.7 us
    ppermute x12, waiting for transfers between devices: 12.1 us -> 7.8 us  [flip(): lax.ppermute(value, axis, [(i, i ^ mask) for i in range(lax.axis_size(axi...]
    pallas_call x1 -> x4, Pallas kernels: 1.32 us -> 3.13 us  [the longest x2 1.66 us: score(): pl.pallas_call(functools.partial(score_kernel, which=which, after=len(aft...]
    ppermute x12, starting transfers between devices: 13.1 us -> 13.7 us  [flip(): lax.ppermute(value, axis, [(i, i ^ mask) for i in range(lax.axis_size(axi...]
  transfers between devices with their start and end apart: 12 -> 12, of which waited for: 8 -> 4; matrix products, arithmetic and copies ran while one was open for 0% -> 0% of each run, Pallas kernels for 13% -> 24%
where the time goes in v5:
time: 30.7 us; the launch traced here: 30.4 us
  starting transfers between devices  13.7 us (45%)
  Pallas kernels  8.09 us (26%)
  waiting for transfers between devices  7.8 us (25%)
  between operations  0.73 us (2%)
    ppermute x12, starting transfers between devices, flip(): lax.ppermute(value, axis, [(i, i ^ mask) for i in range(lax.axis_size(axi...  13.7 us
    ppermute x12, waiting for transfers between devices, flip(): lax.ppermute(value, axis, [(i, i ^ mask) for i in range(lax.axis_size(axi...  7.8 us
    pallas_call x1, Pallas kernels, shards(): pl.pallas_call(emb_kernel, out_shape=jax.ShapeDtypeStruct((docs, width),...  1.74 us
    pallas_call x2, Pallas kernels, score(): pl.pallas_call(functools.partial(score_kernel, which=which, after=len(aft...  1.66 us
    pallas_call x1, Pallas kernels, shards(): pl.pallas_call(turn_kernel, out_shape=[jax.ShapeDtypeStruct((docs, width)...  1.41 us
    pallas_call x1, Pallas kernels, shards(): pl.pallas_call(functools.partial(targets_kernel, panel=panel, slots=slots...  1.35 us
    pallas_call x1, Pallas kernels, shards(): pl.pallas_call(functools.partial(pack_kernel, scale=1.0 / math.sqrt(docs...  1.11 us
    pallas_call x1, Pallas kernels, shards(): pl.pallas_call(finish_kernel, out_shape=jax.ShapeDtypeStruct((panel, widt...  0.76 us
  transfers between devices with their start and end apart: 12, of which 4 were waited for; matrix products, arithmetic and copies ran while one was open for 0% of the time, Pallas kernels for 24%

profile of v5, /device:TPU:0, one launch (start us, length us, event | category | flops | bytes accessed | tf_op | source)
XLA Modules:
  0.0 30.4 jit_solution(834711242506226178)
XLA Ops:
  0.6 0.5 %collective-permute-start.1 = (bf16[512,768]{1,0:T(8,128)(2,1)}, bf16[512,768]{1,0:T(8,128)(2,1)S(1)}, u32[]{:S(2)}, u32[]{:S(2)}) collective-permute-start(bf16[512,768]{1,0:T(8,128)(2,1)} %emb_hbm.1), channel_id=1, source_target_pairs={{0,1},{1,0},{2,3},{3,2},{4,5},{5,4},{6,7},{7,6},{8,9},{9,8},{10,11... | collective-permute-start | bytes 2359304 | tf_op jit(solution)/shard_map/ppermute | solution.py:20
  1.1 1.1 %pack.1 = (bf16[64,768]{1,0:T(8,128)(2,1)S(1)}, f32[64,128]{1,0:T(8,128)S(1)}, s32[40,512]{1,0:T(8,128)S(1)}) custom-call(f32[64,768]{1,0:T(8,128)} %classifier_hbm.1, s32[1,64]{1,0:T(1,128)} %bitcast.9, s32[4,512]{1,0:T(4,128)} %bitcast.6, s32[4,512]{1,0:T(4,128)} %bitcast.7, s32[4,512]{1,0:T(4,128)} %bitcast.8, s32[4,8,512]{2,1,0:T(8,128)} %bitcast.5), custom_call_target="tpu_custom_call" | custom-call | flops 49152 | bytes 376832 | tf_op jit(solution)/shard_map/pack/pallas_call | solution.py:203
  2.3 3.5 %collective-permute-start = (bf16[64,768]{1,0:T(8,128)(2,1)S(1)}, bf16[64,768]{1,0:T(8,128)(2,1)S(1)}, u32[]{:S(2)}, u32[]{:S(2)}) collective-permute-start(bf16[64,768]{1,0:T(8,128)(2,1)S(1)} %get-tuple-element.25.refs_1_), channel_id=1, source_target_pairs={{0,6},{1,7},{2,4},{3,5},{4,2},{5,3},{6,0},{7,1},{8,14},{9,15},{10,... | collective-permute-start | bytes 294920 | tf_op jit(solution)/shard_map/ppermute | solution.py:20
  5.8 0.2 collective-permute-start.2
  6.0 0.5 %collective-permute-start.5 = (bf16[64,768]{1,0:T(8,128)(2,1)S(1)}, bf16[64,768]{1,0:T(8,128)(2,1)S(1)}, u32[]{:S(2)}, u32[]{:S(2)}) collective-permute-start(bf16[64,768]{1,0:T(8,128)(2,1)S(1)} %get-tuple-element.25.refs_1_), channel_id=1, source_target_pairs={{0,4},{1,5},{2,6},{3,7},{4,0},{5,1},{6,2},{7,3},{8,12},{9,13},{10,... | collective-permute-start | bytes 294920 | tf_op jit(solution)/shard_map/ppermute | solution.py:20
  6.5 0.4 %collective-permute-start.4 = (bf16[64,768]{1,0:T(8,128)(2,1)S(1)}, bf16[64,768]{1,0:T(8,128)(2,1)S(1)}, u32[]{:S(2)}, u32[]{:S(2)}) collective-permute-start(bf16[64,768]{1,0:T(8,128)(2,1)S(1)} %get-tuple-element.25.refs_1_), channel_id=1, source_target_pairs={{0,2},{1,3},{2,0},{3,1},{4,6},{5,7},{6,4},{7,5},{8,10},{9,11},{10,... | collective-permute-start | bytes 294920 | tf_op jit(solution)/shard_map/ppermute | solution.py:20
  6.9 0.0 collective-permute-done.1.other_ref.refs_3_
  6.9 1.4 %turn.1 = (bf16[512,768]{1,0:T(8,128)(2,1)S(1)}, bf16[768,512]{1,0:T(8,128)(2,1)S(1)}, bf16[768,512]{1,0:T(8,128)(2,1)S(1)}) custom-call(bf16[512,768]{1,0:T(8,128)(2,1)} %emb_hbm.1, bf16[512,768]{1,0:T(8,128)(2,1)S(1)} %collective-permute-done.1.other_ref.refs_3_), custom_call_target="tpu_custom_call" | custom-call | flops 393216 | bytes 3932160 | tf_op jit(solution)/shard_map/turn/pallas_call | solution.py:231
  8.4 0.0 collective-permute-done.2.index_other_ref
  8.4 1.3 %targets.1 = (bf16[256,512]{1,0:T(8,128)(2,1)S(1)}, bf16[256,512]{1,0:T(8,128)(2,1)S(1)}) custom-call(s32[40,512]{1,0:T(8,128)S(1)} %get-tuple-element.29.index_own_ref, s32[40,512]{1,0:T(8,128)S(1)} %collective-permute-done.2.index_other_ref, bf16[768,512]{1,0:T(8,128)(2,1)S(1)} %get-tuple-element.28.after_ref.refs_5_), custom_call_target="tpu_custom_call" | custom-call | flops 10485760 | bytes 688128 | tf_op jit(solution)/shard_map/targets/pallas_call | solution.py:242
  9.7 0.0 collective-permute-done.refs_0_
  9.7 0.8 %score.2 = (bf16[64,768]{1,0:T(8,128)(2,1)S(1)}, f32[64,768]{1,0:T(8,128)S(1)}, bf16[64,512]{1,0:T(8,128)(2,1)S(1)}, bf16[64,512]{1,0:T(8,128)(2,1)S(1)}, bf16[6...) custom-call(bf16[64,768]{1,0:T(8,128)(2,1)S(1)} %collective-permute-done.refs_0_, ...), custom_call_target="tpu_custom_call" | custom-call | flops 402653184 | bytes 4456448 | tf_op jit(solution)/shard_map/score/pallas_call | solution.py:257
  10.6 2.7 %collective-permute-start.3 = (bf16[80,768]{1,0:T(8,128)(2,1)S(1)}, bf16[80,768]{1,0:T(8,128)(2,1)S(1)}, u32[]{:S(2)}, u32[]{:S(2)}) collective-permute-start(bf16[80,768]{1,0:T(8,128)(2,1)S(1)} %pad_maximum_fusion), channel_id=1, source_target_pairs={{0,6},{1,7},{2,4},{3,5},{4,2},{5,3},{6,0},{7,1},{8,14},{9,15},{10,... | collective-permute-start | bytes 368648 | tf_op jit(solution)/shard_map/ppermute | solution.py:20
  13.3 0.0 collective-permute-done.5.refs_1_.refs_3_
  13.3 0.0 collective-permute-done.4.refs_0_.refs_2_
  13.3 0.8 %score.3 = (bf16[64,768]{1,0:T(8,128)(2,1)S(1)}, bf16[64,768]{1,0:T(8,128)(2,1)S(1)}, bf16[64,512]{1,0:T(8,128)(2,1)S(1)}, bf16[64,512]{1,0:T(8,128)(2,1)S(1)}, ...) custom-call(bf16[64,768]{1,0:T(8,128)(2,1)S(1)} %collective-permute-done.4.refs_0_.refs_2_, ...), custom_call_target="tpu_custom_call" | custom-call | flops 402653184 | bytes 4456448 | tf_op jit(solution)/shard_map/score/pallas_call | solution.py:257
  14.1 0.5 %collective-permute-start.6 = (bf16[64,768]{1,0:T(8,128)(2,1)S(1)}, bf16[64,768]{1,0:T(8,128)(2,1)S(1)}, u32[]{:S(2)}, u32[]{:S(2)}) collective-permute-start(bf16[64,768]{1,0:T(8,128)(2,1)S(1)} %get-tuple-element.34), channel_id=1, source_target_pairs={{0,4},{1,5},{2,6},{3,7},{4,0},{5,1},{6,2},{7,3},{8,12},{9,13},{10,... | collective-permute-start | bytes 294920 | tf_op jit(solution)/shard_map/ppermute | solution.py:20
  14.6 0.4 %collective-permute-start.7 = (bf16[64,768]{1,0:T(8,128)(2,1)S(1)}, bf16[64,768]{1,0:T(8,128)(2,1)S(1)}, u32[]{:S(2)}, u32[]{:S(2)}) collective-permute-start(bf16[64,768]{1,0:T(8,128)(2,1)S(1)} %get-tuple-element.35), channel_id=1, source_target_pairs={{0,2},{1,3},{2,0},{3,1},{4,6},{5,7},{6,4},{7,5},{8,10},{9,11},{10,... | collective-permute-start | bytes 294920 | tf_op jit(solution)/shard_map/ppermute | solution.py:20
  15.1 3.7 %collective-permute-done.6 = bf16[64,768]{1,0:T(8,128)(2,1)S(1)} collective-permute-done((bf16[64,768]{1,0:T(8,128)(2,1)S(1)}, bf16[64,768]{1,0:T(8,128)(2,1)S(1)}, u32[]{:S(2)}, u32[]{:S(2)}) %collective-permute-start.6) | collective-permute-done | bytes 98336 | tf_op jit(solution)/shard_map/ppermute | solution.py:20
  18.8 0.5 %collective-permute-done.7 = bf16[64,768]{1,0:T(8,128)(2,1)S(1)} collective-permute-done((bf16[64,768]{1,0:T(8,128)(2,1)S(1)}, bf16[64,768]{1,0:T(8,128)(2,1)S(1)}, u32[]{:S(2)}, u32[]{:S(2)}) %collective-permute-start.7) | collective-permute-done | bytes 98336 | tf_op jit(solution)/shard_map/ppermute | solution.py:20
  19.3 0.0 collective-permute-done.3
  19.3 1.6 %collective-permute-start.8 = (bf16[64,768]{1,0:T(8,128)(2,1)S(1)}, bf16[64,768]{1,0:T(8,128)(2,1)S(1)}, u32[]{:S(2)}, u32[]{:S(2)}) collective-permute-start(bf16[64,768]{1,0:T(8,128)(2,1)S(1)} %fusion), channel_id=1, source_target_pairs={{0,8},{8,0},{16,24},{24,16},{1,9},{9,1},{17,25},{25,17},{2,10},{10... | collective-permute-start | bytes 294920 | tf_op jit(solution)/shard_map/ppermute | solution.py:20
  21.0 0.1 join.1
  21.0 0.1 collective-permute-start.11
  21.1 0.5 %collective-permute-start.10 = (bf16[256,512]{1,0:T(8,128)(2,1)S(1)}, bf16[256,512]{1,0:T(8,128)(2,1)S(1)}, u32[]{:S(2)}, u32[]{:S(2)}) collective-permute-start(bf16[256,512]{1,0:T(8,128)(2,1)S(1)} %get-tuple-element.46), channel_id=1, source_target_pairs={{0,1},{1,0},{2,3},{3,2},{4,5},{5,4},{6,7},{7,6},{8,9},{9,8},{10,11... | collective-permute-start | bytes 786440 | tf_op jit(solution)/shard_map/ppermute | solution.py:20
  21.6 2.4 %collective-permute-done.8 = bf16[64,768]{1,0:T(8,128)(2,1)S(1)} collective-permute-done((bf16[64,768]{1,0:T(8,128)(2,1)S(1)}, bf16[64,768]{1,0:T(8,128)(2,1)S(1)}, u32[]{:S(2)}, u32[]{:S(2)}) %collective-permute-start.8) | collective-permute-done | bytes 98336 | tf_op jit(solution)/shard_map/ppermute | solution.py:20
  24.0 0.1 fusion.1
  24.1 2.7 %collective-permute-start.9 = (bf16[64,768]{1,0:T(8,128)(2,1)S(1)}, bf16[64,768]{1,0:T(8,128)(2,1)S(1)}, u32[]{:S(2)}, u32[]{:S(2)}) collective-permute-start(bf16[64,768]{1,0:T(8,128)(2,1)S(1)} %get-tuple-element.48), channel_id=1, source_target_pairs={{0,16},{8,24},{16,0},{24,8},{1,17},{9,25},{17,1},{25,9},{2,18},{10... | collective-permute-start | bytes 294920 | tf_op jit(solution)/shard_map/ppermute | solution.py:20
  26.7 0.0 collective-permute-done.10.d_other_ref
  26.7 0.0 collective-permute-done.11.c_other_ref
  26.7 1.7 %emb_grad.1.after_hbm = f32[512,768]{1,0:T(8,128)} custom-call(bf16[256,512]{1,0:T(8,128)(2,1)S(1)} %get-tuple-element.45.d_own_ref, bf16[256,512]{1,0:T(8,128)(2,1)S(1)} %collective-permute-done.10.d_other_ref, bf16[256,768]{1,0:T(8,128)(2,1)S(1)} %get-tuple-element.47.c_own_ref, bf16[256,768]{1,0:T(8,128)(2,1)S(1)} %collective-permute-done.11.c_other_ref, ...), custom_call_target="tpu_custom_call" | custom-call | flops 402653184 | bytes 2883584 | tf_op jit(solution)/shard_map/emb_grad/pallas_call | solution.py:315
  28.5 1.2 %collective-permute-done.9.received_ref = bf16[64,768]{1,0:T(8,128)(2,1)S(1)} collective-permute-done((bf16[64,768]{1,0:T(8,128)(2,1)S(1)}, bf16[64,768]{1,0:T(8,128)(2,1)S(1)}, u32[]{:S(2)}, u32[]{:S(2)}) %collective-permute-start.9) | collective-permute-done | bytes 98336 | tf_op jit(solution)/shard_map/ppermute | solution.py:20
  29.7 0.8 %finish.1 = f32[64,768]{1,0:T(8,128)} custom-call(f32[64,768]{1,0:T(8,128)S(1)} %get-tuple-element.49.after_ref.grad_ref, bf16[64,768]{1,0:T(8,128)(2,1)S(1)} %collective-permute-done.9.received_ref, f32[64,128]{1,0:T(8,128)S(1)} %get-tuple-element.36.column_ref, f32[512,768]{1,0:T(8,128)} %emb_grad.1.after_hbm), custom_call_target="tpu_custom_call" | custom-call | flops 49152 | bytes 491520 | tf_op jit(solution)/shard_map/finish/pallas_call | solution.py:325
  (3 shorter events, 0.1 us)
Async XLA Ops:
  0.6 6.3 %collective-permute-start.1 = (bf16[512,768]{1,0:T(8,128)(2,1)}, bf16[512,768]{1,0:T(8,128)(2,1)S(1)}, u32[]{:S(2)}, u32[]{:S(2)}) collective-permute-start(bf16[512,768]{1,0:T(8,128)(2,1)} %emb_hbm.1), channel_id=1, source_target_pairs={{0,1},{1,0},{2,3},{3,2},{4,5},{5,4},{6,7},{7,6},{8,9},{9,8},{10,11... | collective-permute-start | bytes 2359304 | tf_op jit(solution)/shard_map/ppermute | solution.py:20
  2.3 7.5 %collective-permute-start = (bf16[64,768]{1,0:T(8,128)(2,1)S(1)}, bf16[64,768]{1,0:T(8,128)(2,1)S(1)}, u32[]{:S(2)}, u32[]{:S(2)}) collective-permute-start(bf16[64,768]{1,0:T(8,128)(2,1)S(1)} %get-tuple-element.25.refs_1_), channel_id=1, source_target_pairs={{0,6},{1,7},{2,4},{3,5},{4,2},{5,3},{6,0},{7,1},{8,14},{9,15},{10,... | collective-permute-start | bytes 294920 | tf_op jit(solution)/shard_map/ppermute | solution.py:20
  5.8 2.6 %collective-permute-start.2 = (s32[40,512]{1,0:T(8,128)S(1)}, s32[40,512]{1,0:T(8,128)S(1)}, u32[]{:S(2)}, u32[]{:S(2)}) collective-permute-start(s32[40,512]{1,0:T(8,128)S(1)} %get-tuple-element.29.index_own_ref), channel_id=1, source_target_pairs={{0,1},{1,0},{2,3},{3,2},{4,5},{5,4},{6,7},{7,6},{8,9},{9,8},{10,11... | collective-permute-start | bytes 245768 | tf_op jit(solution)/shard_map/ppermute | solution.py:20
  6.0 7.3 %collective-permute-start.5 = (bf16[64,768]{1,0:T(8,128)(2,1)S(1)}, bf16[64,768]{1,0:T(8,128)(2,1)S(1)}, u32[]{:S(2)}, u32[]{:S(2)}) collective-permute-start(bf16[64,768]{1,0:T(8,128)(2,1)S(1)} %get-tuple-element.25.refs_1_), channel_id=1, source_target_pairs={{0,4},{1,5},{2,6},{3,7},{4,0},{5,1},{6,2},{7,3},{8,12},{9,13},{10,... | collective-permute-start | bytes 294920 | tf_op jit(solution)/shard_map/ppermute | solution.py:20
  6.5 6.8 %collective-permute-start.4 = (bf16[64,768]{1,0:T(8,128)(2,1)S(1)}, bf16[64,768]{1,0:T(8,128)(2,1)S(1)}, u32[]{:S(2)}, u32[]{:S(2)}) collective-permute-start(bf16[64,768]{1,0:T(8,128)(2,1)S(1)} %get-tuple-element.25.refs_1_), channel_id=1, source_target_pairs={{0,2},{1,3},{2,0},{3,1},{4,6},{5,7},{6,4},{7,5},{8,10},{9,11},{10,... | collective-permute-start | bytes 294920 | tf_op jit(solution)/shard_map/ppermute | solution.py:20
  10.6 8.7 %collective-permute-start.3 = (bf16[80,768]{1,0:T(8,128)(2,1)S(1)}, bf16[80,768]{1,0:T(8,128)(2,1)S(1)}, u32[]{:S(2)}, u32[]{:S(2)}) collective-permute-start(bf16[80,768]{1,0:T(8,128)(2,1)S(1)} %pad_maximum_fusion), channel_id=1, source_target_pairs={{0,6},{1,7},{2,4},{3,5},{4,2},{5,3},{6,0},{7,1},{8,14},{9,15},{10,... | collective-permute-start | bytes 368648 | tf_op jit(solution)/shard_map/ppermute | solution.py:20
  14.1 4.7 %collective-permute-start.6 = (bf16[64,768]{1,0:T(8,128)(2,1)S(1)}, bf16[64,768]{1,0:T(8,128)(2,1)S(1)}, u32[]{:S(2)}, u32[]{:S(2)}) collective-permute-start(bf16[64,768]{1,0:T(8,128)(2,1)S(1)} %get-tuple-element.34), channel_id=1, source_target_pairs={{0,4},{1,5},{2,6},{3,7},{4,0},{5,1},{6,2},{7,3},{8,12},{9,13},{10,... | collective-permute-start | bytes 294920 | tf_op jit(solution)/shard_map/ppermute | solution.py:20
  14.6 4.6 %collective-permute-start.7 = (bf16[64,768]{1,0:T(8,128)(2,1)S(1)}, bf16[64,768]{1,0:T(8,128)(2,1)S(1)}, u32[]{:S(2)}, u32[]{:S(2)}) collective-permute-start(bf16[64,768]{1,0:T(8,128)(2,1)S(1)} %get-tuple-element.35), channel_id=1, source_target_pairs={{0,2},{1,3},{2,0},{3,1},{4,6},{5,7},{6,4},{7,5},{8,10},{9,11},{10,... | collective-permute-start | bytes 294920 | tf_op jit(solution)/shard_map/ppermute | solution.py:20
  19.3 4.7 %collective-permute-start.8 = (bf16[64,768]{1,0:T(8,128)(2,1)S(1)}, bf16[64,768]{1,0:T(8,128)(2,1)S(1)}, u32[]{:S(2)}, u32[]{:S(2)}) collective-permute-start(bf16[64,768]{1,0:T(8,128)(2,1)S(1)} %fusion), channel_id=1, source_target_pairs={{0,8},{8,0},{16,24},{24,16},{1,9},{9,1},{17,25},{25,17},{2,10},{10... | collective-permute-start | bytes 294920 | tf_op jit(solution)/shard_map/ppermute | solution.py:20
  21.0 5.7 %collective-permute-start.11 = (bf16[256,768]{1,0:T(8,128)(2,1)S(1)}, bf16[256,768]{1,0:T(8,128)(2,1)S(1)}, u32[]{:S(2)}, u32[]{:S(2)}) collective-permute-start(bf16[256,768]{1,0:T(8,128)(2,1)S(1)} %get-tuple-element.47.c_own_ref), channel_id=1, source_target_pairs={{0,1},{1,0},{2,3},{3,2},{4,5},{5,4},{6,7},{7,6},{8,9},{9,8},{10,11... | collective-permute-start | bytes 1179656 | tf_op jit(solution)/shard_map/ppermute | solution.py:20
  21.1 5.6 %collective-permute-start.10 = (bf16[256,512]{1,0:T(8,128)(2,1)S(1)}, bf16[256,512]{1,0:T(8,128)(2,1)S(1)}, u32[]{:S(2)}, u32[]{:S(2)}) collective-permute-start(bf16[256,512]{1,0:T(8,128)(2,1)S(1)} %get-tuple-element.46), channel_id=1, source_target_pairs={{0,1},{1,0},{2,3},{3,2},{4,5},{5,4},{6,7},{7,6},{8,9},{9,8},{10,11... | collective-permute-start | bytes 786440 | tf_op jit(solution)/shard_map/ppermute | solution.py:20
  24.1 5.6 %collective-permute-start.9 = (bf16[64,768]{1,0:T(8,128)(2,1)S(1)}, bf16[64,768]{1,0:T(8,128)(2,1)S(1)}, u32[]{:S(2)}, u32[]{:S(2)}) collective-permute-start(bf16[64,768]{1,0:T(8,128)(2,1)S(1)} %get-tuple-element.48), channel_id=1, source_target_pairs={{0,16},{8,24},{16,0},{24,8},{1,17},{9,25},{17,1},{25,9},{2,18},{10... | collective-permute-start | bytes 294920 | tf_op jit(solution)/shard_map/ppermute | solution.py:20

commit v6 on v5

--- a/solution.py
+++ b/solution.py
@@ -11,7 +11,7 @@
 BF16 = jnp.bfloat16
 F32 = jnp.float32
 LANES = 128
-SUBLANES = 8
+PACKED = 16
 ROWS = 256
 MIB = 1024 * 1024
 
@@ -48,22 +48,25 @@
 
 def pack_kernel(
     classifier_hbm, valid_hbm, short_hbm, live_hbm, pos_hbm, neg_hbm, rows_ref, column_ref, index_ref,
-    classifier_ref, valid_ref, short_ref, live_ref, pos_ref, sem, *, scale
+    classifier_ref, valid_ref, short_ref, live_ref, pos_ref, neg_ref, sem, *, scale
 ):
-    slots, negatives, docs = neg_hbm.shape
+    slots, negatives, docs = neg_ref.shape
     fetch(
-        (classifier_hbm, valid_hbm, short_hbm, live_hbm, pos_hbm)
-        + tuple(neg_hbm.at[s] for s in range(slots)),
-        (classifier_ref, valid_ref, short_ref, live_ref, pos_ref)
-        + tuple(index_ref.at[pl.ds(s * negatives, negatives)] for s in range(slots)),
+        (classifier_hbm, valid_hbm, short_hbm, live_hbm, pos_hbm, neg_hbm),
+        (classifier_ref, valid_ref, short_ref, live_ref, pos_ref, neg_ref),
         sem,
     )
     column = flag_column(valid_ref[...])
     rows_ref[...] = (classifier_ref[...] * column).astype(BF16)
     column_ref[...] = jnp.broadcast_to(column * scale, column_ref.shape)
-    index_ref[slots * negatives : slots * (negatives + 2)] = jnp.concatenate(
-        [pos_ref[...], jnp.where(live_ref[...] > 0, short_ref[...], -1)], 0
-    )
+    index_ref[...] = jnp.concatenate(
+        [
+            neg_ref[...].reshape(slots * negatives, docs),
+            pos_ref[...],
+            jnp.where(live_ref[...] > 0, short_ref[...], -1),
+        ],
+        0,
+    ).astype(F32).astype(BF16)
 
 
 def turn_kernel(emb_hbm, other_ref, own_ref, own_turned_ref, other_turned_ref, sem):
@@ -78,27 +81,31 @@
     me = lax.axis_index("lab")
     docs = index_own_ref.shape[1]
     negatives = index_own_ref.shape[0] // slots - 2
-    groups = panel // SUBLANES
-    shape = (groups, SUBLANES, LANES)
-    label = SUBLANES * lax.broadcasted_iota(jnp.int32, shape, 0) + lax.broadcasted_iota(jnp.int32, shape, 1)
+    shape = (panel // PACKED, PACKED, LANES)
+    label = PACKED * lax.broadcasted_iota(jnp.int32, shape, 0) + lax.broadcasted_iota(jnp.int32, shape, 1)
+    label = label.astype(F32).astype(BF16)
+    one, zero = jnp.ones((), BF16), jnp.zeros((), BF16)
 
     def fill(index_ref, out_ref, lanes):
+        index = index_ref[:, lanes].astype(F32)
+
         def row(at):
-            return jnp.broadcast_to(index_ref[at : at + 1, lanes], (SUBLANES, LANES))
+            return jnp.broadcast_to(index[at : at + 1], (PACKED, LANES))
 
         values, relative = [], []
         for s in range(slots):
-            count = jnp.zeros(shape, F32)
+            count = jnp.zeros(shape, BF16)
             for k in range(negatives):
-                count = count + jnp.where(row(s * negatives + k)[None] == label, 1.0, 0.0)
-            hot = row(slots * negatives + s)[None] == label
-            values.append(jnp.where(hot, -1.0 - count, count))
-            relative.append(row(slots * (negatives + 1) + s) ^ me)
+                count = count + jnp.where(row(s * negatives + k).astype(BF16)[None] == label, one, zero)
+            hot = row(slots * negatives + s).astype(BF16)[None] == label
+            values.append(jnp.where(hot, -one - count, count))
+            relative.append(row(slots * (negatives + 1) + s).astype(jnp.int32) ^ me)
         for j in range(out_ref.shape[0] // panel):
-            block = jnp.zeros(shape, F32)
+            block = jnp.zeros(shape, BF16)
             for s in range(slots):
-                block = jnp.where((relative[s] == 2 * j)[None], values[s], block)
-            out_ref[pl.ds(j * panel, panel), lanes] = block.reshape(panel, LANES).astype(BF16)
+                chosen = jnp.where(relative[s] == 2 * j, 1.0, 0.0).astype(BF16)
+                block = block + chosen[None] * values[s]
+            out_ref[pl.ds(j * panel, panel), lanes] = block.reshape(panel, LANES)
 
     def chunk(i, carry):
         lanes = pl.ds(pl.multiple_of(i * LANES, LANES), LANES)
@@ -205,13 +212,13 @@
         out_shape=[
             jax.ShapeDtypeStruct((panel, width), BF16),
             jax.ShapeDtypeStruct((panel, LANES), F32),
-            jax.ShapeDtypeStruct((height, docs), jnp.int32),
+            jax.ShapeDtypeStruct((height, docs), BF16),
         ],
         in_specs=hbm(6),
         out_specs=vmem(3),
         scratch_shapes=[pltpu.VMEM((panel, width), F32), pltpu.VMEM((1, panel), jnp.int32)]
         + [pltpu.VMEM((slots, docs), jnp.int32)] * 3
-        + [pltpu.SemaphoreType.DMA((5 + slots,))],
+        + [pltpu.VMEM((slots, negatives, docs), jnp.int32), pltpu.SemaphoreType.DMA((6,))],
         compiler_params=params(panel * width * 6, height * docs * 4),
         cost_estimate=cost(panel * width, panel * width * 6 + height * docs * 4),
         name="pack",

time: 30.7 us -> 30.5 us (level)
  Pallas kernels: 8.09 us -> 7.58 us
  starting transfers between devices: 13.7 us -> 14.1 us
    pallas_call x1, Pallas kernels: 1.35 us -> 0.82 us  [shards(): pl.pallas_call(functools.partial(targets_kernel, panel=panel, slots=slots...]
    ppermute x12, starting transfers between devices: 13.7 us -> 14.1 us  [flip(): lax.ppermute(value, axis, [(i, i ^ mask) for i in range(lax.axis_size(axi...]
  transfers between devices with their start and end apart: 12 -> 12, of which waited for: 4 -> 5; matrix products, arithmetic and copies ran while one was open for 0% -> 0% of each run, Pallas kernels for 24% -> 23%
where the time goes in v6:
time: 30.5 us; the launch traced here: 30.3 us
  starting transfers between devices  14.1 us (46%)
  waiting for transfers between devices  7.76 us (25%)
  Pallas kernels  7.58 us (25%)
  between operations  0.72 us (2%)
    ppermute x12, starting transfers between devices, flip(): lax.ppermute(value, axis, [(i, i ^ mask) for i in range(lax.axis_size(axi...  14.1 us
    ppermute x12, waiting for transfers between devices, flip(): lax.ppermute(value, axis, [(i, i ^ mask) for i in range(lax.axis_size(axi...  7.76 us
    pallas_call x1, Pallas kernels, shards(): pl.pallas_call(emb_kernel, out_shape=jax.ShapeDtypeStruct((docs, width),...  1.74 us
    pallas_call x2, Pallas kernels, score(): pl.pallas_call(functools.partial(score_kernel, which=which, after=len(aft...  1.65 us
    pallas_call x1, Pallas kernels, shards(): pl.pallas_call(turn_kernel, out_shape=[jax.ShapeDtypeStruct((docs, width)...  1.41 us
    pallas_call x1, Pallas kernels, shards(): pl.pallas_call(functools.partial(pack_kernel, scale=1.0 / math.sqrt(docs...  1.15 us
    pallas_call x1, Pallas kernels, shards(): pl.pallas_call(functools.partial(targets_kernel, panel=panel, slots=slots...  0.82 us
    pallas_call x1, Pallas kernels, shards(): pl.pallas_call(finish_kernel, out_shape=jax.ShapeDtypeStruct((panel, widt...  0.76 us
  transfers between devices with their start and end apart: 12, of which 5 were waited for; matrix products, arithmetic and copies ran while one was open for 0% of the time, Pallas kernels for 23%

profile of v6, /device:TPU:0, one launch (start us, length us, event | category | flops | bytes accessed | tf_op | source)
XLA Modules:
  0.0 30.3 jit_solution(16293208511906719712)
XLA Ops:
  0.6 0.5 %collective-permute-start.1 = (bf16[512,768]{1,0:T(8,128)(2,1)}, bf16[512,768]{1,0:T(8,128)(2,1)S(1)}, u32[]{:S(2)}, u32[]{:S(2)}) collective-permute-start(bf16[512,768]{1,0:T(8,128)(2,1)} %emb_hbm.1), channel_id=1, source_target_pairs={{0,1},{1,0},{2,3},{3,2},{4,5},{5,4},{6,7},{7,6},{8,9},{9,8},{10,11... | collective-permute-start | bytes 2359304 | tf_op jit(solution)/shard_map/ppermute | solution.py:20
  1.1 1.1 %pack.1 = (bf16[64,768]{1,0:T(8,128)(2,1)S(1)}, f32[64,128]{1,0:T(8,128)S(1)}, bf16[40,512]{1,0:T(8,128)(2,1)S(1)}) custom-call(f32[64,768]{1,0:T(8,128)} %classifier_hbm.1, s32[1,64]{1,0:T(1,128)} %bitcast.9, s32[4,512]{1,0:T(4,128)} %bitcast.6, s32[4,512]{1,0:T(4,128)} %bitcast.7, s32[4,512]{1,0:T(4,128)} %bitcast.8, s32[4,8,512]{2,1,0:T(8,128)} %bitcast.5), custom_call_target="tpu_custom_call" | custom-call | flops 49152 | bytes 376832 | tf_op jit(solution)/shard_map/pack/pallas_call | solution.py:210
  2.3 3.5 %collective-permute-start = (bf16[64,768]{1,0:T(8,128)(2,1)S(1)}, bf16[64,768]{1,0:T(8,128)(2,1)S(1)}, u32[]{:S(2)}, u32[]{:S(2)}) collective-permute-start(bf16[64,768]{1,0:T(8,128)(2,1)S(1)} %get-tuple-element.25.refs_1_), channel_id=1, source_target_pairs={{0,6},{1,7},{2,4},{3,5},{4,2},{5,3},{6,0},{7,1},{8,14},{9,15},{10,... | collective-permute-start | bytes 294920 | tf_op jit(solution)/shard_map/ppermute | solution.py:20
  5.8 0.2 collective-permute-start.2
  6.0 0.5 %collective-permute-start.5 = (bf16[64,768]{1,0:T(8,128)(2,1)S(1)}, bf16[64,768]{1,0:T(8,128)(2,1)S(1)}, u32[]{:S(2)}, u32[]{:S(2)}) collective-permute-start(bf16[64,768]{1,0:T(8,128)(2,1)S(1)} %get-tuple-element.25.refs_1_), channel_id=1, source_target_pairs={{0,4},{1,5},{2,6},{3,7},{4,0},{5,1},{6,2},{7,3},{8,12},{9,13},{10,... | collective-permute-start | bytes 294920 | tf_op jit(solution)/shard_map/ppermute | solution.py:20
  6.5 0.4 %collective-permute-start.4 = (bf16[64,768]{1,0:T(8,128)(2,1)S(1)}, bf16[64,768]{1,0:T(8,128)(2,1)S(1)}, u32[]{:S(2)}, u32[]{:S(2)}) collective-permute-start(bf16[64,768]{1,0:T(8,128)(2,1)S(1)} %get-tuple-element.25.refs_1_), channel_id=1, source_target_pairs={{0,2},{1,3},{2,0},{3,1},{4,6},{5,7},{6,4},{7,5},{8,10},{9,11},{10,... | collective-permute-start | bytes 294920 | tf_op jit(solution)/shard_map/ppermute | solution.py:20
  7.0 0.0 collective-permute-done.1.other_ref.refs_3_
  7.0 1.4 %turn.1 = (bf16[512,768]{1,0:T(8,128)(2,1)S(1)}, bf16[768,512]{1,0:T(8,128)(2,1)S(1)}, bf16[768,512]{1,0:T(8,128)(2,1)S(1)}) custom-call(bf16[512,768]{1,0:T(8,128)(2,1)} %emb_hbm.1, bf16[512,768]{1,0:T(8,128)(2,1)S(1)} %collective-permute-done.1.other_ref.refs_3_), custom_call_target="tpu_custom_call" | custom-call | flops 393216 | bytes 3932160 | tf_op jit(solution)/shard_map/turn/pallas_call | solution.py:238
  8.4 0.0 collective-permute-done.2.index_other_ref
  8.4 0.8 %targets.1 = (bf16[256,512]{1,0:T(8,128)(2,1)S(1)}, bf16[256,512]{1,0:T(8,128)(2,1)S(1)}) custom-call(bf16[40,512]{1,0:T(8,128)(2,1)S(1)} %get-tuple-element.29.index_own_ref, bf16[40,512]{1,0:T(8,128)(2,1)S(1)} %collective-permute-done.2.index_other_ref, bf16[768,512]{1,0:T(8,128)(2,1)S(1)} %get-tuple-element.28.after_ref.refs_5_), custom_call_target="tpu_custom_call" | custom-call | flops 10485760 | bytes 688128 | tf_op jit(solution)/shard_map/targets/pallas_call | solution.py:249
  9.2 0.1 collective-permute-done.refs_0_
  9.3 0.8 %score.2 = (bf16[64,768]{1,0:T(8,128)(2,1)S(1)}, f32[64,768]{1,0:T(8,128)S(1)}, bf16[64,512]{1,0:T(8,128)(2,1)S(1)}, bf16[64,512]{1,0:T(8,128)(2,1)S(1)}, bf16[6...) custom-call(bf16[64,768]{1,0:T(8,128)(2,1)S(1)} %collective-permute-done.refs_0_, ...), custom_call_target="tpu_custom_call" | custom-call | flops 402653184 | bytes 4456448 | tf_op jit(solution)/shard_map/score/pallas_call | solution.py:264
  10.2 3.1 %collective-permute-start.3 = (bf16[80,768]{1,0:T(8,128)(2,1)S(1)}, bf16[80,768]{1,0:T(8,128)(2,1)S(1)}, u32[]{:S(2)}, u32[]{:S(2)}) collective-permute-start(bf16[80,768]{1,0:T(8,128)(2,1)S(1)} %pad_maximum_fusion), channel_id=1, source_target_pairs={{0,6},{1,7},{2,4},{3,5},{4,2},{5,3},{6,0},{7,1},{8,14},{9,15},{10,... | collective-permute-start | bytes 368648 | tf_op jit(solution)/shard_map/ppermute | solution.py:20
  13.3 0.0 collective-permute-done.5.refs_1_.refs_3_
  13.3 0.0 collective-permute-done.4.refs_0_.refs_2_
  13.3 0.8 %score.3 = (bf16[64,768]{1,0:T(8,128)(2,1)S(1)}, bf16[64,768]{1,0:T(8,128)(2,1)S(1)}, bf16[64,512]{1,0:T(8,128)(2,1)S(1)}, bf16[64,512]{1,0:T(8,128)(2,1)S(1)}, ...) custom-call(bf16[64,768]{1,0:T(8,128)(2,1)S(1)} %collective-permute-done.4.refs_0_.refs_2_, ...), custom_call_target="tpu_custom_call" | custom-call | flops 402653184 | bytes 4456448 | tf_op jit(solution)/shard_map/score/pallas_call | solution.py:264
  14.1 0.4 %collective-permute-start.6 = (bf16[64,768]{1,0:T(8,128)(2,1)S(1)}, bf16[64,768]{1,0:T(8,128)(2,1)S(1)}, u32[]{:S(2)}, u32[]{:S(2)}) collective-permute-start(bf16[64,768]{1,0:T(8,128)(2,1)S(1)} %get-tuple-element.34), channel_id=1, source_target_pairs={{0,4},{1,5},{2,6},{3,7},{4,0},{5,1},{6,2},{7,3},{8,12},{9,13},{10,... | collective-permute-start | bytes 294920 | tf_op jit(solution)/shard_map/ppermute | solution.py:20
  14.5 0.4 %collective-permute-start.7 = (bf16[64,768]{1,0:T(8,128)(2,1)S(1)}, bf16[64,768]{1,0:T(8,128)(2,1)S(1)}, u32[]{:S(2)}, u32[]{:S(2)}) collective-permute-start(bf16[64,768]{1,0:T(8,128)(2,1)S(1)} %get-tuple-element.35), channel_id=1, source_target_pairs={{0,2},{1,3},{2,0},{3,1},{4,6},{5,7},{6,4},{7,5},{8,10},{9,11},{10,... | collective-permute-start | bytes 294920 | tf_op jit(solution)/shard_map/ppermute | solution.py:20
  14.9 4.0 %collective-permute-done.6 = bf16[64,768]{1,0:T(8,128)(2,1)S(1)} collective-permute-done((bf16[64,768]{1,0:T(8,128)(2,1)S(1)}, bf16[64,768]{1,0:T(8,128)(2,1)S(1)}, u32[]{:S(2)}, u32[]{:S(2)}) %collective-permute-start.6) | collective-permute-done | bytes 98336 | tf_op jit(solution)/shard_map/ppermute | solution.py:20
  18.8 0.3 %collective-permute-done.7 = bf16[64,768]{1,0:T(8,128)(2,1)S(1)} collective-permute-done((bf16[64,768]{1,0:T(8,128)(2,1)S(1)}, bf16[64,768]{1,0:T(8,128)(2,1)S(1)}, u32[]{:S(2)}, u32[]{:S(2)}) %collective-permute-start.7) | collective-permute-done | bytes 98336 | tf_op jit(solution)/shard_map/ppermute | solution.py:20
  19.1 0.0 collective-permute-done.3
  19.2 1.6 %collective-permute-start.8 = (bf16[64,768]{1,0:T(8,128)(2,1)S(1)}, bf16[64,768]{1,0:T(8,128)(2,1)S(1)}, u32[]{:S(2)}, u32[]{:S(2)}) collective-permute-start(bf16[64,768]{1,0:T(8,128)(2,1)S(1)} %fusion), channel_id=1, source_target_pairs={{0,8},{8,0},{16,24},{24,16},{1,9},{9,1},{17,25},{25,17},{2,10},{10... | collective-permute-start | bytes 294920 | tf_op jit(solution)/shard_map/ppermute | solution.py:20
  20.8 0.1 join.1
  20.9 0.1 collective-permute-start.11
  21.0 0.5 %collective-permute-start.10 = (bf16[256,512]{1,0:T(8,128)(2,1)S(1)}, bf16[256,512]{1,0:T(8,128)(2,1)S(1)}, u32[]{:S(2)}, u32[]{:S(2)}) collective-permute-start(bf16[256,512]{1,0:T(8,128)(2,1)S(1)} %get-tuple-element.46), channel_id=1, source_target_pairs={{0,1},{1,0},{2,3},{3,2},{4,5},{5,4},{6,7},{7,6},{8,9},{9,8},{10,11... | collective-permute-start | bytes 786440 | tf_op jit(solution)/shard_map/ppermute | solution.py:20
  21.5 2.4 %collective-permute-done.8 = bf16[64,768]{1,0:T(8,128)(2,1)S(1)} collective-permute-done((bf16[64,768]{1,0:T(8,128)(2,1)S(1)}, bf16[64,768]{1,0:T(8,128)(2,1)S(1)}, u32[]{:S(2)}, u32[]{:S(2)}) %collective-permute-start.8) | collective-permute-done | bytes 98336 | tf_op jit(solution)/shard_map/ppermute | solution.py:20
  23.9 0.1 fusion.1
  23.9 2.9 %collective-permute-start.9 = (bf16[64,768]{1,0:T(8,128)(2,1)S(1)}, bf16[64,768]{1,0:T(8,128)(2,1)S(1)}, u32[]{:S(2)}, u32[]{:S(2)}) collective-permute-start(bf16[64,768]{1,0:T(8,128)(2,1)S(1)} %get-tuple-element.48), channel_id=1, source_target_pairs={{0,16},{8,24},{16,0},{24,8},{1,17},{9,25},{17,1},{25,9},{2,18},{10... | collective-permute-start | bytes 294920 | tf_op jit(solution)/shard_map/ppermute | solution.py:20
  26.8 0.0 collective-permute-done.10.d_other_ref
  26.8 0.0 collective-permute-done.11.c_other_ref
  26.8 1.7 %emb_grad.1.after_hbm = f32[512,768]{1,0:T(8,128)} custom-call(bf16[256,512]{1,0:T(8,128)(2,1)S(1)} %get-tuple-element.45.d_own_ref, bf16[256,512]{1,0:T(8,128)(2,1)S(1)} %collective-permute-done.10.d_other_ref, bf16[256,768]{1,0:T(8,128)(2,1)S(1)} %get-tuple-element.47.c_own_ref, bf16[256,768]{1,0:T(8,128)(2,1)S(1)} %collective-permute-done.11.c_other_ref, ...), custom_call_target="tpu_custom_call" | custom-call | flops 402653184 | bytes 2883584 | tf_op jit(solution)/shard_map/emb_grad/pallas_call | solution.py:322
  28.5 1.0 %collective-permute-done.9.received_ref = bf16[64,768]{1,0:T(8,128)(2,1)S(1)} collective-permute-done((bf16[64,768]{1,0:T(8,128)(2,1)S(1)}, bf16[64,768]{1,0:T(8,128)(2,1)S(1)}, u32[]{:S(2)}, u32[]{:S(2)}) %collective-permute-start.9) | collective-permute-done | bytes 98336 | tf_op jit(solution)/shard_map/ppermute | solution.py:20
  29.5 0.8 %finish.1 = f32[64,768]{1,0:T(8,128)} custom-call(f32[64,768]{1,0:T(8,128)S(1)} %get-tuple-element.49.after_ref.grad_ref, bf16[64,768]{1,0:T(8,128)(2,1)S(1)} %collective-permute-done.9.received_ref, f32[64,128]{1,0:T(8,128)S(1)} %get-tuple-element.36.column_ref, f32[512,768]{1,0:T(8,128)} %emb_grad.1.after_hbm), custom_call_target="tpu_custom_call" | custom-call | flops 49152 | bytes 491520 | tf_op jit(solution)/shard_map/finish/pallas_call | solution.py:332
  (3 shorter events, 0.1 us)
Async XLA Ops:
  0.6 6.3 %collective-permute-start.1 = (bf16[512,768]{1,0:T(8,128)(2,1)}, bf16[512,768]{1,0:T(8,128)(2,1)S(1)}, u32[]{:S(2)}, u32[]{:S(2)}) collective-permute-start(bf16[512,768]{1,0:T(8,128)(2,1)} %emb_hbm.1), channel_id=1, source_target_pairs={{0,1},{1,0},{2,3},{3,2},{4,5},{5,4},{6,7},{7,6},{8,9},{9,8},{10,11... | collective-permute-start | bytes 2359304 | tf_op jit(solution)/shard_map/ppermute | solution.py:20
  2.3 7.0 %collective-permute-start = (bf16[64,768]{1,0:T(8,128)(2,1)S(1)}, bf16[64,768]{1,0:T(8,128)(2,1)S(1)}, u32[]{:S(2)}, u32[]{:S(2)}) collective-permute-start(bf16[64,768]{1,0:T(8,128)(2,1)S(1)} %get-tuple-element.25.refs_1_), channel_id=1, source_target_pairs={{0,6},{1,7},{2,4},{3,5},{4,2},{5,3},{6,0},{7,1},{8,14},{9,15},{10,... | collective-permute-start | bytes 294920 | tf_op jit(solution)/shard_map/ppermute | solution.py:20
  5.8 2.6 %collective-permute-start.2 = (bf16[40,512]{1,0:T(8,128)(2,1)S(1)}, bf16[40,512]{1,0:T(8,128)(2,1)S(1)}, u32[]{:S(2)}, u32[]{:S(2)}) collective-permute-start(bf16[40,512]{1,0:T(8,128)(2,1)S(1)} %get-tuple-element.29.index_own_ref), channel_id=1, source_target_pairs={{0,1},{1,0},{2,3},{3,2},{4,5},{5,4},{6,7},{7,6},{8,9},{9,8},{10,11... | collective-permute-start | bytes 122888 | tf_op jit(solution)/shard_map/ppermute | solution.py:20
  6.0 7.3 %collective-permute-start.5 = (bf16[64,768]{1,0:T(8,128)(2,1)S(1)}, bf16[64,768]{1,0:T(8,128)(2,1)S(1)}, u32[]{:S(2)}, u32[]{:S(2)}) collective-permute-start(bf16[64,768]{1,0:T(8,128)(2,1)S(1)} %get-tuple-element.25.refs_1_), channel_id=1, source_target_pairs={{0,4},{1,5},{2,6},{3,7},{4,0},{5,1},{6,2},{7,3},{8,12},{9,13},{10,... | collective-permute-start | bytes 294920 | tf_op jit(solution)/shard_map/ppermute | solution.py:20
  6.5 6.8 %collective-permute-start.4 = (bf16[64,768]{1,0:T(8,128)(2,1)S(1)}, bf16[64,768]{1,0:T(8,128)(2,1)S(1)}, u32[]{:S(2)}, u32[]{:S(2)}) collective-permute-start(bf16[64,768]{1,0:T(8,128)(2,1)S(1)} %get-tuple-element.25.refs_1_), channel_id=1, source_target_pairs={{0,2},{1,3},{2,0},{3,1},{4,6},{5,7},{6,4},{7,5},{8,10},{9,11},{10,... | collective-permute-start | bytes 294920 | tf_op jit(solution)/shard_map/ppermute | solution.py:20
  10.2 9.0 %collective-permute-start.3 = (bf16[80,768]{1,0:T(8,128)(2,1)S(1)}, bf16[80,768]{1,0:T(8,128)(2,1)S(1)}, u32[]{:S(2)}, u32[]{:S(2)}) collective-permute-start(bf16[80,768]{1,0:T(8,128)(2,1)S(1)} %pad_maximum_fusion), channel_id=1, source_target_pairs={{0,6},{1,7},{2,4},{3,5},{4,2},{5,3},{6,0},{7,1},{8,14},{9,15},{10,... | collective-permute-start | bytes 368648 | tf_op jit(solution)/shard_map/ppermute | solution.py:20
  14.1 4.7 %collective-permute-start.6 = (bf16[64,768]{1,0:T(8,128)(2,1)S(1)}, bf16[64,768]{1,0:T(8,128)(2,1)S(1)}, u32[]{:S(2)}, u32[]{:S(2)}) collective-permute-start(bf16[64,768]{1,0:T(8,128)(2,1)S(1)} %get-tuple-element.34), channel_id=1, source_target_pairs={{0,4},{1,5},{2,6},{3,7},{4,0},{5,1},{6,2},{7,3},{8,12},{9,13},{10,... | collective-permute-start | bytes 294920 | tf_op jit(solution)/shard_map/ppermute | solution.py:20
  14.5 4.6 %collective-permute-start.7 = (bf16[64,768]{1,0:T(8,128)(2,1)S(1)}, bf16[64,768]{1,0:T(8,128)(2,1)S(1)}, u32[]{:S(2)}, u32[]{:S(2)}) collective-permute-start(bf16[64,768]{1,0:T(8,128)(2,1)S(1)} %get-tuple-element.35), channel_id=1, source_target_pairs={{0,2},{1,3},{2,0},{3,1},{4,6},{5,7},{6,4},{7,5},{8,10},{9,11},{10,... | collective-permute-start | bytes 294920 | tf_op jit(solution)/shard_map/ppermute | solution.py:20
  19.2 4.7 %collective-permute-start.8 = (bf16[64,768]{1,0:T(8,128)(2,1)S(1)}, bf16[64,768]{1,0:T(8,128)(2,1)S(1)}, u32[]{:S(2)}, u32[]{:S(2)}) collective-permute-start(bf16[64,768]{1,0:T(8,128)(2,1)S(1)} %fusion), channel_id=1, source_target_pairs={{0,8},{8,0},{16,24},{24,16},{1,9},{9,1},{17,25},{25,17},{2,10},{10... | collective-permute-start | bytes 294920 | tf_op jit(solution)/shard_map/ppermute | solution.py:20
  20.9 5.9 %collective-permute-start.11 = (bf16[256,768]{1,0:T(8,128)(2,1)S(1)}, bf16[256,768]{1,0:T(8,128)(2,1)S(1)}, u32[]{:S(2)}, u32[]{:S(2)}) collective-permute-start(bf16[256,768]{1,0:T(8,128)(2,1)S(1)} %get-tuple-element.47.c_own_ref), channel_id=1, source_target_pairs={{0,1},{1,0},{2,3},{3,2},{4,5},{5,4},{6,7},{7,6},{8,9},{9,8},{10,11... | collective-permute-start | bytes 1179656 | tf_op jit(solution)/shard_map/ppermute | solution.py:20
  21.0 5.8 %collective-permute-start.10 = (bf16[256,512]{1,0:T(8,128)(2,1)S(1)}, bf16[256,512]{1,0:T(8,128)(2,1)S(1)}, u32[]{:S(2)}, u32[]{:S(2)}) collective-permute-start(bf16[256,512]{1,0:T(8,128)(2,1)S(1)} %get-tuple-element.46), channel_id=1, source_target_pairs={{0,1},{1,0},{2,3},{3,2},{4,5},{5,4},{6,7},{7,6},{8,9},{9,8},{10,11... | collective-permute-start | bytes 786440 | tf_op jit(solution)/shard_map/ppermute | solution.py:20
  23.9 5.6 %collective-permute-start.9 = (bf16[64,768]{1,0:T(8,128)(2,1)S(1)}, bf16[64,768]{1,0:T(8,128)(2,1)S(1)}, u32[]{:S(2)}, u32[]{:S(2)}) collective-permute-start(bf16[64,768]{1,0:T(8,128)(2,1)S(1)} %get-tuple-element.48), channel_id=1, source_target_pairs={{0,16},{8,24},{16,0},{24,8},{1,17},{9,25},{17,1},{25,9},{2,18},{10... | collective-permute-start | bytes 294920 | tf_op jit(solution)/shard_map/ppermute | solution.py:20

commit v7 on v6

--- a/solution.py
+++ b/solution.py
@@ -306,7 +306,7 @@
         for i in reversed(range(len(masks))):
             value = grads[i + 1]
             if i == 2:
-                value = jnp.concatenate([value, value[:16]], 0)
+                value = jnp.concatenate([value, value[:1]], 0)
             received.append(flip(value, "lab", masks[i])[: grads[i + 1].shape[0]])
         grad = grads[0]
         for r in received:

time: 30.5 us -> 30.5 us (level)
  no operation moved by 1% of the time
where the time goes in v7:
time: 30.5 us; the launch traced here: 30.3 us
  starting transfers between devices  14.2 us (47%)
  waiting for transfers between devices  7.64 us (25%)
  Pallas kernels  7.59 us (25%)
  between operations  0.72 us (2%)
    ppermute x12, starting transfers between devices, flip(): lax.ppermute(value, axis, [(i, i ^ mask) for i in range(lax.axis_size(axi...  14.2 us
    ppermute x12, waiting for transfers between devices, flip(): lax.ppermute(value, axis, [(i, i ^ mask) for i in range(lax.axis_size(axi...  7.64 us
    pallas_call x1, Pallas kernels, shards(): pl.pallas_call(emb_kernel, out_shape=jax.ShapeDtypeStruct((docs, width),...  1.75 us
    pallas_call x2, Pallas kernels, score(): pl.pallas_call(functools.partial(score_kernel, which=which, after=len(aft...  1.65 us
    pallas_call x1, Pallas kernels, shards(): pl.pallas_call(turn_kernel, out_shape=[jax.ShapeDtypeStruct((docs, width)...  1.41 us
    pallas_call x1, Pallas kernels, shards(): pl.pallas_call(functools.partial(pack_kernel, scale=1.0 / math.sqrt(docs...  1.15 us
    pallas_call x1, Pallas kernels, shards(): pl.pallas_call(functools.partial(targets_kernel, panel=panel, slots=slots...  0.82 us
    pallas_call x1, Pallas kernels, shards(): pl.pallas_call(finish_kernel, out_shape=jax.ShapeDtypeStruct((panel, widt...  0.76 us
  transfers between devices with their start and end apart: 12, of which 5 were waited for; matrix products, arithmetic and copies ran while one was open for 0% of the time, Pallas kernels for 23%

profile of v7, /device:TPU:0, one launch (start us, length us, event | category | flops | bytes accessed | tf_op | source)
XLA Modules:
  0.0 30.3 jit_solution(8505494172073236092)
XLA Ops:
  0.6 0.5 %collective-permute-start.1 = (bf16[512,768]{1,0:T(8,128)(2,1)}, bf16[512,768]{1,0:T(8,128)(2,1)S(1)}, u32[]{:S(2)}, u32[]{:S(2)}) collective-permute-start(bf16[512,768]{1,0:T(8,128)(2,1)} %emb_hbm.1), channel_id=1, source_target_pairs={{0,1},{1,0},{2,3},{3,2},{4,5},{5,4},{6,7},{7,6},{8,9},{9,8},{10,11... | collective-permute-start | bytes 2359304 | tf_op jit(solution)/shard_map/ppermute | solution.py:20
  1.1 1.1 %pack.1 = (bf16[64,768]{1,0:T(8,128)(2,1)S(1)}, f32[64,128]{1,0:T(8,128)S(1)}, bf16[40,512]{1,0:T(8,128)(2,1)S(1)}) custom-call(f32[64,768]{1,0:T(8,128)} %classifier_hbm.1, s32[1,64]{1,0:T(1,128)} %bitcast.9, s32[4,512]{1,0:T(4,128)} %bitcast.6, s32[4,512]{1,0:T(4,128)} %bitcast.7, s32[4,512]{1,0:T(4,128)} %bitcast.8, s32[4,8,512]{2,1,0:T(8,128)} %bitcast.5), custom_call_target="tpu_custom_call" | custom-call | flops 49152 | bytes 376832 | tf_op jit(solution)/shard_map/pack/pallas_call | solution.py:210
  2.3 3.5 %collective-permute-start = (bf16[64,768]{1,0:T(8,128)(2,1)S(1)}, bf16[64,768]{1,0:T(8,128)(2,1)S(1)}, u32[]{:S(2)}, u32[]{:S(2)}) collective-permute-start(bf16[64,768]{1,0:T(8,128)(2,1)S(1)} %get-tuple-element.25.refs_1_), channel_id=1, source_target_pairs={{0,6},{1,7},{2,4},{3,5},{4,2},{5,3},{6,0},{7,1},{8,14},{9,15},{10,... | collective-permute-start | bytes 294920 | tf_op jit(solution)/shard_map/ppermute | solution.py:20
  5.8 0.2 collective-permute-start.2
  6.0 0.5 %collective-permute-start.5 = (bf16[64,768]{1,0:T(8,128)(2,1)S(1)}, bf16[64,768]{1,0:T(8,128)(2,1)S(1)}, u32[]{:S(2)}, u32[]{:S(2)}) collective-permute-start(bf16[64,768]{1,0:T(8,128)(2,1)S(1)} %get-tuple-element.25.refs_1_), channel_id=1, source_target_pairs={{0,4},{1,5},{2,6},{3,7},{4,0},{5,1},{6,2},{7,3},{8,12},{9,13},{10,... | collective-permute-start | bytes 294920 | tf_op jit(solution)/shard_map/ppermute | solution.py:20
  6.5 0.4 %collective-permute-start.4 = (bf16[64,768]{1,0:T(8,128)(2,1)S(1)}, bf16[64,768]{1,0:T(8,128)(2,1)S(1)}, u32[]{:S(2)}, u32[]{:S(2)}) collective-permute-start(bf16[64,768]{1,0:T(8,128)(2,1)S(1)} %get-tuple-element.25.refs_1_), channel_id=1, source_target_pairs={{0,2},{1,3},{2,0},{3,1},{4,6},{5,7},{6,4},{7,5},{8,10},{9,11},{10,... | collective-permute-start | bytes 294920 | tf_op jit(solution)/shard_map/ppermute | solution.py:20
  7.0 0.0 collective-permute-done.1.other_ref.refs_3_
  7.0 1.4 %turn.1 = (bf16[512,768]{1,0:T(8,128)(2,1)S(1)}, bf16[768,512]{1,0:T(8,128)(2,1)S(1)}, bf16[768,512]{1,0:T(8,128)(2,1)S(1)}) custom-call(bf16[512,768]{1,0:T(8,128)(2,1)} %emb_hbm.1, bf16[512,768]{1,0:T(8,128)(2,1)S(1)} %collective-permute-done.1.other_ref.refs_3_), custom_call_target="tpu_custom_call" | custom-call | flops 393216 | bytes 3932160 | tf_op jit(solution)/shard_map/turn/pallas_call | solution.py:238
  8.4 0.0 collective-permute-done.2.index_other_ref
  8.4 0.8 %targets.1 = (bf16[256,512]{1,0:T(8,128)(2,1)S(1)}, bf16[256,512]{1,0:T(8,128)(2,1)S(1)}) custom-call(bf16[40,512]{1,0:T(8,128)(2,1)S(1)} %get-tuple-element.29.index_own_ref, bf16[40,512]{1,0:T(8,128)(2,1)S(1)} %collective-permute-done.2.index_other_ref, bf16[768,512]{1,0:T(8,128)(2,1)S(1)} %get-tuple-element.28.after_ref.refs_5_), custom_call_target="tpu_custom_call" | custom-call | flops 10485760 | bytes 688128 | tf_op jit(solution)/shard_map/targets/pallas_call | solution.py:249
  9.2 0.1 collective-permute-done.refs_0_
  9.3 0.8 %score.2 = (bf16[64,768]{1,0:T(8,128)(2,1)S(1)}, f32[64,768]{1,0:T(8,128)S(1)}, bf16[64,512]{1,0:T(8,128)(2,1)S(1)}, bf16[64,512]{1,0:T(8,128)(2,1)S(1)}, bf16[6...) custom-call(bf16[64,768]{1,0:T(8,128)(2,1)S(1)} %collective-permute-done.refs_0_, ...), custom_call_target="tpu_custom_call" | custom-call | flops 402653184 | bytes 4456448 | tf_op jit(solution)/shard_map/score/pallas_call | solution.py:264
  10.2 3.1 %collective-permute-start.3 = (bf16[65,768]{1,0:T(8,128)(2,1)S(1)}, bf16[65,768]{1,0:T(8,128)(2,1)S(1)}, u32[]{:S(2)}, u32[]{:S(2)}) collective-permute-start(bf16[65,768]{1,0:T(8,128)(2,1)S(1)} %pad_maximum_fusion), channel_id=1, source_target_pairs={{0,6},{1,7},{2,4},{3,5},{4,2},{5,3},{6,0},{7,1},{8,14},{9,15},{10,... | collective-permute-start | bytes 299528 | tf_op jit(solution)/shard_map/ppermute | solution.py:20
  13.3 0.0 collective-permute-done.5.refs_1_.refs_3_
  13.3 0.0 collective-permute-done.4.refs_0_.refs_2_
  13.3 0.8 %score.3 = (bf16[64,768]{1,0:T(8,128)(2,1)S(1)}, bf16[64,768]{1,0:T(8,128)(2,1)S(1)}, bf16[64,512]{1,0:T(8,128)(2,1)S(1)}, bf16[64,512]{1,0:T(8,128)(2,1)S(1)}, ...) custom-call(bf16[64,768]{1,0:T(8,128)(2,1)S(1)} %collective-permute-done.4.refs_0_.refs_2_, ...), custom_call_target="tpu_custom_call" | custom-call | flops 402653184 | bytes 4456448 | tf_op jit(solution)/shard_map/score/pallas_call | solution.py:264
  14.1 0.4 %collective-permute-start.6 = (bf16[64,768]{1,0:T(8,128)(2,1)S(1)}, bf16[64,768]{1,0:T(8,128)(2,1)S(1)}, u32[]{:S(2)}, u32[]{:S(2)}) collective-permute-start(bf16[64,768]{1,0:T(8,128)(2,1)S(1)} %get-tuple-element.34), channel_id=1, source_target_pairs={{0,4},{1,5},{2,6},{3,7},{4,0},{5,1},{6,2},{7,3},{8,12},{9,13},{10,... | collective-permute-start | bytes 294920 | tf_op jit(solution)/shard_map/ppermute | solution.py:20
  14.5 0.3 %collective-permute-start.7 = (bf16[64,768]{1,0:T(8,128)(2,1)S(1)}, bf16[64,768]{1,0:T(8,128)(2,1)S(1)}, u32[]{:S(2)}, u32[]{:S(2)}) collective-permute-start(bf16[64,768]{1,0:T(8,128)(2,1)S(1)} %get-tuple-element.35), channel_id=1, source_target_pairs={{0,2},{1,3},{2,0},{3,1},{4,6},{5,7},{6,4},{7,5},{8,10},{9,11},{10,... | collective-permute-start | bytes 294920 | tf_op jit(solution)/shard_map/ppermute | solution.py:20
  14.9 4.0 %collective-permute-done.6 = bf16[64,768]{1,0:T(8,128)(2,1)S(1)} collective-permute-done((bf16[64,768]{1,0:T(8,128)(2,1)S(1)}, bf16[64,768]{1,0:T(8,128)(2,1)S(1)}, u32[]{:S(2)}, u32[]{:S(2)}) %collective-permute-start.6) | collective-permute-done | bytes 98336 | tf_op jit(solution)/shard_map/ppermute | solution.py:20
  18.8 0.3 %collective-permute-done.7 = bf16[64,768]{1,0:T(8,128)(2,1)S(1)} collective-permute-done((bf16[64,768]{1,0:T(8,128)(2,1)S(1)}, bf16[64,768]{1,0:T(8,128)(2,1)S(1)}, u32[]{:S(2)}, u32[]{:S(2)}) %collective-permute-start.7) | collective-permute-done | bytes 98336 | tf_op jit(solution)/shard_map/ppermute | solution.py:20
  19.1 0.0 collective-permute-done.3
  19.2 1.6 %collective-permute-start.8 = (bf16[64,768]{1,0:T(8,128)(2,1)S(1)}, bf16[64,768]{1,0:T(8,128)(2,1)S(1)}, u32[]{:S(2)}, u32[]{:S(2)}) collective-permute-start(bf16[64,768]{1,0:T(8,128)(2,1)S(1)} %fusion), channel_id=1, source_target_pairs={{0,8},{8,0},{16,24},{24,16},{1,9},{9,1},{17,25},{25,17},{2,10},{10... | collective-permute-start | bytes 294920 | tf_op jit(solution)/shard_map/ppermute | solution.py:20
  20.8 0.1 join.1
  20.9 0.1 collective-permute-start.11
  21.0 0.5 %collective-permute-start.10 = (bf16[256,512]{1,0:T(8,128)(2,1)S(1)}, bf16[256,512]{1,0:T(8,128)(2,1)S(1)}, u32[]{:S(2)}, u32[]{:S(2)}) collective-permute-start(bf16[256,512]{1,0:T(8,128)(2,1)S(1)} %get-tuple-element.46), channel_id=1, source_target_pairs={{0,1},{1,0},{2,3},{3,2},{4,5},{5,4},{6,7},{7,6},{8,9},{9,8},{10,11... | collective-permute-start | bytes 786440 | tf_op jit(solution)/shard_map/ppermute | solution.py:20
  21.5 2.4 %collective-permute-done.8 = bf16[64,768]{1,0:T(8,128)(2,1)S(1)} collective-permute-done((bf16[64,768]{1,0:T(8,128)(2,1)S(1)}, bf16[64,768]{1,0:T(8,128)(2,1)S(1)}, u32[]{:S(2)}, u32[]{:S(2)}) %collective-permute-start.8) | collective-permute-done | bytes 98336 | tf_op jit(solution)/shard_map/ppermute | solution.py:20
  23.9 0.1 fusion.1
  23.9 3.0 %collective-permute-start.9 = (bf16[64,768]{1,0:T(8,128)(2,1)S(1)}, bf16[64,768]{1,0:T(8,128)(2,1)S(1)}, u32[]{:S(2)}, u32[]{:S(2)}) collective-permute-start(bf16[64,768]{1,0:T(8,128)(2,1)S(1)} %get-tuple-element.48), channel_id=1, source_target_pairs={{0,16},{8,24},{16,0},{24,8},{1,17},{9,25},{17,1},{25,9},{2,18},{10... | collective-permute-start | bytes 294920 | tf_op jit(solution)/shard_map/ppermute | solution.py:20
  26.9 0.0 collective-permute-done.10.d_other_ref
  26.9 0.0 collective-permute-done.11.c_other_ref
  26.9 1.7 %emb_grad.1.after_hbm = f32[512,768]{1,0:T(8,128)} custom-call(bf16[256,512]{1,0:T(8,128)(2,1)S(1)} %get-tuple-element.45.d_own_ref, bf16[256,512]{1,0:T(8,128)(2,1)S(1)} %collective-permute-done.10.d_other_ref, bf16[256,768]{1,0:T(8,128)(2,1)S(1)} %get-tuple-element.47.c_own_ref, bf16[256,768]{1,0:T(8,128)(2,1)S(1)} %collective-permute-done.11.c_other_ref, ...), custom_call_target="tpu_custom_call" | custom-call | flops 402653184 | bytes 2883584 | tf_op jit(solution)/shard_map/emb_grad/pallas_call | solution.py:322
  28.7 0.9 %collective-permute-done.9.received_ref = bf16[64,768]{1,0:T(8,128)(2,1)S(1)} collective-permute-done((bf16[64,768]{1,0:T(8,128)(2,1)S(1)}, bf16[64,768]{1,0:T(8,128)(2,1)S(1)}, u32[]{:S(2)}, u32[]{:S(2)}) %collective-permute-start.9) | collective-permute-done | bytes 98336 | tf_op jit(solution)/shard_map/ppermute | solution.py:20
  29.6 0.8 %finish.1 = f32[64,768]{1,0:T(8,128)} custom-call(f32[64,768]{1,0:T(8,128)S(1)} %get-tuple-element.49.after_ref.grad_ref, bf16[64,768]{1,0:T(8,128)(2,1)S(1)} %collective-permute-done.9.received_ref, f32[64,128]{1,0:T(8,128)S(1)} %get-tuple-element.36.column_ref, f32[512,768]{1,0:T(8,128)} %emb_grad.1.after_hbm), custom_call_target="tpu_custom_call" | custom-call | flops 49152 | bytes 491520 | tf_op jit(solution)/shard_map/finish/pallas_call | solution.py:332
  (3 shorter events, 0.1 us)
Async XLA Ops:
  0.6 6.3 %collective-permute-start.1 = (bf16[512,768]{1,0:T(8,128)(2,1)}, bf16[512,768]{1,0:T(8,128)(2,1)S(1)}, u32[]{:S(2)}, u32[]{:S(2)}) collective-permute-start(bf16[512,768]{1,0:T(8,128)(2,1)} %emb_hbm.1), channel_id=1, source_target_pairs={{0,1},{1,0},{2,3},{3,2},{4,5},{5,4},{6,7},{7,6},{8,9},{9,8},{10,11... | collective-permute-start | bytes 2359304 | tf_op jit(solution)/shard_map/ppermute | solution.py:20
  2.3 7.0 %collective-permute-start = (bf16[64,768]{1,0:T(8,128)(2,1)S(1)}, bf16[64,768]{1,0:T(8,128)(2,1)S(1)}, u32[]{:S(2)}, u32[]{:S(2)}) collective-permute-start(bf16[64,768]{1,0:T(8,128)(2,1)S(1)} %get-tuple-element.25.refs_1_), channel_id=1, source_target_pairs={{0,6},{1,7},{2,4},{3,5},{4,2},{5,3},{6,0},{7,1},{8,14},{9,15},{10,... | collective-permute-start | bytes 294920 | tf_op jit(solution)/shard_map/ppermute | solution.py:20
  5.8 2.6 %collective-permute-start.2 = (bf16[40,512]{1,0:T(8,128)(2,1)S(1)}, bf16[40,512]{1,0:T(8,128)(2,1)S(1)}, u32[]{:S(2)}, u32[]{:S(2)}) collective-permute-start(bf16[40,512]{1,0:T(8,128)(2,1)S(1)} %get-tuple-element.29.index_own_ref), channel_id=1, source_target_pairs={{0,1},{1,0},{2,3},{3,2},{4,5},{5,4},{6,7},{7,6},{8,9},{9,8},{10,11... | collective-permute-start | bytes 122888 | tf_op jit(solution)/shard_map/ppermute | solution.py:20
  6.0 7.3 %collective-permute-start.5 = (bf16[64,768]{1,0:T(8,128)(2,1)S(1)}, bf16[64,768]{1,0:T(8,128)(2,1)S(1)}, u32[]{:S(2)}, u32[]{:S(2)}) collective-permute-start(bf16[64,768]{1,0:T(8,128)(2,1)S(1)} %get-tuple-element.25.refs_1_), channel_id=1, source_target_pairs={{0,4},{1,5},{2,6},{3,7},{4,0},{5,1},{6,2},{7,3},{8,12},{9,13},{10,... | collective-permute-start | bytes 294920 | tf_op jit(solution)/shard_map/ppermute | solution.py:20
  6.5 6.8 %collective-permute-start.4 = (bf16[64,768]{1,0:T(8,128)(2,1)S(1)}, bf16[64,768]{1,0:T(8,128)(2,1)S(1)}, u32[]{:S(2)}, u32[]{:S(2)}) collective-permute-start(bf16[64,768]{1,0:T(8,128)(2,1)S(1)} %get-tuple-element.25.refs_1_), channel_id=1, source_target_pairs={{0,2},{1,3},{2,0},{3,1},{4,6},{5,7},{6,4},{7,5},{8,10},{9,11},{10,... | collective-permute-start | bytes 294920 | tf_op jit(solution)/shard_map/ppermute | solution.py:20
  10.2 9.0 %collective-permute-start.3 = (bf16[65,768]{1,0:T(8,128)(2,1)S(1)}, bf16[65,768]{1,0:T(8,128)(2,1)S(1)}, u32[]{:S(2)}, u32[]{:S(2)}) collective-permute-start(bf16[65,768]{1,0:T(8,128)(2,1)S(1)} %pad_maximum_fusion), channel_id=1, source_target_pairs={{0,6},{1,7},{2,4},{3,5},{4,2},{5,3},{6,0},{7,1},{8,14},{9,15},{10,... | collective-permute-start | bytes 299528 | tf_op jit(solution)/shard_map/ppermute | solution.py:20
  14.1 4.7 %collective-permute-start.6 = (bf16[64,768]{1,0:T(8,128)(2,1)S(1)}, bf16[64,768]{1,0:T(8,128)(2,1)S(1)}, u32[]{:S(2)}, u32[]{:S(2)}) collective-permute-start(bf16[64,768]{1,0:T(8,128)(2,1)S(1)} %get-tuple-element.34), channel_id=1, source_target_pairs={{0,4},{1,5},{2,6},{3,7},{4,0},{5,1},{6,2},{7,3},{8,12},{9,13},{10,... | collective-permute-start | bytes 294920 | tf_op jit(solution)/shard_map/ppermute | solution.py:20
  14.5 4.6 %collective-permute-start.7 = (bf16[64,768]{1,0:T(8,128)(2,1)S(1)}, bf16[64,768]{1,0:T(8,128)(2,1)S(1)}, u32[]{:S(2)}, u32[]{:S(2)}) collective-permute-start(bf16[64,768]{1,0:T(8,128)(2,1)S(1)} %get-tuple-element.35), channel_id=1, source_target_pairs={{0,2},{1,3},{2,0},{3,1},{4,6},{5,7},{6,4},{7,5},{8,10},{9,11},{10,... | collective-permute-start | bytes 294920 | tf_op jit(solution)/shard_map/ppermute | solution.py:20
  19.2 4.7 %collective-permute-start.8 = (bf16[64,768]{1,0:T(8,128)(2,1)S(1)}, bf16[64,768]{1,0:T(8,128)(2,1)S(1)}, u32[]{:S(2)}, u32[]{:S(2)}) collective-permute-start(bf16[64,768]{1,0:T(8,128)(2,1)S(1)} %fusion), channel_id=1, source_target_pairs={{0,8},{8,0},{16,24},{24,16},{1,9},{9,1},{17,25},{25,17},{2,10},{10... | collective-permute-start | bytes 294920 | tf_op jit(solution)/shard_map/ppermute | solution.py:20
  20.9 6.1 %collective-permute-start.11 = (bf16[256,768]{1,0:T(8,128)(2,1)S(1)}, bf16[256,768]{1,0:T(8,128)(2,1)S(1)}, u32[]{:S(2)}, u32[]{:S(2)}) collective-permute-start(bf16[256,768]{1,0:T(8,128)(2,1)S(1)} %get-tuple-element.47.c_own_ref), channel_id=1, source_target_pairs={{0,1},{1,0},{2,3},{3,2},{4,5},{5,4},{6,7},{7,6},{8,9},{9,8},{10,11... | collective-permute-start | bytes 1179656 | tf_op jit(solution)/shard_map/ppermute | solution.py:20
  21.0 6.0 %collective-permute-start.10 = (bf16[256,512]{1,0:T(8,128)(2,1)S(1)}, bf16[256,512]{1,0:T(8,128)(2,1)S(1)}, u32[]{:S(2)}, u32[]{:S(2)}) collective-permute-start(bf16[256,512]{1,0:T(8,128)(2,1)S(1)} %get-tuple-element.46), channel_id=1, source_target_pairs={{0,1},{1,0},{2,3},{3,2},{4,5},{5,4},{6,7},{7,6},{8,9},{9,8},{10,11... | collective-permute-start | bytes 786440 | tf_op jit(solution)/shard_map/ppermute | solution.py:20
  23.9 5.6 %collective-permute-start.9 = (bf16[64,768]{1,0:T(8,128)(2,1)S(1)}, bf16[64,768]{1,0:T(8,128)(2,1)S(1)}, u32[]{:S(2)}, u32[]{:S(2)}) collective-permute-start(bf16[64,768]{1,0:T(8,128)(2,1)S(1)} %get-tuple-element.48), channel_id=1, source_target_pairs={{0,16},{8,24},{16,0},{24,8},{1,17},{9,25},{17,1},{25,9},{2,18},{10... | collective-permute-start | bytes 294920 | tf_op jit(solution)/shard_map/ppermute | solution.py:20

commit v8 on v7

--- a/solution.py
+++ b/solution.py
@@ -139,19 +139,20 @@
 
     for unit in units:
         block = gather(unit, piece_refs)
-        grad = None
-        for emb_ref, turned_ref, target_ref, out_refs in zip(emb_refs, turned_refs, target_refs, dlogit_refs):
-            logits = jnp.dot(block, turned_ref[...], preferred_element_type=F32)
+        logits = [jnp.dot(block, ref[...], preferred_element_type=F32) for ref in turned_refs]
+        dlogits = []
+        for x, target_ref in zip(logits, target_refs):
             signed = gather(unit, [target_ref] * count, lambda i: which[i] * each).astype(F32)
-            dlogits = (signed * jax.nn.sigmoid(jnp.where(signed < 0, -logits, logits))).astype(BF16)
-            term = jnp.dot(dlogits, emb_ref[...], preferred_element_type=F32)
-            grad = term if grad is None else grad + term
-            off = 0
-            for i, start, rows in unit:
-                out_refs[i][start : start + rows] = dlogits[off : off + rows]
-                off += rows
+            dlogits.append((signed * jax.nn.sigmoid(jnp.where(signed < 0, -x, x))).astype(BF16))
+        grad = jnp.dot(
+            jnp.concatenate(dlogits, 1),
+            jnp.concatenate([ref[...] for ref in emb_refs], 0),
+            preferred_element_type=F32,
+        )
         off = 0
         for i, start, rows in unit:
+            for d, out_refs in zip(dlogits, dlogit_refs):
+                out_refs[i][start : start + rows] = d[off : off + rows]
             grad_refs[i][start : start + rows] = grad[off : off + rows].astype(grad_refs[i].dtype)
             off += rows
 

time: 30.5 us -> 30.3 us (level)
  transfers between devices with their start and end apart: 12 -> 12, of which waited for: 5 -> 5; matrix products, arithmetic and copies ran while one was open for 0% -> 0% of each run, Pallas kernels for 23% -> 22%
where the time goes in v8:
time: 30.3 us; the launch traced here: 30.1 us
  starting transfers between devices  14.2 us (47%)
  waiting for transfers between devices  7.66 us (25%)
  Pallas kernels  7.37 us (24%)
  between operations  0.72 us (2%)
    ppermute x12, starting transfers between devices, flip(): lax.ppermute(value, axis, [(i, i ^ mask) for i in range(lax.axis_size(axi...  14.2 us
    ppermute x12, waiting for transfers between devices, flip(): lax.ppermute(value, axis, [(i, i ^ mask) for i in range(lax.axis_size(axi...  7.66 us
    pallas_call x1, Pallas kernels, shards(): pl.pallas_call(emb_kernel, out_shape=jax.ShapeDtypeStruct((docs, width),...  1.74 us
    pallas_call x2, Pallas kernels, score(): pl.pallas_call(functools.partial(score_kernel, which=which, after=len(aft...  1.44 us
    pallas_call x1, Pallas kernels, shards(): pl.pallas_call(turn_kernel, out_shape=[jax.ShapeDtypeStruct((docs, width)...  1.41 us
    pallas_call x1, Pallas kernels, shards(): pl.pallas_call(functools.partial(pack_kernel, scale=1.0 / math.sqrt(docs...  1.15 us
    pallas_call x1, Pallas kernels, shards(): pl.pallas_call(functools.partial(targets_kernel, panel=panel, slots=slots...  0.82 us
    pallas_call x1, Pallas kernels, shards(): pl.pallas_call(finish_kernel, out_shape=jax.ShapeDtypeStruct((panel, widt...  0.76 us
  transfers between devices with their start and end apart: 12, of which 5 were waited for; matrix products, arithmetic and copies ran while one was open for 0% of the time, Pallas kernels for 22%

profile of v8, /device:TPU:0, one launch (start us, length us, event | category | flops | bytes accessed | tf_op | source)
XLA Modules:
  0.0 30.1 jit_solution(4409835358556255667)
XLA Ops:
  0.6 0.5 %collective-permute-start.1 = (bf16[512,768]{1,0:T(8,128)(2,1)}, bf16[512,768]{1,0:T(8,128)(2,1)S(1)}, u32[]{:S(2)}, u32[]{:S(2)}) collective-permute-start(bf16[512,768]{1,0:T(8,128)(2,1)} %emb_hbm.1), channel_id=1, source_target_pairs={{0,1},{1,0},{2,3},{3,2},{4,5},{5,4},{6,7},{7,6},{8,9},{9,8},{10,11... | collective-permute-start | bytes 2359304 | tf_op jit(solution)/shard_map/ppermute | solution.py:20
  1.1 1.1 %pack.1 = (bf16[64,768]{1,0:T(8,128)(2,1)S(1)}, f32[64,128]{1,0:T(8,128)S(1)}, bf16[40,512]{1,0:T(8,128)(2,1)S(1)}) custom-call(f32[64,768]{1,0:T(8,128)} %classifier_hbm.1, s32[1,64]{1,0:T(1,128)} %bitcast.9, s32[4,512]{1,0:T(4,128)} %bitcast.6, s32[4,512]{1,0:T(4,128)} %bitcast.7, s32[4,512]{1,0:T(4,128)} %bitcast.8, s32[4,8,512]{2,1,0:T(8,128)} %bitcast.5), custom_call_target="tpu_custom_call" | custom-call | flops 49152 | bytes 376832 | tf_op jit(solution)/shard_map/pack/pallas_call | solution.py:211
  2.3 3.5 %collective-permute-start = (bf16[64,768]{1,0:T(8,128)(2,1)S(1)}, bf16[64,768]{1,0:T(8,128)(2,1)S(1)}, u32[]{:S(2)}, u32[]{:S(2)}) collective-permute-start(bf16[64,768]{1,0:T(8,128)(2,1)S(1)} %get-tuple-element.25.refs_1_), channel_id=1, source_target_pairs={{0,6},{1,7},{2,4},{3,5},{4,2},{5,3},{6,0},{7,1},{8,14},{9,15},{10,... | collective-permute-start | bytes 294920 | tf_op jit(solution)/shard_map/ppermute | solution.py:20
  5.8 0.2 collective-permute-start.2
  6.0 0.5 %collective-permute-start.5 = (bf16[64,768]{1,0:T(8,128)(2,1)S(1)}, bf16[64,768]{1,0:T(8,128)(2,1)S(1)}, u32[]{:S(2)}, u32[]{:S(2)}) collective-permute-start(bf16[64,768]{1,0:T(8,128)(2,1)S(1)} %get-tuple-element.25.refs_1_), channel_id=1, source_target_pairs={{0,4},{1,5},{2,6},{3,7},{4,0},{5,1},{6,2},{7,3},{8,12},{9,13},{10,... | collective-permute-start | bytes 294920 | tf_op jit(solution)/shard_map/ppermute | solution.py:20
  6.5 0.4 %collective-permute-start.4 = (bf16[64,768]{1,0:T(8,128)(2,1)S(1)}, bf16[64,768]{1,0:T(8,128)(2,1)S(1)}, u32[]{:S(2)}, u32[]{:S(2)}) collective-permute-start(bf16[64,768]{1,0:T(8,128)(2,1)S(1)} %get-tuple-element.25.refs_1_), channel_id=1, source_target_pairs={{0,2},{1,3},{2,0},{3,1},{4,6},{5,7},{6,4},{7,5},{8,10},{9,11},{10,... | collective-permute-start | bytes 294920 | tf_op jit(solution)/shard_map/ppermute | solution.py:20
  7.0 0.0 collective-permute-done.1.other_ref.refs_3_
  7.0 1.4 %turn.1 = (bf16[512,768]{1,0:T(8,128)(2,1)S(1)}, bf16[768,512]{1,0:T(8,128)(2,1)S(1)}, bf16[768,512]{1,0:T(8,128)(2,1)S(1)}) custom-call(bf16[512,768]{1,0:T(8,128)(2,1)} %emb_hbm.1, bf16[512,768]{1,0:T(8,128)(2,1)S(1)} %collective-permute-done.1.other_ref.refs_3_), custom_call_target="tpu_custom_call" | custom-call | flops 393216 | bytes 3932160 | tf_op jit(solution)/shard_map/turn/pallas_call | solution.py:239
  8.4 0.0 collective-permute-done.2.index_other_ref
  8.4 0.8 %targets.1 = (bf16[256,512]{1,0:T(8,128)(2,1)S(1)}, bf16[256,512]{1,0:T(8,128)(2,1)S(1)}) custom-call(bf16[40,512]{1,0:T(8,128)(2,1)S(1)} %get-tuple-element.29.index_own_ref, bf16[40,512]{1,0:T(8,128)(2,1)S(1)} %collective-permute-done.2.index_other_ref, bf16[768,512]{1,0:T(8,128)(2,1)S(1)} %get-tuple-element.28.after_ref.refs_5_), custom_call_target="tpu_custom_call" | custom-call | flops 10485760 | bytes 688128 | tf_op jit(solution)/shard_map/targets/pallas_call | solution.py:250
  9.2 0.1 collective-permute-done.refs_0_
  9.3 0.7 %score.2 = (bf16[64,768]{1,0:T(8,128)(2,1)S(1)}, f32[64,768]{1,0:T(8,128)S(1)}, bf16[64,512]{1,0:T(8,128)(2,1)S(1)}, bf16[64,512]{1,0:T(8,128)(2,1)S(1)}, bf16[6...) custom-call(bf16[64,768]{1,0:T(8,128)(2,1)S(1)} %collective-permute-done.refs_0_, ...), custom_call_target="tpu_custom_call" | custom-call | flops 402653184 | bytes 4456448 | tf_op jit(solution)/shard_map/score/pallas_call | solution.py:265
  10.1 3.1 %collective-permute-start.3 = (bf16[65,768]{1,0:T(8,128)(2,1)S(1)}, bf16[65,768]{1,0:T(8,128)(2,1)S(1)}, u32[]{:S(2)}, u32[]{:S(2)}) collective-permute-start(bf16[65,768]{1,0:T(8,128)(2,1)S(1)} %pad_maximum_fusion), channel_id=1, source_target_pairs={{0,6},{1,7},{2,4},{3,5},{4,2},{5,3},{6,0},{7,1},{8,14},{9,15},{10,... | collective-permute-start | bytes 299528 | tf_op jit(solution)/shard_map/ppermute | solution.py:20
  13.2 0.0 collective-permute-done.5.refs_1_.refs_3_
  13.2 0.0 collective-permute-done.4.refs_0_.refs_2_
  13.2 0.7 %score.3 = (bf16[64,768]{1,0:T(8,128)(2,1)S(1)}, bf16[64,768]{1,0:T(8,128)(2,1)S(1)}, bf16[64,512]{1,0:T(8,128)(2,1)S(1)}, bf16[64,512]{1,0:T(8,128)(2,1)S(1)}, ...) custom-call(bf16[64,768]{1,0:T(8,128)(2,1)S(1)} %collective-permute-done.4.refs_0_.refs_2_, ...), custom_call_target="tpu_custom_call" | custom-call | flops 402653184 | bytes 4456448 | tf_op jit(solution)/shard_map/score/pallas_call | solution.py:265
  13.9 0.4 %collective-permute-start.6 = (bf16[64,768]{1,0:T(8,128)(2,1)S(1)}, bf16[64,768]{1,0:T(8,128)(2,1)S(1)}, u32[]{:S(2)}, u32[]{:S(2)}) collective-permute-start(bf16[64,768]{1,0:T(8,128)(2,1)S(1)} %get-tuple-element.34), channel_id=1, source_target_pairs={{0,4},{1,5},{2,6},{3,7},{4,0},{5,1},{6,2},{7,3},{8,12},{9,13},{10,... | collective-permute-start | bytes 294920 | tf_op jit(solution)/shard_map/ppermute | solution.py:20
  14.3 0.5 %collective-permute-start.7 = (bf16[64,768]{1,0:T(8,128)(2,1)S(1)}, bf16[64,768]{1,0:T(8,128)(2,1)S(1)}, u32[]{:S(2)}, u32[]{:S(2)}) collective-permute-start(bf16[64,768]{1,0:T(8,128)(2,1)S(1)} %get-tuple-element.35), channel_id=1, source_target_pairs={{0,2},{1,3},{2,0},{3,1},{4,6},{5,7},{6,4},{7,5},{8,10},{9,11},{10,... | collective-permute-start | bytes 294920 | tf_op jit(solution)/shard_map/ppermute | solution.py:20
  14.8 3.9 %collective-permute-done.6 = bf16[64,768]{1,0:T(8,128)(2,1)S(1)} collective-permute-done((bf16[64,768]{1,0:T(8,128)(2,1)S(1)}, bf16[64,768]{1,0:T(8,128)(2,1)S(1)}, u32[]{:S(2)}, u32[]{:S(2)}) %collective-permute-start.6) | collective-permute-done | bytes 98336 | tf_op jit(solution)/shard_map/ppermute | solution.py:20
  18.6 0.3 %collective-permute-done.7 = bf16[64,768]{1,0:T(8,128)(2,1)S(1)} collective-permute-done((bf16[64,768]{1,0:T(8,128)(2,1)S(1)}, bf16[64,768]{1,0:T(8,128)(2,1)S(1)}, u32[]{:S(2)}, u32[]{:S(2)}) %collective-permute-start.7) | collective-permute-done | bytes 98336 | tf_op jit(solution)/shard_map/ppermute | solution.py:20
  18.9 0.0 collective-permute-done.3
  19.0 1.6 %collective-permute-start.8 = (bf16[64,768]{1,0:T(8,128)(2,1)S(1)}, bf16[64,768]{1,0:T(8,128)(2,1)S(1)}, u32[]{:S(2)}, u32[]{:S(2)}) collective-permute-start(bf16[64,768]{1,0:T(8,128)(2,1)S(1)} %fusion), channel_id=1, source_target_pairs={{0,8},{8,0},{16,24},{24,16},{1,9},{9,1},{17,25},{25,17},{2,10},{10... | collective-permute-start | bytes 294920 | tf_op jit(solution)/shard_map/ppermute | solution.py:20
  20.6 0.1 join.1
  20.7 0.1 collective-permute-start.11
  20.8 0.5 %collective-permute-start.10 = (bf16[256,512]{1,0:T(8,128)(2,1)S(1)}, bf16[256,512]{1,0:T(8,128)(2,1)S(1)}, u32[]{:S(2)}, u32[]{:S(2)}) collective-permute-start(bf16[256,512]{1,0:T(8,128)(2,1)S(1)} %get-tuple-element.46), channel_id=1, source_target_pairs={{0,1},{1,0},{2,3},{3,2},{4,5},{5,4},{6,7},{7,6},{8,9},{9,8},{10,11... | collective-permute-start | bytes 786440 | tf_op jit(solution)/shard_map/ppermute | solution.py:20
  21.3 2.4 %collective-permute-done.8 = bf16[64,768]{1,0:T(8,128)(2,1)S(1)} collective-permute-done((bf16[64,768]{1,0:T(8,128)(2,1)S(1)}, bf16[64,768]{1,0:T(8,128)(2,1)S(1)}, u32[]{:S(2)}, u32[]{:S(2)}) %collective-permute-start.8) | collective-permute-done | bytes 98336 | tf_op jit(solution)/shard_map/ppermute | solution.py:20
  23.7 0.1 fusion.1
  23.7 2.9 %collective-permute-start.9 = (bf16[64,768]{1,0:T(8,128)(2,1)S(1)}, bf16[64,768]{1,0:T(8,128)(2,1)S(1)}, u32[]{:S(2)}, u32[]{:S(2)}) collective-permute-start(bf16[64,768]{1,0:T(8,128)(2,1)S(1)} %get-tuple-element.48), channel_id=1, source_target_pairs={{0,16},{8,24},{16,0},{24,8},{1,17},{9,25},{17,1},{25,9},{2,18},{10... | collective-permute-start | bytes 294920 | tf_op jit(solution)/shard_map/ppermute | solution.py:20
  26.6 0.0 collective-permute-done.10.d_other_ref
  26.6 0.0 collective-permute-done.11.c_other_ref
  26.6 1.7 %emb_grad.1.after_hbm = f32[512,768]{1,0:T(8,128)} custom-call(bf16[256,512]{1,0:T(8,128)(2,1)S(1)} %get-tuple-element.45.d_own_ref, bf16[256,512]{1,0:T(8,128)(2,1)S(1)} %collective-permute-done.10.d_other_ref, bf16[256,768]{1,0:T(8,128)(2,1)S(1)} %get-tuple-element.47.c_own_ref, bf16[256,768]{1,0:T(8,128)(2,1)S(1)} %collective-permute-done.11.c_other_ref, ...), custom_call_target="tpu_custom_call" | custom-call | flops 402653184 | bytes 2883584 | tf_op jit(solution)/shard_map/emb_grad/pallas_call | solution.py:323
  28.3 1.0 %collective-permute-done.9.received_ref = bf16[64,768]{1,0:T(8,128)(2,1)S(1)} collective-permute-done((bf16[64,768]{1,0:T(8,128)(2,1)S(1)}, bf16[64,768]{1,0:T(8,128)(2,1)S(1)}, u32[]{:S(2)}, u32[]{:S(2)}) %collective-permute-start.9) | collective-permute-done | bytes 98336 | tf_op jit(solution)/shard_map/ppermute | solution.py:20
  29.3 0.8 %finish.1 = f32[64,768]{1,0:T(8,128)} custom-call(f32[64,768]{1,0:T(8,128)S(1)} %get-tuple-element.49.after_ref.grad_ref, bf16[64,768]{1,0:T(8,128)(2,1)S(1)} %collective-permute-done.9.received_ref, f32[64,128]{1,0:T(8,128)S(1)} %get-tuple-element.36.column_ref, f32[512,768]{1,0:T(8,128)} %emb_grad.1.after_hbm), custom_call_target="tpu_custom_call" | custom-call | flops 49152 | bytes 491520 | tf_op jit(solution)/shard_map/finish/pallas_call | solution.py:333
  (3 shorter events, 0.1 us)
Async XLA Ops:
  0.6 6.3 %collective-permute-start.1 = (bf16[512,768]{1,0:T(8,128)(2,1)}, bf16[512,768]{1,0:T(8,128)(2,1)S(1)}, u32[]{:S(2)}, u32[]{:S(2)}) collective-permute-start(bf16[512,768]{1,0:T(8,128)(2,1)} %emb_hbm.1), channel_id=1, source_target_pairs={{0,1},{1,0},{2,3},{3,2},{4,5},{5,4},{6,7},{7,6},{8,9},{9,8},{10,11... | collective-permute-start | bytes 2359304 | tf_op jit(solution)/shard_map/ppermute | solution.py:20
  2.3 7.0 %collective-permute-start = (bf16[64,768]{1,0:T(8,128)(2,1)S(1)}, bf16[64,768]{1,0:T(8,128)(2,1)S(1)}, u32[]{:S(2)}, u32[]{:S(2)}) collective-permute-start(bf16[64,768]{1,0:T(8,128)(2,1)S(1)} %get-tuple-element.25.refs_1_), channel_id=1, source_target_pairs={{0,6},{1,7},{2,4},{3,5},{4,2},{5,3},{6,0},{7,1},{8,14},{9,15},{10,... | collective-permute-start | bytes 294920 | tf_op jit(solution)/shard_map/ppermute | solution.py:20
  5.8 2.6 %collective-permute-start.2 = (bf16[40,512]{1,0:T(8,128)(2,1)S(1)}, bf16[40,512]{1,0:T(8,128)(2,1)S(1)}, u32[]{:S(2)}, u32[]{:S(2)}) collective-permute-start(bf16[40,512]{1,0:T(8,128)(2,1)S(1)} %get-tuple-element.29.index_own_ref), channel_id=1, source_target_pairs={{0,1},{1,0},{2,3},{3,2},{4,5},{5,4},{6,7},{7,6},{8,9},{9,8},{10,11... | collective-permute-start | bytes 122888 | tf_op jit(solution)/shard_map/ppermute | solution.py:20
  6.0 7.2 %collective-permute-start.5 = (bf16[64,768]{1,0:T(8,128)(2,1)S(1)}, bf16[64,768]{1,0:T(8,128)(2,1)S(1)}, u32[]{:S(2)}, u32[]{:S(2)}) collective-permute-start(bf16[64,768]{1,0:T(8,128)(2,1)S(1)} %get-tuple-element.25.refs_1_), channel_id=1, source_target_pairs={{0,4},{1,5},{2,6},{3,7},{4,0},{5,1},{6,2},{7,3},{8,12},{9,13},{10,... | collective-permute-start | bytes 294920 | tf_op jit(solution)/shard_map/ppermute | solution.py:20
  6.5 6.7 %collective-permute-start.4 = (bf16[64,768]{1,0:T(8,128)(2,1)S(1)}, bf16[64,768]{1,0:T(8,128)(2,1)S(1)}, u32[]{:S(2)}, u32[]{:S(2)}) collective-permute-start(bf16[64,768]{1,0:T(8,128)(2,1)S(1)} %get-tuple-element.25.refs_1_), channel_id=1, source_target_pairs={{0,2},{1,3},{2,0},{3,1},{4,6},{5,7},{6,4},{7,5},{8,10},{9,11},{10,... | collective-permute-start | bytes 294920 | tf_op jit(solution)/shard_map/ppermute | solution.py:20
  10.1 8.9 %collective-permute-start.3 = (bf16[65,768]{1,0:T(8,128)(2,1)S(1)}, bf16[65,768]{1,0:T(8,128)(2,1)S(1)}, u32[]{:S(2)}, u32[]{:S(2)}) collective-permute-start(bf16[65,768]{1,0:T(8,128)(2,1)S(1)} %pad_maximum_fusion), channel_id=1, source_target_pairs={{0,6},{1,7},{2,4},{3,5},{4,2},{5,3},{6,0},{7,1},{8,14},{9,15},{10,... | collective-permute-start | bytes 299528 | tf_op jit(solution)/shard_map/ppermute | solution.py:20
  13.9 4.7 %collective-permute-start.6 = (bf16[64,768]{1,0:T(8,128)(2,1)S(1)}, bf16[64,768]{1,0:T(8,128)(2,1)S(1)}, u32[]{:S(2)}, u32[]{:S(2)}) collective-permute-start(bf16[64,768]{1,0:T(8,128)(2,1)S(1)} %get-tuple-element.34), channel_id=1, source_target_pairs={{0,4},{1,5},{2,6},{3,7},{4,0},{5,1},{6,2},{7,3},{8,12},{9,13},{10,... | collective-permute-start | bytes 294920 | tf_op jit(solution)/shard_map/ppermute | solution.py:20
  14.3 4.6 %collective-permute-start.7 = (bf16[64,768]{1,0:T(8,128)(2,1)S(1)}, bf16[64,768]{1,0:T(8,128)(2,1)S(1)}, u32[]{:S(2)}, u32[]{:S(2)}) collective-permute-start(bf16[64,768]{1,0:T(8,128)(2,1)S(1)} %get-tuple-element.35), channel_id=1, source_target_pairs={{0,2},{1,3},{2,0},{3,1},{4,6},{5,7},{6,4},{7,5},{8,10},{9,11},{10,... | collective-permute-start | bytes 294920 | tf_op jit(solution)/shard_map/ppermute | solution.py:20
  19.0 4.7 %collective-permute-start.8 = (bf16[64,768]{1,0:T(8,128)(2,1)S(1)}, bf16[64,768]{1,0:T(8,128)(2,1)S(1)}, u32[]{:S(2)}, u32[]{:S(2)}) collective-permute-start(bf16[64,768]{1,0:T(8,128)(2,1)S(1)} %fusion), channel_id=1, source_target_pairs={{0,8},{8,0},{16,24},{24,16},{1,9},{9,1},{17,25},{25,17},{2,10},{10... | collective-permute-start | bytes 294920 | tf_op jit(solution)/shard_map/ppermute | solution.py:20
  20.7 5.9 %collective-permute-start.11 = (bf16[256,768]{1,0:T(8,128)(2,1)S(1)}, bf16[256,768]{1,0:T(8,128)(2,1)S(1)}, u32[]{:S(2)}, u32[]{:S(2)}) collective-permute-start(bf16[256,768]{1,0:T(8,128)(2,1)S(1)} %get-tuple-element.47.c_own_ref), channel_id=1, source_target_pairs={{0,1},{1,0},{2,3},{3,2},{4,5},{5,4},{6,7},{7,6},{8,9},{9,8},{10,11... | collective-permute-start | bytes 1179656 | tf_op jit(solution)/shard_map/ppermute | solution.py:20
  20.8 5.8 %collective-permute-start.10 = (bf16[256,512]{1,0:T(8,128)(2,1)S(1)}, bf16[256,512]{1,0:T(8,128)(2,1)S(1)}, u32[]{:S(2)}, u32[]{:S(2)}) collective-permute-start(bf16[256,512]{1,0:T(8,128)(2,1)S(1)} %get-tuple-element.46), channel_id=1, source_target_pairs={{0,1},{1,0},{2,3},{3,2},{4,5},{5,4},{6,7},{7,6},{8,9},{9,8},{10,11... | collective-permute-start | bytes 786440 | tf_op jit(solution)/shard_map/ppermute | solution.py:20
  23.7 5.6 %collective-permute-start.9 = (bf16[64,768]{1,0:T(8,128)(2,1)S(1)}, bf16[64,768]{1,0:T(8,128)(2,1)S(1)}, u32[]{:S(2)}, u32[]{:S(2)}) collective-permute-start(bf16[64,768]{1,0:T(8,128)(2,1)S(1)} %get-tuple-element.48), channel_id=1, source_target_pairs={{0,16},{8,24},{16,0},{24,8},{1,17},{9,25},{17,1},{25,9},{2,18},{10... | collective-permute-start | bytes 294920 | tf_op jit(solution)/shard_map/ppermute | solution.py:20

commit v9 on v8

--- a/solution.py
+++ b/solution.py
@@ -155,6 +155,9 @@
                 out_refs[i][start : start + rows] = d[off : off + rows]
             grad_refs[i][start : start + rows] = grad[off : off + rows].astype(grad_refs[i].dtype)
             off += rows
+    for ref in grad_refs:
+        if ref.shape[0] > each:
+            ref[each:] = jnp.zeros((ref.shape[0] - each, ref.shape[1]), ref.dtype)
 
 
 def join_kernel(*refs, count):
@@ -264,7 +267,10 @@
         count, rows = len(which), each * len(which)
         outs = pl.pallas_call(
             functools.partial(score_kernel, which=which, after=len(after)),
-            out_shape=[jax.ShapeDtypeStruct((each, width), BF16 if i else F32) for i in which]
+            out_shape=[
+                jax.ShapeDtypeStruct((each + (PACKED if i == 3 else 0), width), BF16 if i else F32)
+                for i in which
+            ]
             + [jax.ShapeDtypeStruct((each, docs), BF16)] * (2 * count),
             in_specs=vmem(count + 6 + len(after)),
             out_specs=vmem(3 * count),
@@ -306,9 +312,9 @@
         received = []
         for i in reversed(range(len(masks))):
             value = grads[i + 1]
-            if i == 2:
+            if i == 2 and value.shape[0] == grads[0].shape[0]:
                 value = jnp.concatenate([value, value[:1]], 0)
-            received.append(flip(value, "lab", masks[i])[: grads[i + 1].shape[0]])
+            received.append(flip(value, "lab", masks[i])[: grads[0].shape[0]])
         grad = grads[0]
         for r in received:
             grad = grad + r.astype(F32)
@@ -316,9 +322,14 @@
         grad = grads[0]
     d_other, classifier_other = flip(d_theirs, "lab", 1), flip(classifier_own, "lab", 1)
     bits = [1 << bit for bit in range(enc.bit_length() - 1)]
-    for bit in bits[:-1]:
-        grad = grad + flip(grad.astype(BF16), "enc", bit).astype(F32)
-    received = flip(grad.astype(BF16), "enc", bits[-1])
+
+    def along(value, even, odd):
+        pairs = [(i, i ^ lab * (odd if i & 1 else even)) for i in range(enc * lab)]
+        return lax.ppermute(value, ("enc", "lab"), pairs)
+
+    for even, odd in list(zip(bits, reversed(bits)))[:-1]:
+        grad = grad + along(grad.astype(BF16), even, odd).astype(F32)
+    received = along(grad.astype(BF16), bits[-1], bits[0])
 
     emb_grad = pl.pallas_call(
         emb_kernel,

time: 30.3 us -> 30.4 us (level)
  waiting for transfers between devices: 7.66 us -> 8.69 us
  starting transfers between devices: 14.2 us -> 13.3 us
    ppermute x12 -> x10, starting transfers between devices: 14.2 us -> 9.01 us  [flip(): lax.ppermute(value, axis, [(i, i ^ mask) for i in range(lax.axis_size(axi...]
    ppermute x0 -> x2, starting transfers between devices: none -> 4.29 us  [along(): return lax.ppermute(value, ('enc', 'lab'), pairs)]
    ppermute x0 -> x2, waiting for transfers between devices: none -> 3.58 us  [along(): return lax.ppermute(value, ('enc', 'lab'), pairs)]
    ppermute x12 -> x10, waiting for transfers between devices: 7.66 us -> 5.11 us  [flip(): lax.ppermute(value, axis, [(i, i ^ mask) for i in range(lax.axis_size(axi...]
where the time goes in v9:
time: 30.4 us; the launch traced here: 30.2 us
  starting transfers between devices  13.3 us (44%)
  waiting for transfers between devices  8.69 us (29%)
  Pallas kernels  7.39 us (24%)
  between operations  0.71 us (2%)
    ppermute x10, starting transfers between devices, flip(): lax.ppermute(value, axis, [(i, i ^ mask) for i in range(lax.axis_size(axi...  9.01 us
    ppermute x10, waiting for transfers between devices, flip(): lax.ppermute(value, axis, [(i, i ^ mask) for i in range(lax.axis_size(axi...  5.11 us
    ppermute x2, starting transfers between devices, along(): return lax.ppermute(value, ('enc', 'lab'), pairs)  4.29 us
    ppermute x2, waiting for transfers between devices, along(): return lax.ppermute(value, ('enc', 'lab'), pairs)  3.58 us
    pallas_call x1, Pallas kernels, shards(): pl.pallas_call(emb_kernel, out_shape=jax.ShapeDtypeStruct((docs, width),...  1.74 us
    pallas_call x2, Pallas kernels, score(): pl.pallas_call(functools.partial(score_kernel, which=which, after=len(aft...  1.46 us
    pallas_call x1, Pallas kernels, shards(): pl.pallas_call(turn_kernel, out_shape=[jax.ShapeDtypeStruct((docs, width)...  1.41 us
    pallas_call x1, Pallas kernels, shards(): pl.pallas_call(functools.partial(pack_kernel, scale=1.0 / math.sqrt(docs...  1.15 us
  transfers between devices with their start and end apart: 12, of which 5 were waited for; matrix products, arithmetic and copies ran while one was open for 0% of the time, Pallas kernels for 22%

profile of v9, /device:TPU:0, one launch (start us, length us, event | category | flops | bytes accessed | tf_op | source)
XLA Modules:
  0.0 30.2 jit_solution(16067479220198368895)
XLA Ops:
  0.6 0.5 %collective-permute-start.1 = (bf16[512,768]{1,0:T(8,128)(2,1)}, bf16[512,768]{1,0:T(8,128)(2,1)S(1)}, u32[]{:S(2)}, u32[]{:S(2)}) collective-permute-start(bf16[512,768]{1,0:T(8,128)(2,1)} %emb_hbm.1), channel_id=1, source_target_pairs={{0,1},{1,0},{2,3},{3,2},{4,5},{5,4},{6,7},{7,6},{8,9},{9,8},{10,11... | collective-permute-start | bytes 2359304 | tf_op jit(solution)/shard_map/ppermute | solution.py:20
  1.1 1.1 %pack.1 = (bf16[64,768]{1,0:T(8,128)(2,1)S(1)}, f32[64,128]{1,0:T(8,128)S(1)}, bf16[40,512]{1,0:T(8,128)(2,1)S(1)}) custom-call(f32[64,768]{1,0:T(8,128)} %classifier_hbm.1, s32[1,64]{1,0:T(1,128)} %bitcast.9, s32[4,512]{1,0:T(4,128)} %bitcast.6, s32[4,512]{1,0:T(4,128)} %bitcast.7, s32[4,512]{1,0:T(4,128)} %bitcast.8, s32[4,8,512]{2,1,0:T(8,128)} %bitcast.5), custom_call_target="tpu_custom_call" | custom-call | flops 49152 | bytes 376832 | tf_op jit(solution)/shard_map/pack/pallas_call | solution.py:214
  2.3 3.5 %collective-permute-start = (bf16[64,768]{1,0:T(8,128)(2,1)S(1)}, bf16[64,768]{1,0:T(8,128)(2,1)S(1)}, u32[]{:S(2)}, u32[]{:S(2)}) collective-permute-start(bf16[64,768]{1,0:T(8,128)(2,1)S(1)} %get-tuple-element.25.refs_1_), channel_id=1, source_target_pairs={{0,6},{1,7},{2,4},{3,5},{4,2},{5,3},{6,0},{7,1},{8,14},{9,15},{10,... | collective-permute-start | bytes 294920 | tf_op jit(solution)/shard_map/ppermute | solution.py:20
  5.8 0.5 %collective-permute-start.5 = (bf16[64,768]{1,0:T(8,128)(2,1)S(1)}, bf16[64,768]{1,0:T(8,128)(2,1)S(1)}, u32[]{:S(2)}, u32[]{:S(2)}) collective-permute-start(bf16[64,768]{1,0:T(8,128)(2,1)S(1)} %get-tuple-element.25.refs_1_), channel_id=1, source_target_pairs={{0,4},{1,5},{2,6},{3,7},{4,0},{5,1},{6,2},{7,3},{8,12},{9,13},{10,... | collective-permute-start | bytes 294920 | tf_op jit(solution)/shard_map/ppermute | solution.py:20
  6.3 0.1 collective-permute-start.4
  6.5 0.0 collective-permute-start.2
  6.5 0.0 collective-permute-done.1.other_ref.refs_3_
  6.5 1.4 %turn.1 = (bf16[512,768]{1,0:T(8,128)(2,1)S(1)}, bf16[768,512]{1,0:T(8,128)(2,1)S(1)}, bf16[768,512]{1,0:T(8,128)(2,1)S(1)}) custom-call(bf16[512,768]{1,0:T(8,128)(2,1)} %emb_hbm.1, bf16[512,768]{1,0:T(8,128)(2,1)S(1)} %collective-permute-done.1.other_ref.refs_3_), custom_call_target="tpu_custom_call" | custom-call | flops 393216 | bytes 3932160 | tf_op jit(solution)/shard_map/turn/pallas_call | solution.py:242
  7.9 0.0 collective-permute-done.2.index_other_ref
  7.9 0.8 %targets.1 = (bf16[256,512]{1,0:T(8,128)(2,1)S(1)}, bf16[256,512]{1,0:T(8,128)(2,1)S(1)}) custom-call(bf16[40,512]{1,0:T(8,128)(2,1)S(1)} %get-tuple-element.29.index_own_ref, bf16[40,512]{1,0:T(8,128)(2,1)S(1)} %collective-permute-done.2.index_other_ref, bf16[768,512]{1,0:T(8,128)(2,1)S(1)} %get-tuple-element.28.after_ref.refs_5_), custom_call_target="tpu_custom_call" | custom-call | flops 10485760 | bytes 688128 | tf_op jit(solution)/shard_map/targets/pallas_call | solution.py:253
  8.7 0.6 %collective-permute-done.refs_0_ = bf16[64,768]{1,0:T(8,128)(2,1)S(1)} collective-permute-done((bf16[64,768]{1,0:T(8,128)(2,1)S(1)}, bf16[64,768]{1,0:T(8,128)(2,1)S(1)}, u32[]{:S(2)}, u32[]{:S(2)}) %collective-permute-start) | collective-permute-done | bytes 98336 | tf_op jit(solution)/shard_map/ppermute | solution.py:20
  9.3 0.7 %score.2 = (bf16[80,768]{1,0:T(8,128)(2,1)S(1)}, f32[64,768]{1,0:T(8,128)S(1)}, bf16[64,512]{1,0:T(8,128)(2,1)S(1)}, bf16[64,512]{1,0:T(8,128)(2,1)S(1)}, bf16[6...) custom-call(bf16[64,768]{1,0:T(8,128)(2,1)S(1)} %collective-permute-done.refs_0_, ...), custom_call_target="tpu_custom_call" | custom-call | flops 402653184 | bytes 4456448 | tf_op jit(solution)/shard_map/score/pallas_call | solution.py:268
  10.1 3.1 %collective-permute-start.3 = (bf16[80,768]{1,0:T(8,128)(2,1)S(1)}, bf16[80,768]{1,0:T(8,128)(2,1)S(1)}, u32[]{:S(2)}, u32[]{:S(2)}) collective-permute-start(bf16[80,768]{1,0:T(8,128)(2,1)S(1)} %get-tuple-element.33.refs_8_), channel_id=1, source_target_pairs={{0,6},{1,7},{2,4},{3,5},{4,2},{5,3},{6,0},{7,1},{8,14},{9,15},{10,... | collective-permute-start | bytes 368648 | tf_op jit(solution)/shard_map/ppermute | solution.py:20
  13.2 0.0 collective-permute-done.5.refs_1_.refs_3_
  13.2 0.0 collective-permute-done.4.refs_0_.refs_2_
  13.2 0.7 %score.3 = (bf16[64,768]{1,0:T(8,128)(2,1)S(1)}, bf16[64,768]{1,0:T(8,128)(2,1)S(1)}, bf16[64,512]{1,0:T(8,128)(2,1)S(1)}, bf16[64,512]{1,0:T(8,128)(2,1)S(1)}, ...) custom-call(bf16[64,768]{1,0:T(8,128)(2,1)S(1)} %collective-permute-done.4.refs_0_.refs_2_, ...), custom_call_target="tpu_custom_call" | custom-call | flops 402653184 | bytes 4456448 | tf_op jit(solution)/shard_map/score/pallas_call | solution.py:268
  13.9 0.5 %collective-permute-start.6 = (bf16[64,768]{1,0:T(8,128)(2,1)S(1)}, bf16[64,768]{1,0:T(8,128)(2,1)S(1)}, u32[]{:S(2)}, u32[]{:S(2)}) collective-permute-start(bf16[64,768]{1,0:T(8,128)(2,1)S(1)} %get-tuple-element.34), channel_id=1, source_target_pairs={{0,4},{1,5},{2,6},{3,7},{4,0},{5,1},{6,2},{7,3},{8,12},{9,13},{10,... | collective-permute-start | bytes 294920 | tf_op jit(solution)/shard_map/ppermute | solution.py:20
  14.4 0.1 collective-permute-start.7
  14.6 4.0 %collective-permute-done.6 = bf16[64,768]{1,0:T(8,128)(2,1)S(1)} collective-permute-done((bf16[64,768]{1,0:T(8,128)(2,1)S(1)}, bf16[64,768]{1,0:T(8,128)(2,1)S(1)}, u32[]{:S(2)}, u32[]{:S(2)}) %collective-permute-start.6) | collective-permute-done | bytes 98336 | tf_op jit(solution)/shard_map/ppermute | solution.py:20
  18.6 0.5 %collective-permute-done.7 = bf16[64,768]{1,0:T(8,128)(2,1)S(1)} collective-permute-done((bf16[64,768]{1,0:T(8,128)(2,1)S(1)}, bf16[64,768]{1,0:T(8,128)(2,1)S(1)}, u32[]{:S(2)}, u32[]{:S(2)}) %collective-permute-start.7) | collective-permute-done | bytes 98336 | tf_op jit(solution)/shard_map/ppermute | solution.py:20
  19.1 0.0 collective-permute-done.3
  19.1 1.6 %collective-permute-start.8 = (bf16[64,768]{1,0:T(8,128)(2,1)S(1)}, bf16[64,768]{1,0:T(8,128)(2,1)S(1)}, u32[]{:S(2)}, u32[]{:S(2)}) collective-permute-start(bf16[64,768]{1,0:T(8,128)(2,1)S(1)} %fusion), channel_id=1, source_target_pairs={{0,8},{1,17},{2,10},{3,19},{4,12},{5,21},{6,14},{7,23},{8,0},{9,25... | collective-permute-start | bytes 294920 | tf_op jit(solution)/shard_map/ppermute | solution.py:328
  20.8 0.1 join.1
  20.8 0.1 collective-permute-start.11
  20.9 0.5 %collective-permute-start.10 = (bf16[256,512]{1,0:T(8,128)(2,1)S(1)}, bf16[256,512]{1,0:T(8,128)(2,1)S(1)}, u32[]{:S(2)}, u32[]{:S(2)}) collective-permute-start(bf16[256,512]{1,0:T(8,128)(2,1)S(1)} %get-tuple-element.46), channel_id=1, source_target_pairs={{0,1},{1,0},{2,3},{3,2},{4,5},{5,4},{6,7},{7,6},{8,9},{9,8},{10,11... | collective-permute-start | bytes 786440 | tf_op jit(solution)/shard_map/ppermute | solution.py:20
  21.4 2.4 %collective-permute-done.8 = bf16[64,768]{1,0:T(8,128)(2,1)S(1)} collective-permute-done((bf16[64,768]{1,0:T(8,128)(2,1)S(1)}, bf16[64,768]{1,0:T(8,128)(2,1)S(1)}, u32[]{:S(2)}, u32[]{:S(2)}) %collective-permute-start.8) | collective-permute-done | bytes 98336 | tf_op jit(solution)/shard_map/ppermute | solution.py:328
  23.8 0.1 fusion.1
  23.9 2.6 %collective-permute-start.9 = (bf16[64,768]{1,0:T(8,128)(2,1)S(1)}, bf16[64,768]{1,0:T(8,128)(2,1)S(1)}, u32[]{:S(2)}, u32[]{:S(2)}) collective-permute-start(bf16[64,768]{1,0:T(8,128)(2,1)S(1)} %get-tuple-element.48), channel_id=1, source_target_pairs={{0,16},{1,9},{2,18},{3,11},{4,20},{5,13},{6,22},{7,15},{8,24},{9,1... | collective-permute-start | bytes 294920 | tf_op jit(solution)/shard_map/ppermute | solution.py:328
  26.5 0.0 collective-permute-done.10.d_other_ref
  26.5 0.0 collective-permute-done.11.c_other_ref
  26.5 1.7 %emb_grad.1.after_hbm = f32[512,768]{1,0:T(8,128)} custom-call(bf16[256,512]{1,0:T(8,128)(2,1)S(1)} %get-tuple-element.45.d_own_ref, bf16[256,512]{1,0:T(8,128)(2,1)S(1)} %collective-permute-done.10.d_other_ref, bf16[256,768]{1,0:T(8,128)(2,1)S(1)} %get-tuple-element.47.c_own_ref, bf16[256,768]{1,0:T(8,128)(2,1)S(1)} %collective-permute-done.11.c_other_ref, ...), custom_call_target="tpu_custom_call" | custom-call | flops 402653184 | bytes 2883584 | tf_op jit(solution)/shard_map/emb_grad/pallas_call | solution.py:334
  28.2 1.2 %collective-permute-done.9.received_ref = bf16[64,768]{1,0:T(8,128)(2,1)S(1)} collective-permute-done((bf16[64,768]{1,0:T(8,128)(2,1)S(1)}, bf16[64,768]{1,0:T(8,128)(2,1)S(1)}, u32[]{:S(2)}, u32[]{:S(2)}) %collective-permute-start.9) | collective-permute-done | bytes 98336 | tf_op jit(solution)/shard_map/ppermute | solution.py:328
  29.4 0.8 %finish.1 = f32[64,768]{1,0:T(8,128)} custom-call(f32[64,768]{1,0:T(8,128)S(1)} %get-tuple-element.49.after_ref.grad_ref, bf16[64,768]{1,0:T(8,128)(2,1)S(1)} %collective-permute-done.9.received_ref, f32[64,128]{1,0:T(8,128)S(1)} %get-tuple-element.36.column_ref, f32[512,768]{1,0:T(8,128)} %emb_grad.1.after_hbm), custom_call_target="tpu_custom_call" | custom-call | flops 49152 | bytes 491520 | tf_op jit(solution)/shard_map/finish/pallas_call | solution.py:344
  (1 shorter events, 0.0 us)
Async XLA Ops:
  0.6 5.8 %collective-permute-start.1 = (bf16[512,768]{1,0:T(8,128)(2,1)}, bf16[512,768]{1,0:T(8,128)(2,1)S(1)}, u32[]{:S(2)}, u32[]{:S(2)}) collective-permute-start(bf16[512,768]{1,0:T(8,128)(2,1)} %emb_hbm.1), channel_id=1, source_target_pairs={{0,1},{1,0},{2,3},{3,2},{4,5},{5,4},{6,7},{7,6},{8,9},{9,8},{10,11... | collective-permute-start | bytes 2359304 | tf_op jit(solution)/shard_map/ppermute | solution.py:20
  2.3 7.0 %collective-permute-start = (bf16[64,768]{1,0:T(8,128)(2,1)S(1)}, bf16[64,768]{1,0:T(8,128)(2,1)S(1)}, u32[]{:S(2)}, u32[]{:S(2)}) collective-permute-start(bf16[64,768]{1,0:T(8,128)(2,1)S(1)} %get-tuple-element.25.refs_1_), channel_id=1, source_target_pairs={{0,6},{1,7},{2,4},{3,5},{4,2},{5,3},{6,0},{7,1},{8,14},{9,15},{10,... | collective-permute-start | bytes 294920 | tf_op jit(solution)/shard_map/ppermute | solution.py:20
  5.8 7.3 %collective-permute-start.5 = (bf16[64,768]{1,0:T(8,128)(2,1)S(1)}, bf16[64,768]{1,0:T(8,128)(2,1)S(1)}, u32[]{:S(2)}, u32[]{:S(2)}) collective-permute-start(bf16[64,768]{1,0:T(8,128)(2,1)S(1)} %get-tuple-element.25.refs_1_), channel_id=1, source_target_pairs={{0,4},{1,5},{2,6},{3,7},{4,0},{5,1},{6,2},{7,3},{8,12},{9,13},{10,... | collective-permute-start | bytes 294920 | tf_op jit(solution)/shard_map/ppermute | solution.py:20
  6.3 6.8 %collective-permute-start.4 = (bf16[64,768]{1,0:T(8,128)(2,1)S(1)}, bf16[64,768]{1,0:T(8,128)(2,1)S(1)}, u32[]{:S(2)}, u32[]{:S(2)}) collective-permute-start(bf16[64,768]{1,0:T(8,128)(2,1)S(1)} %get-tuple-element.25.refs_1_), channel_id=1, source_target_pairs={{0,2},{1,3},{2,0},{3,1},{4,6},{5,7},{6,4},{7,5},{8,10},{9,11},{10,... | collective-permute-start | bytes 294920 | tf_op jit(solution)/shard_map/ppermute | solution.py:20
  6.5 1.4 %collective-permute-start.2 = (bf16[40,512]{1,0:T(8,128)(2,1)S(1)}, bf16[40,512]{1,0:T(8,128)(2,1)S(1)}, u32[]{:S(2)}, u32[]{:S(2)}) collective-permute-start(bf16[40,512]{1,0:T(8,128)(2,1)S(1)} %get-tuple-element.29.index_own_ref), channel_id=1, source_target_pairs={{0,1},{1,0},{2,3},{3,2},{4,5},{5,4},{6,7},{7,6},{8,9},{9,8},{10,11... | collective-permute-start | bytes 122888 | tf_op jit(solution)/shard_map/ppermute | solution.py:20
  10.1 9.0 %collective-permute-start.3 = (bf16[80,768]{1,0:T(8,128)(2,1)S(1)}, bf16[80,768]{1,0:T(8,128)(2,1)S(1)}, u32[]{:S(2)}, u32[]{:S(2)}) collective-permute-start(bf16[80,768]{1,0:T(8,128)(2,1)S(1)} %get-tuple-element.33.refs_8_), channel_id=1, source_target_pairs={{0,6},{1,7},{2,4},{3,5},{4,2},{5,3},{6,0},{7,1},{8,14},{9,15},{10,... | collective-permute-start | bytes 368648 | tf_op jit(solution)/shard_map/ppermute | solution.py:20
  13.9 4.7 %collective-permute-start.6 = (bf16[64,768]{1,0:T(8,128)(2,1)S(1)}, bf16[64,768]{1,0:T(8,128)(2,1)S(1)}, u32[]{:S(2)}, u32[]{:S(2)}) collective-permute-start(bf16[64,768]{1,0:T(8,128)(2,1)S(1)} %get-tuple-element.34), channel_id=1, source_target_pairs={{0,4},{1,5},{2,6},{3,7},{4,0},{5,1},{6,2},{7,3},{8,12},{9,13},{10,... | collective-permute-start | bytes 294920 | tf_op jit(solution)/shard_map/ppermute | solution.py:20
  14.4 4.6 %collective-permute-start.7 = (bf16[64,768]{1,0:T(8,128)(2,1)S(1)}, bf16[64,768]{1,0:T(8,128)(2,1)S(1)}, u32[]{:S(2)}, u32[]{:S(2)}) collective-permute-start(bf16[64,768]{1,0:T(8,128)(2,1)S(1)} %get-tuple-element.35), channel_id=1, source_target_pairs={{0,2},{1,3},{2,0},{3,1},{4,6},{5,7},{6,4},{7,5},{8,10},{9,11},{10,... | collective-permute-start | bytes 294920 | tf_op jit(solution)/shard_map/ppermute | solution.py:20
  19.1 4.7 %collective-permute-start.8 = (bf16[64,768]{1,0:T(8,128)(2,1)S(1)}, bf16[64,768]{1,0:T(8,128)(2,1)S(1)}, u32[]{:S(2)}, u32[]{:S(2)}) collective-permute-start(bf16[64,768]{1,0:T(8,128)(2,1)S(1)} %fusion), channel_id=1, source_target_pairs={{0,8},{1,17},{2,10},{3,19},{4,12},{5,21},{6,14},{7,23},{8,0},{9,25... | collective-permute-start | bytes 294920 | tf_op jit(solution)/shard_map/ppermute | solution.py:328
  20.8 5.7 %collective-permute-start.11 = (bf16[256,768]{1,0:T(8,128)(2,1)S(1)}, bf16[256,768]{1,0:T(8,128)(2,1)S(1)}, u32[]{:S(2)}, u32[]{:S(2)}) collective-permute-start(bf16[256,768]{1,0:T(8,128)(2,1)S(1)} %get-tuple-element.47.c_own_ref), channel_id=1, source_target_pairs={{0,1},{1,0},{2,3},{3,2},{4,5},{5,4},{6,7},{7,6},{8,9},{9,8},{10,11... | collective-permute-start | bytes 1179656 | tf_op jit(solution)/shard_map/ppermute | solution.py:20
  20.9 5.6 %collective-permute-start.10 = (bf16[256,512]{1,0:T(8,128)(2,1)S(1)}, bf16[256,512]{1,0:T(8,128)(2,1)S(1)}, u32[]{:S(2)}, u32[]{:S(2)}) collective-permute-start(bf16[256,512]{1,0:T(8,128)(2,1)S(1)} %get-tuple-element.46), channel_id=1, source_target_pairs={{0,1},{1,0},{2,3},{3,2},{4,5},{5,4},{6,7},{7,6},{8,9},{9,8},{10,11... | collective-permute-start | bytes 786440 | tf_op jit(solution)/shard_map/ppermute | solution.py:20
  23.9 5.6 %collective-permute-start.9 = (bf16[64,768]{1,0:T(8,128)(2,1)S(1)}, bf16[64,768]{1,0:T(8,128)(2,1)S(1)}, u32[]{:S(2)}, u32[]{:S(2)}) collective-permute-start(bf16[64,768]{1,0:T(8,128)(2,1)S(1)} %get-tuple-element.48), channel_id=1, source_target_pairs={{0,16},{1,9},{2,18},{3,11},{4,20},{5,13},{6,22},{7,15},{8,24},{9,1... | collective-permute-start | bytes 294920 | tf_op jit(solution)/shard_map/ppermute | solution.py:328

commit v10 on v8

--- a/solution.py
+++ b/solution.py
@@ -316,9 +316,14 @@
         grad = grads[0]
     d_other, classifier_other = flip(d_theirs, "lab", 1), flip(classifier_own, "lab", 1)
     bits = [1 << bit for bit in range(enc.bit_length() - 1)]
-    for bit in bits[:-1]:
-        grad = grad + flip(grad.astype(BF16), "enc", bit).astype(F32)
-    received = flip(grad.astype(BF16), "enc", bits[-1])
+
+    def along(value, even, odd):
+        pairs = [(i, i ^ lab * (odd if i & 1 else even)) for i in range(enc * lab)]
+        return lax.ppermute(value, ("enc", "lab"), pairs)
+
+    for even, odd in list(zip(bits, reversed(bits)))[:-1]:
+        grad = grad + along(grad.astype(BF16), even, odd).astype(F32)
+    received = along(grad.astype(BF16), bits[-1], bits[0])
 
     emb_grad = pl.pallas_call(
         emb_kernel,

time: 30.3 us -> 30.3 us (level)
    ppermute x12 -> x10, starting transfers between devices: 14.2 us -> 9.7 us  [flip(): lax.ppermute(value, axis, [(i, i ^ mask) for i in range(lax.axis_size(axi...]
    ppermute x0 -> x2, starting transfers between devices: none -> 4.3 us  [along(): return lax.ppermute(value, ('enc', 'lab'), pairs)]
    ppermute x0 -> x2, waiting for transfers between devices: none -> 3.59 us  [along(): return lax.ppermute(value, ('enc', 'lab'), pairs)]
    ppermute x12 -> x10, waiting for transfers between devices: 7.66 us -> 4.28 us  [flip(): lax.ppermute(value, axis, [(i, i ^ mask) for i in range(lax.axis_size(axi...]
where the time goes in v10:
time: 30.3 us; the launch traced here: 30.1 us
  starting transfers between devices  14 us (46%)
  waiting for transfers between devices  7.86 us (26%)
  Pallas kernels  7.37 us (24%)
  between operations  0.72 us (2%)
    ppermute x10, starting transfers between devices, flip(): lax.ppermute(value, axis, [(i, i ^ mask) for i in range(lax.axis_size(axi...  9.7 us
    ppermute x2, starting transfers between devices, along(): return lax.ppermute(value, ('enc', 'lab'), pairs)  4.3 us
    ppermute x10, waiting for transfers between devices, flip(): lax.ppermute(value, axis, [(i, i ^ mask) for i in range(lax.axis_size(axi...  4.28 us
    ppermute x2, waiting for transfers between devices, along(): return lax.ppermute(value, ('enc', 'lab'), pairs)  3.59 us
    pallas_call x1, Pallas kernels, shards(): pl.pallas_call(emb_kernel, out_shape=jax.ShapeDtypeStruct((docs, width),...  1.74 us
    pallas_call x2, Pallas kernels, score(): pl.pallas_call(functools.partial(score_kernel, which=which, after=len(aft...  1.44 us
    pallas_call x1, Pallas kernels, shards(): pl.pallas_call(turn_kernel, out_shape=[jax.ShapeDtypeStruct((docs, width)...  1.41 us
    pallas_call x1, Pallas kernels, shards(): pl.pallas_call(functools.partial(pack_kernel, scale=1.0 / math.sqrt(docs...  1.15 us
  transfers between devices with their start and end apart: 12, of which 5 were waited for; matrix products, arithmetic and copies ran while one was open for 0% of the time, Pallas kernels for 22%

profile of v10, /device:TPU:0, one launch (start us, length us, event | category | flops | bytes accessed | tf_op | source)
XLA Modules:
  0.0 30.1 jit_solution(18070429206905177037)
XLA Ops:
  0.6 0.5 %collective-permute-start.1 = (bf16[512,768]{1,0:T(8,128)(2,1)}, bf16[512,768]{1,0:T(8,128)(2,1)S(1)}, u32[]{:S(2)}, u32[]{:S(2)}) collective-permute-start(bf16[512,768]{1,0:T(8,128)(2,1)} %emb_hbm.1), channel_id=1, source_target_pairs={{0,1},{1,0},{2,3},{3,2},{4,5},{5,4},{6,7},{7,6},{8,9},{9,8},{10,11... | collective-permute-start | bytes 2359304 | tf_op jit(solution)/shard_map/ppermute | solution.py:20
  1.1 1.1 %pack.1 = (bf16[64,768]{1,0:T(8,128)(2,1)S(1)}, f32[64,128]{1,0:T(8,128)S(1)}, bf16[40,512]{1,0:T(8,128)(2,1)S(1)}) custom-call(f32[64,768]{1,0:T(8,128)} %classifier_hbm.1, s32[1,64]{1,0:T(1,128)} %bitcast.9, s32[4,512]{1,0:T(4,128)} %bitcast.6, s32[4,512]{1,0:T(4,128)} %bitcast.7, s32[4,512]{1,0:T(4,128)} %bitcast.8, s32[4,8,512]{2,1,0:T(8,128)} %bitcast.5), custom_call_target="tpu_custom_call" | custom-call | flops 49152 | bytes 376832 | tf_op jit(solution)/shard_map/pack/pallas_call | solution.py:211
  2.3 3.5 %collective-permute-start = (bf16[64,768]{1,0:T(8,128)(2,1)S(1)}, bf16[64,768]{1,0:T(8,128)(2,1)S(1)}, u32[]{:S(2)}, u32[]{:S(2)}) collective-permute-start(bf16[64,768]{1,0:T(8,128)(2,1)S(1)} %get-tuple-element.25.refs_1_), channel_id=1, source_target_pairs={{0,6},{1,7},{2,4},{3,5},{4,2},{5,3},{6,0},{7,1},{8,14},{9,15},{10,... | collective-permute-start | bytes 294920 | tf_op jit(solution)/shard_map/ppermute | solution.py:20
  5.8 0.2 collective-permute-start.2
  6.0 0.5 %collective-permute-start.5 = (bf16[64,768]{1,0:T(8,128)(2,1)S(1)}, bf16[64,768]{1,0:T(8,128)(2,1)S(1)}, u32[]{:S(2)}, u32[]{:S(2)}) collective-permute-start(bf16[64,768]{1,0:T(8,128)(2,1)S(1)} %get-tuple-element.25.refs_1_), channel_id=1, source_target_pairs={{0,4},{1,5},{2,6},{3,7},{4,0},{5,1},{6,2},{7,3},{8,12},{9,13},{10,... | collective-permute-start | bytes 294920 | tf_op jit(solution)/shard_map/ppermute | solution.py:20
  6.5 0.4 %collective-permute-start.4 = (bf16[64,768]{1,0:T(8,128)(2,1)S(1)}, bf16[64,768]{1,0:T(8,128)(2,1)S(1)}, u32[]{:S(2)}, u32[]{:S(2)}) collective-permute-start(bf16[64,768]{1,0:T(8,128)(2,1)S(1)} %get-tuple-element.25.refs_1_), channel_id=1, source_target_pairs={{0,2},{1,3},{2,0},{3,1},{4,6},{5,7},{6,4},{7,5},{8,10},{9,11},{10,... | collective-permute-start | bytes 294920 | tf_op jit(solution)/shard_map/ppermute | solution.py:20
  7.0 0.0 collective-permute-done.1.other_ref.refs_3_
  7.0 1.4 %turn.1 = (bf16[512,768]{1,0:T(8,128)(2,1)S(1)}, bf16[768,512]{1,0:T(8,128)(2,1)S(1)}, bf16[768,512]{1,0:T(8,128)(2,1)S(1)}) custom-call(bf16[512,768]{1,0:T(8,128)(2,1)} %emb_hbm.1, bf16[512,768]{1,0:T(8,128)(2,1)S(1)} %collective-permute-done.1.other_ref.refs_3_), custom_call_target="tpu_custom_call" | custom-call | flops 393216 | bytes 3932160 | tf_op jit(solution)/shard_map/turn/pallas_call | solution.py:239
  8.4 0.0 collective-permute-done.2.index_other_ref
  8.4 0.8 %targets.1 = (bf16[256,512]{1,0:T(8,128)(2,1)S(1)}, bf16[256,512]{1,0:T(8,128)(2,1)S(1)}) custom-call(bf16[40,512]{1,0:T(8,128)(2,1)S(1)} %get-tuple-element.29.index_own_ref, bf16[40,512]{1,0:T(8,128)(2,1)S(1)} %collective-permute-done.2.index_other_ref, bf16[768,512]{1,0:T(8,128)(2,1)S(1)} %get-tuple-element.28.after_ref.refs_5_), custom_call_target="tpu_custom_call" | custom-call | flops 10485760 | bytes 688128 | tf_op jit(solution)/shard_map/targets/pallas_call | solution.py:250
  9.2 0.1 collective-permute-done.refs_0_
  9.3 0.7 %score.2 = (bf16[64,768]{1,0:T(8,128)(2,1)S(1)}, f32[64,768]{1,0:T(8,128)S(1)}, bf16[64,512]{1,0:T(8,128)(2,1)S(1)}, bf16[64,512]{1,0:T(8,128)(2,1)S(1)}, bf16[6...) custom-call(bf16[64,768]{1,0:T(8,128)(2,1)S(1)} %collective-permute-done.refs_0_, ...), custom_call_target="tpu_custom_call" | custom-call | flops 402653184 | bytes 4456448 | tf_op jit(solution)/shard_map/score/pallas_call | solution.py:265
  10.1 3.1 %collective-permute-start.3 = (bf16[65,768]{1,0:T(8,128)(2,1)S(1)}, bf16[65,768]{1,0:T(8,128)(2,1)S(1)}, u32[]{:S(2)}, u32[]{:S(2)}) collective-permute-start(bf16[65,768]{1,0:T(8,128)(2,1)S(1)} %pad_maximum_fusion), channel_id=1, source_target_pairs={{0,6},{1,7},{2,4},{3,5},{4,2},{5,3},{6,0},{7,1},{8,14},{9,15},{10,... | collective-permute-start | bytes 299528 | tf_op jit(solution)/shard_map/ppermute | solution.py:20
  13.2 0.0 collective-permute-done.5.refs_1_.refs_3_
  13.2 0.0 collective-permute-done.4.refs_0_.refs_2_
  13.2 0.7 %score.3 = (bf16[64,768]{1,0:T(8,128)(2,1)S(1)}, bf16[64,768]{1,0:T(8,128)(2,1)S(1)}, bf16[64,512]{1,0:T(8,128)(2,1)S(1)}, bf16[64,512]{1,0:T(8,128)(2,1)S(1)}, ...) custom-call(bf16[64,768]{1,0:T(8,128)(2,1)S(1)} %collective-permute-done.4.refs_0_.refs_2_, ...), custom_call_target="tpu_custom_call" | custom-call | flops 402653184 | bytes 4456448 | tf_op jit(solution)/shard_map/score/pallas_call | solution.py:265
  13.9 0.4 %collective-permute-start.6 = (bf16[64,768]{1,0:T(8,128)(2,1)S(1)}, bf16[64,768]{1,0:T(8,128)(2,1)S(1)}, u32[]{:S(2)}, u32[]{:S(2)}) collective-permute-start(bf16[64,768]{1,0:T(8,128)(2,1)S(1)} %get-tuple-element.34), channel_id=1, source_target_pairs={{0,4},{1,5},{2,6},{3,7},{4,0},{5,1},{6,2},{7,3},{8,12},{9,13},{10,... | collective-permute-start | bytes 294920 | tf_op jit(solution)/shard_map/ppermute | solution.py:20
  14.3 0.5 %collective-permute-start.7 = (bf16[64,768]{1,0:T(8,128)(2,1)S(1)}, bf16[64,768]{1,0:T(8,128)(2,1)S(1)}, u32[]{:S(2)}, u32[]{:S(2)}) collective-permute-start(bf16[64,768]{1,0:T(8,128)(2,1)S(1)} %get-tuple-element.35), channel_id=1, source_target_pairs={{0,2},{1,3},{2,0},{3,1},{4,6},{5,7},{6,4},{7,5},{8,10},{9,11},{10,... | collective-permute-start | bytes 294920 | tf_op jit(solution)/shard_map/ppermute | solution.py:20
  14.8 3.9 %collective-permute-done.6 = bf16[64,768]{1,0:T(8,128)(2,1)S(1)} collective-permute-done((bf16[64,768]{1,0:T(8,128)(2,1)S(1)}, bf16[64,768]{1,0:T(8,128)(2,1)S(1)}, u32[]{:S(2)}, u32[]{:S(2)}) %collective-permute-start.6) | collective-permute-done | bytes 98336 | tf_op jit(solution)/shard_map/ppermute | solution.py:20
  18.6 0.3 %collective-permute-done.7 = bf16[64,768]{1,0:T(8,128)(2,1)S(1)} collective-permute-done((bf16[64,768]{1,0:T(8,128)(2,1)S(1)}, bf16[64,768]{1,0:T(8,128)(2,1)S(1)}, u32[]{:S(2)}, u32[]{:S(2)}) %collective-permute-start.7) | collective-permute-done | bytes 98336 | tf_op jit(solution)/shard_map/ppermute | solution.py:20
  18.9 0.0 collective-permute-done.3
  19.0 1.6 %collective-permute-start.8 = (bf16[64,768]{1,0:T(8,128)(2,1)S(1)}, bf16[64,768]{1,0:T(8,128)(2,1)S(1)}, u32[]{:S(2)}, u32[]{:S(2)}) collective-permute-start(bf16[64,768]{1,0:T(8,128)(2,1)S(1)} %fusion), channel_id=1, source_target_pairs={{0,8},{1,17},{2,10},{3,19},{4,12},{5,21},{6,14},{7,23},{8,0},{9,25... | collective-permute-start | bytes 294920 | tf_op jit(solution)/shard_map/ppermute | solution.py:322
  20.6 0.1 join.1
  20.7 0.1 collective-permute-start.11
  20.8 0.5 %collective-permute-start.10 = (bf16[256,512]{1,0:T(8,128)(2,1)S(1)}, bf16[256,512]{1,0:T(8,128)(2,1)S(1)}, u32[]{:S(2)}, u32[]{:S(2)}) collective-permute-start(bf16[256,512]{1,0:T(8,128)(2,1)S(1)} %get-tuple-element.46), channel_id=1, source_target_pairs={{0,1},{1,0},{2,3},{3,2},{4,5},{5,4},{6,7},{7,6},{8,9},{9,8},{10,11... | collective-permute-start | bytes 786440 | tf_op jit(solution)/shard_map/ppermute | solution.py:20
  21.3 2.4 %collective-permute-done.8 = bf16[64,768]{1,0:T(8,128)(2,1)S(1)} collective-permute-done((bf16[64,768]{1,0:T(8,128)(2,1)S(1)}, bf16[64,768]{1,0:T(8,128)(2,1)S(1)}, u32[]{:S(2)}, u32[]{:S(2)}) %collective-permute-start.8) | collective-permute-done | bytes 98336 | tf_op jit(solution)/shard_map/ppermute | solution.py:322
  23.7 0.1 fusion.1
  23.7 2.7 %collective-permute-start.9 = (bf16[64,768]{1,0:T(8,128)(2,1)S(1)}, bf16[64,768]{1,0:T(8,128)(2,1)S(1)}, u32[]{:S(2)}, u32[]{:S(2)}) collective-permute-start(bf16[64,768]{1,0:T(8,128)(2,1)S(1)} %get-tuple-element.48), channel_id=1, source_target_pairs={{0,16},{1,9},{2,18},{3,11},{4,20},{5,13},{6,22},{7,15},{8,24},{9,1... | collective-permute-start | bytes 294920 | tf_op jit(solution)/shard_map/ppermute | solution.py:322
  26.4 0.0 collective-permute-done.10.d_other_ref
  26.4 0.0 collective-permute-done.11.c_other_ref
  26.4 1.7 %emb_grad.1.after_hbm = f32[512,768]{1,0:T(8,128)} custom-call(bf16[256,512]{1,0:T(8,128)(2,1)S(1)} %get-tuple-element.45.d_own_ref, bf16[256,512]{1,0:T(8,128)(2,1)S(1)} %collective-permute-done.10.d_other_ref, bf16[256,768]{1,0:T(8,128)(2,1)S(1)} %get-tuple-element.47.c_own_ref, bf16[256,768]{1,0:T(8,128)(2,1)S(1)} %collective-permute-done.11.c_other_ref, ...), custom_call_target="tpu_custom_call" | custom-call | flops 402653184 | bytes 2883584 | tf_op jit(solution)/shard_map/emb_grad/pallas_call | solution.py:328
  28.1 1.2 %collective-permute-done.9.received_ref = bf16[64,768]{1,0:T(8,128)(2,1)S(1)} collective-permute-done((bf16[64,768]{1,0:T(8,128)(2,1)S(1)}, bf16[64,768]{1,0:T(8,128)(2,1)S(1)}, u32[]{:S(2)}, u32[]{:S(2)}) %collective-permute-start.9) | collective-permute-done | bytes 98336 | tf_op jit(solution)/shard_map/ppermute | solution.py:322
  29.3 0.8 %finish.1 = f32[64,768]{1,0:T(8,128)} custom-call(f32[64,768]{1,0:T(8,128)S(1)} %get-tuple-element.49.after_ref.grad_ref, bf16[64,768]{1,0:T(8,128)(2,1)S(1)} %collective-permute-done.9.received_ref, f32[64,128]{1,0:T(8,128)S(1)} %get-tuple-element.36.column_ref, f32[512,768]{1,0:T(8,128)} %emb_grad.1.after_hbm), custom_call_target="tpu_custom_call" | custom-call | flops 49152 | bytes 491520 | tf_op jit(solution)/shard_map/finish/pallas_call | solution.py:338
  (3 shorter events, 0.1 us)
Async XLA Ops:
  0.6 6.3 %collective-permute-start.1 = (bf16[512,768]{1,0:T(8,128)(2,1)}, bf16[512,768]{1,0:T(8,128)(2,1)S(1)}, u32[]{:S(2)}, u32[]{:S(2)}) collective-permute-start(bf16[512,768]{1,0:T(8,128)(2,1)} %emb_hbm.1), channel_id=1, source_target_pairs={{0,1},{1,0},{2,3},{3,2},{4,5},{5,4},{6,7},{7,6},{8,9},{9,8},{10,11... | collective-permute-start | bytes 2359304 | tf_op jit(solution)/shard_map/ppermute | solution.py:20
  2.3 7.0 %collective-permute-start = (bf16[64,768]{1,0:T(8,128)(2,1)S(1)}, bf16[64,768]{1,0:T(8,128)(2,1)S(1)}, u32[]{:S(2)}, u32[]{:S(2)}) collective-permute-start(bf16[64,768]{1,0:T(8,128)(2,1)S(1)} %get-tuple-element.25.refs_1_), channel_id=1, source_target_pairs={{0,6},{1,7},{2,4},{3,5},{4,2},{5,3},{6,0},{7,1},{8,14},{9,15},{10,... | collective-permute-start | bytes 294920 | tf_op jit(solution)/shard_map/ppermute | solution.py:20
  5.8 2.6 %collective-permute-start.2 = (bf16[40,512]{1,0:T(8,128)(2,1)S(1)}, bf16[40,512]{1,0:T(8,128)(2,1)S(1)}, u32[]{:S(2)}, u32[]{:S(2)}) collective-permute-start(bf16[40,512]{1,0:T(8,128)(2,1)S(1)} %get-tuple-element.29.index_own_ref), channel_id=1, source_target_pairs={{0,1},{1,0},{2,3},{3,2},{4,5},{5,4},{6,7},{7,6},{8,9},{9,8},{10,11... | collective-permute-start | bytes 122888 | tf_op jit(solution)/shard_map/ppermute | solution.py:20
  6.0 7.2 %collective-permute-start.5 = (bf16[64,768]{1,0:T(8,128)(2,1)S(1)}, bf16[64,768]{1,0:T(8,128)(2,1)S(1)}, u32[]{:S(2)}, u32[]{:S(2)}) collective-permute-start(bf16[64,768]{1,0:T(8,128)(2,1)S(1)} %get-tuple-element.25.refs_1_), channel_id=1, source_target_pairs={{0,4},{1,5},{2,6},{3,7},{4,0},{5,1},{6,2},{7,3},{8,12},{9,13},{10,... | collective-permute-start | bytes 294920 | tf_op jit(solution)/shard_map/ppermute | solution.py:20
  6.5 6.7 %collective-permute-start.4 = (bf16[64,768]{1,0:T(8,128)(2,1)S(1)}, bf16[64,768]{1,0:T(8,128)(2,1)S(1)}, u32[]{:S(2)}, u32[]{:S(2)}) collective-permute-start(bf16[64,768]{1,0:T(8,128)(2,1)S(1)} %get-tuple-element.25.refs_1_), channel_id=1, source_target_pairs={{0,2},{1,3},{2,0},{3,1},{4,6},{5,7},{6,4},{7,5},{8,10},{9,11},{10,... | collective-permute-start | bytes 294920 | tf_op jit(solution)/shard_map/ppermute | solution.py:20
  10.1 8.9 %collective-permute-start.3 = (bf16[65,768]{1,0:T(8,128)(2,1)S(1)}, bf16[65,768]{1,0:T(8,128)(2,1)S(1)}, u32[]{:S(2)}, u32[]{:S(2)}) collective-permute-start(bf16[65,768]{1,0:T(8,128)(2,1)S(1)} %pad_maximum_fusion), channel_id=1, source_target_pairs={{0,6},{1,7},{2,4},{3,5},{4,2},{5,3},{6,0},{7,1},{8,14},{9,15},{10,... | collective-permute-start | bytes 299528 | tf_op jit(solution)/shard_map/ppermute | solution.py:20
  13.9 4.7 %collective-permute-start.6 = (bf16[64,768]{1,0:T(8,128)(2,1)S(1)}, bf16[64,768]{1,0:T(8,128)(2,1)S(1)}, u32[]{:S(2)}, u32[]{:S(2)}) collective-permute-start(bf16[64,768]{1,0:T(8,128)(2,1)S(1)} %get-tuple-element.34), channel_id=1, source_target_pairs={{0,4},{1,5},{2,6},{3,7},{4,0},{5,1},{6,2},{7,3},{8,12},{9,13},{10,... | collective-permute-start | bytes 294920 | tf_op jit(solution)/shard_map/ppermute | solution.py:20
  14.3 4.6 %collective-permute-start.7 = (bf16[64,768]{1,0:T(8,128)(2,1)S(1)}, bf16[64,768]{1,0:T(8,128)(2,1)S(1)}, u32[]{:S(2)}, u32[]{:S(2)}) collective-permute-start(bf16[64,768]{1,0:T(8,128)(2,1)S(1)} %get-tuple-element.35), channel_id=1, source_target_pairs={{0,2},{1,3},{2,0},{3,1},{4,6},{5,7},{6,4},{7,5},{8,10},{9,11},{10,... | collective-permute-start | bytes 294920 | tf_op jit(solution)/shard_map/ppermute | solution.py:20
  19.0 4.7 %collective-permute-start.8 = (bf16[64,768]{1,0:T(8,128)(2,1)S(1)}, bf16[64,768]{1,0:T(8,128)(2,1)S(1)}, u32[]{:S(2)}, u32[]{:S(2)}) collective-permute-start(bf16[64,768]{1,0:T(8,128)(2,1)S(1)} %fusion), channel_id=1, source_target_pairs={{0,8},{1,17},{2,10},{3,19},{4,12},{5,21},{6,14},{7,23},{8,0},{9,25... | collective-permute-start | bytes 294920 | tf_op jit(solution)/shard_map/ppermute | solution.py:322
  20.7 5.7 %collective-permute-start.11 = (bf16[256,768]{1,0:T(8,128)(2,1)S(1)}, bf16[256,768]{1,0:T(8,128)(2,1)S(1)}, u32[]{:S(2)}, u32[]{:S(2)}) collective-permute-start(bf16[256,768]{1,0:T(8,128)(2,1)S(1)} %get-tuple-element.47.c_own_ref), channel_id=1, source_target_pairs={{0,1},{1,0},{2,3},{3,2},{4,5},{5,4},{6,7},{7,6},{8,9},{9,8},{10,11... | collective-permute-start | bytes 1179656 | tf_op jit(solution)/shard_map/ppermute | solution.py:20
  20.8 5.6 %collective-permute-start.10 = (bf16[256,512]{1,0:T(8,128)(2,1)S(1)}, bf16[256,512]{1,0:T(8,128)(2,1)S(1)}, u32[]{:S(2)}, u32[]{:S(2)}) collective-permute-start(bf16[256,512]{1,0:T(8,128)(2,1)S(1)} %get-tuple-element.46), channel_id=1, source_target_pairs={{0,1},{1,0},{2,3},{3,2},{4,5},{5,4},{6,7},{7,6},{8,9},{9,8},{10,11... | collective-permute-start | bytes 786440 | tf_op jit(solution)/shard_map/ppermute | solution.py:20
  23.7 5.6 %collective-permute-start.9 = (bf16[64,768]{1,0:T(8,128)(2,1)S(1)}, bf16[64,768]{1,0:T(8,128)(2,1)S(1)}, u32[]{:S(2)}, u32[]{:S(2)}) collective-permute-start(bf16[64,768]{1,0:T(8,128)(2,1)S(1)} %get-tuple-element.48), channel_id=1, source_target_pairs={{0,16},{1,9},{2,18},{3,11},{4,20},{5,13},{6,22},{7,15},{8,24},{9,1... | collective-permute-start | bytes 294920 | tf_op jit(solution)/shard_map/ppermute | solution.py:322

commit v11 on v9

--- a/solution.py
+++ b/solution.py
@@ -322,14 +322,9 @@
         grad = grads[0]
     d_other, classifier_other = flip(d_theirs, "lab", 1), flip(classifier_own, "lab", 1)
     bits = [1 << bit for bit in range(enc.bit_length() - 1)]
-
-    def along(value, even, odd):
-        pairs = [(i, i ^ lab * (odd if i & 1 else even)) for i in range(enc * lab)]
-        return lax.ppermute(value, ("enc", "lab"), pairs)
-
-    for even, odd in list(zip(bits, reversed(bits)))[:-1]:
-        grad = grad + along(grad.astype(BF16), even, odd).astype(F32)
-    received = along(grad.astype(BF16), bits[-1], bits[0])
+    for bit in bits[:-1]:
+        grad = grad + flip(grad.astype(BF16), "enc", bit).astype(F32)
+    received = flip(grad.astype(BF16), "enc", bits[-1])
 
     emb_grad = pl.pallas_call(
         emb_kernel,

time: 30.4 us -> 30.4 us (level)
    ppermute x10 -> x12, starting transfers between devices: 9.01 us -> 13.3 us  [flip(): lax.ppermute(value, axis, [(i, i ^ mask) for i in range(lax.axis_size(axi...]
    ppermute x2 -> x0, starting transfers between devices: 4.29 us -> none  [along(): return lax.ppermute(value, ('enc', 'lab'), pairs)]
    ppermute x10 -> x12, waiting for transfers between devices: 5.11 us -> 8.7 us  [flip(): lax.ppermute(value, axis, [(i, i ^ mask) for i in range(lax.axis_size(axi...]
    ppermute x2 -> x0, waiting for transfers between devices: 3.58 us -> none  [along(): return lax.ppermute(value, ('enc', 'lab'), pairs)]
where the time goes in v11:
time: 30.4 us; the launch traced here: 30.2 us
  starting transfers between devices  13.3 us (44%)
  waiting for transfers between devices  8.7 us (29%)
  Pallas kernels  7.39 us (24%)
  between operations  0.71 us (2%)
    ppermute x12, starting transfers between devices, flip(): lax.ppermute(value, axis, [(i, i ^ mask) for i in range(lax.axis_size(axi...  13.3 us
    ppermute x12, waiting for transfers between devices, flip(): lax.ppermute(value, axis, [(i, i ^ mask) for i in range(lax.axis_size(axi...  8.7 us
    pallas_call x1, Pallas kernels, shards(): pl.pallas_call(emb_kernel, out_shape=jax.ShapeDtypeStruct((docs, width),...  1.74 us
    pallas_call x2, Pallas kernels, score(): pl.pallas_call(functools.partial(score_kernel, which=which, after=len(aft...  1.46 us
    pallas_call x1, Pallas kernels, shards(): pl.pallas_call(turn_kernel, out_shape=[jax.ShapeDtypeStruct((docs, width)...  1.41 us
    pallas_call x1, Pallas kernels, shards(): pl.pallas_call(functools.partial(pack_kernel, scale=1.0 / math.sqrt(docs...  1.15 us
    pallas_call x1, Pallas kernels, shards(): pl.pallas_call(functools.partial(targets_kernel, panel=panel, slots=slots...  0.82 us
    pallas_call x1, Pallas kernels, shards(): pl.pallas_call(finish_kernel, out_shape=jax.ShapeDtypeStruct((panel, widt...  0.76 us
  transfers between devices with their start and end apart: 12, of which 5 were waited for; matrix products, arithmetic and copies ran while one was open for 0% of the time, Pallas kernels for 22%

profile of v11, /device:TPU:0, one launch (start us, length us, event | category | flops | bytes accessed | tf_op | source)
XLA Modules:
  0.0 30.2 jit_solution(17981637972443035873)
XLA Ops:
  0.6 0.5 %collective-permute-start.1 = (bf16[512,768]{1,0:T(8,128)(2,1)}, bf16[512,768]{1,0:T(8,128)(2,1)S(1)}, u32[]{:S(2)}, u32[]{:S(2)}) collective-permute-start(bf16[512,768]{1,0:T(8,128)(2,1)} %emb_hbm.1), channel_id=1, source_target_pairs={{0,1},{1,0},{2,3},{3,2},{4,5},{5,4},{6,7},{7,6},{8,9},{9,8},{10,11... | collective-permute-start | bytes 2359304 | tf_op jit(solution)/shard_map/ppermute | solution.py:20
  1.1 1.1 %pack.1 = (bf16[64,768]{1,0:T(8,128)(2,1)S(1)}, f32[64,128]{1,0:T(8,128)S(1)}, bf16[40,512]{1,0:T(8,128)(2,1)S(1)}) custom-call(f32[64,768]{1,0:T(8,128)} %classifier_hbm.1, s32[1,64]{1,0:T(1,128)} %bitcast.9, s32[4,512]{1,0:T(4,128)} %bitcast.6, s32[4,512]{1,0:T(4,128)} %bitcast.7, s32[4,512]{1,0:T(4,128)} %bitcast.8, s32[4,8,512]{2,1,0:T(8,128)} %bitcast.5), custom_call_target="tpu_custom_call" | custom-call | flops 49152 | bytes 376832 | tf_op jit(solution)/shard_map/pack/pallas_call | solution.py:214
  2.3 3.5 %collective-permute-start = (bf16[64,768]{1,0:T(8,128)(2,1)S(1)}, bf16[64,768]{1,0:T(8,128)(2,1)S(1)}, u32[]{:S(2)}, u32[]{:S(2)}) collective-permute-start(bf16[64,768]{1,0:T(8,128)(2,1)S(1)} %get-tuple-element.25.refs_1_), channel_id=1, source_target_pairs={{0,6},{1,7},{2,4},{3,5},{4,2},{5,3},{6,0},{7,1},{8,14},{9,15},{10,... | collective-permute-start | bytes 294920 | tf_op jit(solution)/shard_map/ppermute | solution.py:20
  5.8 0.5 %collective-permute-start.5 = (bf16[64,768]{1,0:T(8,128)(2,1)S(1)}, bf16[64,768]{1,0:T(8,128)(2,1)S(1)}, u32[]{:S(2)}, u32[]{:S(2)}) collective-permute-start(bf16[64,768]{1,0:T(8,128)(2,1)S(1)} %get-tuple-element.25.refs_1_), channel_id=1, source_target_pairs={{0,4},{1,5},{2,6},{3,7},{4,0},{5,1},{6,2},{7,3},{8,12},{9,13},{10,... | collective-permute-start | bytes 294920 | tf_op jit(solution)/shard_map/ppermute | solution.py:20
  6.3 0.1 collective-permute-start.4
  6.5 0.0 collective-permute-start.2
  6.5 0.0 collective-permute-done.1.other_ref.refs_3_
  6.5 1.4 %turn.1 = (bf16[512,768]{1,0:T(8,128)(2,1)S(1)}, bf16[768,512]{1,0:T(8,128)(2,1)S(1)}, bf16[768,512]{1,0:T(8,128)(2,1)S(1)}) custom-call(bf16[512,768]{1,0:T(8,128)(2,1)} %emb_hbm.1, bf16[512,768]{1,0:T(8,128)(2,1)S(1)} %collective-permute-done.1.other_ref.refs_3_), custom_call_target="tpu_custom_call" | custom-call | flops 393216 | bytes 3932160 | tf_op jit(solution)/shard_map/turn/pallas_call | solution.py:242
  7.9 0.0 collective-permute-done.2.index_other_ref
  7.9 0.8 %targets.1 = (bf16[256,512]{1,0:T(8,128)(2,1)S(1)}, bf16[256,512]{1,0:T(8,128)(2,1)S(1)}) custom-call(bf16[40,512]{1,0:T(8,128)(2,1)S(1)} %get-tuple-element.29.index_own_ref, bf16[40,512]{1,0:T(8,128)(2,1)S(1)} %collective-permute-done.2.index_other_ref, bf16[768,512]{1,0:T(8,128)(2,1)S(1)} %get-tuple-element.28.after_ref.refs_5_), custom_call_target="tpu_custom_call" | custom-call | flops 10485760 | bytes 688128 | tf_op jit(solution)/shard_map/targets/pallas_call | solution.py:253
  8.7 0.6 %collective-permute-done.refs_0_ = bf16[64,768]{1,0:T(8,128)(2,1)S(1)} collective-permute-done((bf16[64,768]{1,0:T(8,128)(2,1)S(1)}, bf16[64,768]{1,0:T(8,128)(2,1)S(1)}, u32[]{:S(2)}, u32[]{:S(2)}) %collective-permute-start) | collective-permute-done | bytes 98336 | tf_op jit(solution)/shard_map/ppermute | solution.py:20
  9.3 0.7 %score.2 = (bf16[80,768]{1,0:T(8,128)(2,1)S(1)}, f32[64,768]{1,0:T(8,128)S(1)}, bf16[64,512]{1,0:T(8,128)(2,1)S(1)}, bf16[64,512]{1,0:T(8,128)(2,1)S(1)}, bf16[6...) custom-call(bf16[64,768]{1,0:T(8,128)(2,1)S(1)} %collective-permute-done.refs_0_, ...), custom_call_target="tpu_custom_call" | custom-call | flops 402653184 | bytes 4456448 | tf_op jit(solution)/shard_map/score/pallas_call | solution.py:268
  10.1 3.1 %collective-permute-start.3 = (bf16[80,768]{1,0:T(8,128)(2,1)S(1)}, bf16[80,768]{1,0:T(8,128)(2,1)S(1)}, u32[]{:S(2)}, u32[]{:S(2)}) collective-permute-start(bf16[80,768]{1,0:T(8,128)(2,1)S(1)} %get-tuple-element.33.refs_8_), channel_id=1, source_target_pairs={{0,6},{1,7},{2,4},{3,5},{4,2},{5,3},{6,0},{7,1},{8,14},{9,15},{10,... | collective-permute-start | bytes 368648 | tf_op jit(solution)/shard_map/ppermute | solution.py:20
  13.2 0.0 collective-permute-done.5.refs_1_.refs_3_
  13.2 0.0 collective-permute-done.4.refs_0_.refs_2_
  13.2 0.7 %score.3 = (bf16[64,768]{1,0:T(8,128)(2,1)S(1)}, bf16[64,768]{1,0:T(8,128)(2,1)S(1)}, bf16[64,512]{1,0:T(8,128)(2,1)S(1)}, bf16[64,512]{1,0:T(8,128)(2,1)S(1)}, ...) custom-call(bf16[64,768]{1,0:T(8,128)(2,1)S(1)} %collective-permute-done.4.refs_0_.refs_2_, ...), custom_call_target="tpu_custom_call" | custom-call | flops 402653184 | bytes 4456448 | tf_op jit(solution)/shard_map/score/pallas_call | solution.py:268
  13.9 0.5 %collective-permute-start.6 = (bf16[64,768]{1,0:T(8,128)(2,1)S(1)}, bf16[64,768]{1,0:T(8,128)(2,1)S(1)}, u32[]{:S(2)}, u32[]{:S(2)}) collective-permute-start(bf16[64,768]{1,0:T(8,128)(2,1)S(1)} %get-tuple-element.34), channel_id=1, source_target_pairs={{0,4},{1,5},{2,6},{3,7},{4,0},{5,1},{6,2},{7,3},{8,12},{9,13},{10,... | collective-permute-start | bytes 294920 | tf_op jit(solution)/shard_map/ppermute | solution.py:20
  14.4 0.1 collective-permute-start.7
  14.6 4.0 %collective-permute-done.6 = bf16[64,768]{1,0:T(8,128)(2,1)S(1)} collective-permute-done((bf16[64,768]{1,0:T(8,128)(2,1)S(1)}, bf16[64,768]{1,0:T(8,128)(2,1)S(1)}, u32[]{:S(2)}, u32[]{:S(2)}) %collective-permute-start.6) | collective-permute-done | bytes 98336 | tf_op jit(solution)/shard_map/ppermute | solution.py:20
  18.6 0.5 %collective-permute-done.7 = bf16[64,768]{1,0:T(8,128)(2,1)S(1)} collective-permute-done((bf16[64,768]{1,0:T(8,128)(2,1)S(1)}, bf16[64,768]{1,0:T(8,128)(2,1)S(1)}, u32[]{:S(2)}, u32[]{:S(2)}) %collective-permute-start.7) | collective-permute-done | bytes 98336 | tf_op jit(solution)/shard_map/ppermute | solution.py:20
  19.1 0.0 collective-permute-done.3
  19.1 1.6 %collective-permute-start.8 = (bf16[64,768]{1,0:T(8,128)(2,1)S(1)}, bf16[64,768]{1,0:T(8,128)(2,1)S(1)}, u32[]{:S(2)}, u32[]{:S(2)}) collective-permute-start(bf16[64,768]{1,0:T(8,128)(2,1)S(1)} %fusion), channel_id=1, source_target_pairs={{0,8},{8,0},{16,24},{24,16},{1,9},{9,1},{17,25},{25,17},{2,10},{10... | collective-permute-start | bytes 294920 | tf_op jit(solution)/shard_map/ppermute | solution.py:20
  20.8 0.1 join.1
  20.8 0.1 collective-permute-start.11
  20.9 0.5 %collective-permute-start.10 = (bf16[256,512]{1,0:T(8,128)(2,1)S(1)}, bf16[256,512]{1,0:T(8,128)(2,1)S(1)}, u32[]{:S(2)}, u32[]{:S(2)}) collective-permute-start(bf16[256,512]{1,0:T(8,128)(2,1)S(1)} %get-tuple-element.46), channel_id=1, source_target_pairs={{0,1},{1,0},{2,3},{3,2},{4,5},{5,4},{6,7},{7,6},{8,9},{9,8},{10,11... | collective-permute-start | bytes 786440 | tf_op jit(solution)/shard_map/ppermute | solution.py:20
  21.4 2.4 %collective-permute-done.8 = bf16[64,768]{1,0:T(8,128)(2,1)S(1)} collective-permute-done((bf16[64,768]{1,0:T(8,128)(2,1)S(1)}, bf16[64,768]{1,0:T(8,128)(2,1)S(1)}, u32[]{:S(2)}, u32[]{:S(2)}) %collective-permute-start.8) | collective-permute-done | bytes 98336 | tf_op jit(solution)/shard_map/ppermute | solution.py:20
  23.8 0.1 fusion.1
  23.9 2.6 %collective-permute-start.9 = (bf16[64,768]{1,0:T(8,128)(2,1)S(1)}, bf16[64,768]{1,0:T(8,128)(2,1)S(1)}, u32[]{:S(2)}, u32[]{:S(2)}) collective-permute-start(bf16[64,768]{1,0:T(8,128)(2,1)S(1)} %get-tuple-element.48), channel_id=1, source_target_pairs={{0,16},{8,24},{16,0},{24,8},{1,17},{9,25},{17,1},{25,9},{2,18},{10... | collective-permute-start | bytes 294920 | tf_op jit(solution)/shard_map/ppermute | solution.py:20
  26.5 0.0 collective-permute-done.10.d_other_ref
  26.5 0.0 collective-permute-done.11.c_other_ref
  26.5 1.7 %emb_grad.1.after_hbm = f32[512,768]{1,0:T(8,128)} custom-call(bf16[256,512]{1,0:T(8,128)(2,1)S(1)} %get-tuple-element.45.d_own_ref, bf16[256,512]{1,0:T(8,128)(2,1)S(1)} %collective-permute-done.10.d_other_ref, bf16[256,768]{1,0:T(8,128)(2,1)S(1)} %get-tuple-element.47.c_own_ref, bf16[256,768]{1,0:T(8,128)(2,1)S(1)} %collective-permute-done.11.c_other_ref, ...), custom_call_target="tpu_custom_call" | custom-call | flops 402653184 | bytes 2883584 | tf_op jit(solution)/shard_map/emb_grad/pallas_call | solution.py:329
  28.2 1.2 %collective-permute-done.9.received_ref = bf16[64,768]{1,0:T(8,128)(2,1)S(1)} collective-permute-done((bf16[64,768]{1,0:T(8,128)(2,1)S(1)}, bf16[64,768]{1,0:T(8,128)(2,1)S(1)}, u32[]{:S(2)}, u32[]{:S(2)}) %collective-permute-start.9) | collective-permute-done | bytes 98336 | tf_op jit(solution)/shard_map/ppermute | solution.py:20
  29.4 0.8 %finish.1 = f32[64,768]{1,0:T(8,128)} custom-call(f32[64,768]{1,0:T(8,128)S(1)} %get-tuple-element.49.after_ref.grad_ref, bf16[64,768]{1,0:T(8,128)(2,1)S(1)} %collective-permute-done.9.received_ref, f32[64,128]{1,0:T(8,128)S(1)} %get-tuple-element.36.column_ref, f32[512,768]{1,0:T(8,128)} %emb_grad.1.after_hbm), custom_call_target="tpu_custom_call" | custom-call | flops 49152 | bytes 491520 | tf_op jit(solution)/shard_map/finish/pallas_call | solution.py:339
  (1 shorter events, 0.0 us)
Async XLA Ops:
  0.6 5.8 %collective-permute-start.1 = (bf16[512,768]{1,0:T(8,128)(2,1)}, bf16[512,768]{1,0:T(8,128)(2,1)S(1)}, u32[]{:S(2)}, u32[]{:S(2)}) collective-permute-start(bf16[512,768]{1,0:T(8,128)(2,1)} %emb_hbm.1), channel_id=1, source_target_pairs={{0,1},{1,0},{2,3},{3,2},{4,5},{5,4},{6,7},{7,6},{8,9},{9,8},{10,11... | collective-permute-start | bytes 2359304 | tf_op jit(solution)/shard_map/ppermute | solution.py:20
  2.3 7.0 %collective-permute-start = (bf16[64,768]{1,0:T(8,128)(2,1)S(1)}, bf16[64,768]{1,0:T(8,128)(2,1)S(1)}, u32[]{:S(2)}, u32[]{:S(2)}) collective-permute-start(bf16[64,768]{1,0:T(8,128)(2,1)S(1)} %get-tuple-element.25.refs_1_), channel_id=1, source_target_pairs={{0,6},{1,7},{2,4},{3,5},{4,2},{5,3},{6,0},{7,1},{8,14},{9,15},{10,... | collective-permute-start | bytes 294920 | tf_op jit(solution)/shard_map/ppermute | solution.py:20
  5.8 7.3 %collective-permute-start.5 = (bf16[64,768]{1,0:T(8,128)(2,1)S(1)}, bf16[64,768]{1,0:T(8,128)(2,1)S(1)}, u32[]{:S(2)}, u32[]{:S(2)}) collective-permute-start(bf16[64,768]{1,0:T(8,128)(2,1)S(1)} %get-tuple-element.25.refs_1_), channel_id=1, source_target_pairs={{0,4},{1,5},{2,6},{3,7},{4,0},{5,1},{6,2},{7,3},{8,12},{9,13},{10,... | collective-permute-start | bytes 294920 | tf_op jit(solution)/shard_map/ppermute | solution.py:20
  6.3 6.8 %collective-permute-start.4 = (bf16[64,768]{1,0:T(8,128)(2,1)S(1)}, bf16[64,768]{1,0:T(8,128)(2,1)S(1)}, u32[]{:S(2)}, u32[]{:S(2)}) collective-permute-start(bf16[64,768]{1,0:T(8,128)(2,1)S(1)} %get-tuple-element.25.refs_1_), channel_id=1, source_target_pairs={{0,2},{1,3},{2,0},{3,1},{4,6},{5,7},{6,4},{7,5},{8,10},{9,11},{10,... | collective-permute-start | bytes 294920 | tf_op jit(solution)/shard_map/ppermute | solution.py:20
  6.5 1.4 %collective-permute-start.2 = (bf16[40,512]{1,0:T(8,128)(2,1)S(1)}, bf16[40,512]{1,0:T(8,128)(2,1)S(1)}, u32[]{:S(2)}, u32[]{:S(2)}) collective-permute-start(bf16[40,512]{1,0:T(8,128)(2,1)S(1)} %get-tuple-element.29.index_own_ref), channel_id=1, source_target_pairs={{0,1},{1,0},{2,3},{3,2},{4,5},{5,4},{6,7},{7,6},{8,9},{9,8},{10,11... | collective-permute-start | bytes 122888 | tf_op jit(solution)/shard_map/ppermute | solution.py:20
  10.1 9.0 %collective-permute-start.3 = (bf16[80,768]{1,0:T(8,128)(2,1)S(1)}, bf16[80,768]{1,0:T(8,128)(2,1)S(1)}, u32[]{:S(2)}, u32[]{:S(2)}) collective-permute-start(bf16[80,768]{1,0:T(8,128)(2,1)S(1)} %get-tuple-element.33.refs_8_), channel_id=1, source_target_pairs={{0,6},{1,7},{2,4},{3,5},{4,2},{5,3},{6,0},{7,1},{8,14},{9,15},{10,... | collective-permute-start | bytes 368648 | tf_op jit(solution)/shard_map/ppermute | solution.py:20
  13.9 4.7 %collective-permute-start.6 = (bf16[64,768]{1,0:T(8,128)(2,1)S(1)}, bf16[64,768]{1,0:T(8,128)(2,1)S(1)}, u32[]{:S(2)}, u32[]{:S(2)}) collective-permute-start(bf16[64,768]{1,0:T(8,128)(2,1)S(1)} %get-tuple-element.34), channel_id=1, source_target_pairs={{0,4},{1,5},{2,6},{3,7},{4,0},{5,1},{6,2},{7,3},{8,12},{9,13},{10,... | collective-permute-start | bytes 294920 | tf_op jit(solution)/shard_map/ppermute | solution.py:20
  14.4 4.6 %collective-permute-start.7 = (bf16[64,768]{1,0:T(8,128)(2,1)S(1)}, bf16[64,768]{1,0:T(8,128)(2,1)S(1)}, u32[]{:S(2)}, u32[]{:S(2)}) collective-permute-start(bf16[64,768]{1,0:T(8,128)(2,1)S(1)} %get-tuple-element.35), channel_id=1, source_target_pairs={{0,2},{1,3},{2,0},{3,1},{4,6},{5,7},{6,4},{7,5},{8,10},{9,11},{10,... | collective-permute-start | bytes 294920 | tf_op jit(solution)/shard_map/ppermute | solution.py:20
  19.1 4.7 %collective-permute-start.8 = (bf16[64,768]{1,0:T(8,128)(2,1)S(1)}, bf16[64,768]{1,0:T(8,128)(2,1)S(1)}, u32[]{:S(2)}, u32[]{:S(2)}) collective-permute-start(bf16[64,768]{1,0:T(8,128)(2,1)S(1)} %fusion), channel_id=1, source_target_pairs={{0,8},{8,0},{16,24},{24,16},{1,9},{9,1},{17,25},{25,17},{2,10},{10... | collective-permute-start | bytes 294920 | tf_op jit(solution)/shard_map/ppermute | solution.py:20
  20.8 5.7 %collective-permute-start.11 = (bf16[256,768]{1,0:T(8,128)(2,1)S(1)}, bf16[256,768]{1,0:T(8,128)(2,1)S(1)}, u32[]{:S(2)}, u32[]{:S(2)}) collective-permute-start(bf16[256,768]{1,0:T(8,128)(2,1)S(1)} %get-tuple-element.47.c_own_ref), channel_id=1, source_target_pairs={{0,1},{1,0},{2,3},{3,2},{4,5},{5,4},{6,7},{7,6},{8,9},{9,8},{10,11... | collective-permute-start | bytes 1179656 | tf_op jit(solution)/shard_map/ppermute | solution.py:20
  20.9 5.6 %collective-permute-start.10 = (bf16[256,512]{1,0:T(8,128)(2,1)S(1)}, bf16[256,512]{1,0:T(8,128)(2,1)S(1)}, u32[]{:S(2)}, u32[]{:S(2)}) collective-permute-start(bf16[256,512]{1,0:T(8,128)(2,1)S(1)} %get-tuple-element.46), channel_id=1, source_target_pairs={{0,1},{1,0},{2,3},{3,2},{4,5},{5,4},{6,7},{7,6},{8,9},{9,8},{10,11... | collective-permute-start | bytes 786440 | tf_op jit(solution)/shard_map/ppermute | solution.py:20
  23.9 5.6 %collective-permute-start.9 = (bf16[64,768]{1,0:T(8,128)(2,1)S(1)}, bf16[64,768]{1,0:T(8,128)(2,1)S(1)}, u32[]{:S(2)}, u32[]{:S(2)}) collective-permute-start(bf16[64,768]{1,0:T(8,128)(2,1)S(1)} %get-tuple-element.48), channel_id=1, source_target_pairs={{0,16},{8,24},{16,0},{24,8},{1,17},{9,25},{17,1},{25,9},{2,18},{10... | collective-permute-start | bytes 294920 | tf_op jit(solution)/shard_map/ppermute | solution.py:20

commit v12 on v11

--- a/solution.py
+++ b/solution.py
@@ -16,8 +16,9 @@
 MIB = 1024 * 1024
 
 
-def flip(value, axis, mask):
-    return lax.ppermute(value, axis, [(i, i ^ mask) for i in range(lax.axis_size(axis))])
+def flip(value, axis, mask, odd=None):
+    masks = (mask, mask if odd is None else odd)
+    return lax.ppermute(value, axis, [(i, i ^ masks[i & 1]) for i in range(lax.axis_size(axis))])
 
 
 def bit_groups(count):
@@ -25,8 +26,18 @@
     return [tuple(masks[i : i + 2]) for i in range(0, len(masks), 2)]
 
 
-def group_masks(group):
-    return [group[0]] if len(group) == 1 else [group[0], group[1], group[0] | group[1]]
+def partners(group):
+    if len(group) == 1:
+        return [(group[0], group[0])]
+    low, high = group
+    return [(low, high), (high, low), (low | high, low | high)]
+
+
+def block_masks(groups):
+    masks = [(0, 0)]
+    for group in groups:
+        masks = [(e ^ x, o ^ y) for e, o in [(0, 0)] + partners(group) for x, y in masks]
+    return masks
 
 
 def fetch(sources, targets, sem):
@@ -77,7 +88,7 @@
     own_turned_ref[...] = own_ref[...].T
 
 
-def targets_kernel(index_own_ref, index_other_ref, after_ref, target_own_ref, target_other_ref, *, panel, slots):
+def targets_kernel(index_own_ref, index_other_ref, after_ref, target_own_ref, target_other_ref, *, panel, slots, masks):
     me = lax.axis_index("lab")
     docs = index_own_ref.shape[1]
     negatives = index_own_ref.shape[0] // slots - 2
@@ -100,10 +111,11 @@
             hot = row(slots * negatives + s).astype(BF16)[None] == label
             values.append(jnp.where(hot, -one - count, count))
             relative.append(row(slots * (negatives + 1) + s).astype(jnp.int32) ^ me)
-        for j in range(out_ref.shape[0] // panel):
+        for j, (even_mask, odd_mask) in enumerate(masks):
+            mask = even_mask + (me & 1) * (odd_mask - even_mask)
             block = jnp.zeros(shape, BF16)
             for s in range(slots):
-                chosen = jnp.where(relative[s] == 2 * j, 1.0, 0.0).astype(BF16)
+                chosen = jnp.where(relative[s] == mask, 1.0, 0.0).astype(BF16)
                 block = block + chosen[None] * values[s]
             out_ref[pl.ds(j * panel, panel), lanes] = block.reshape(panel, LANES)
 
@@ -235,7 +247,7 @@
     pieces = [packed]
     for group in groups:
         own = pieces[0] if len(pieces) == 1 else jnp.concatenate(pieces, 0)
-        pieces = [own] + [flip(own, "lab", mask) for mask in group_masks(group)]
+        pieces = [own] + [flip(own, "lab", *masks) for masks in partners(group)]
 
     emb_other = flip(embeddings, "lab", 1)
     index_other = flip(index_own, "lab", 1)
@@ -251,7 +263,7 @@
         name="turn",
     )(*keep(embeddings), emb_other)
     target_own, target_other = pl.pallas_call(
-        functools.partial(targets_kernel, panel=panel, slots=slots),
+        functools.partial(targets_kernel, panel=panel, slots=slots, masks=block_masks(groups)),
         out_shape=[jax.ShapeDtypeStruct((half, docs), BF16)] * 2,
         in_specs=vmem(3),
         out_specs=vmem(2),
@@ -305,7 +317,7 @@
 
     grad = None
     for group in reversed(groups):
-        masks = group_masks(group)
+        masks = partners(group)
         if grad is not None:
             grad = grad.reshape(len(masks) + 1, -1, width)
             grads = [grad[0]] + [grad[i].astype(BF16) for i in range(1, len(masks) + 1)]
@@ -314,7 +326,7 @@
             value = grads[i + 1]
             if i == 2 and value.shape[0] == grads[0].shape[0]:
                 value = jnp.concatenate([value, value[:1]], 0)
-            received.append(flip(value, "lab", masks[i])[: grads[0].shape[0]])
+            received.append(flip(value, "lab", *masks[i])[: grads[0].shape[0]])
         grad = grads[0]
         for r in received:
             grad = grad + r.astype(F32)

time: 30.4 us -> 30.4 us (level)
  no operation moved by 1% of the time
where the time goes in v12:
time: 30.4 us; the launch traced here: 30.2 us
  starting transfers between devices  13.2 us (43%)
  waiting for transfers between devices  8.79 us (29%)
  Pallas kernels  7.39 us (24%)
  between operations  0.71 us (2%)
    ppermute x12, starting transfers between devices, flip(): lax.ppermute(value, axis, [(i, i ^ masks[i & 1]) for i in range(lax.axis_...  13.2 us
    ppermute x12, waiting for transfers between devices, flip(): lax.ppermute(value, axis, [(i, i ^ masks[i & 1]) for i in range(lax.axis_...  8.79 us
    pallas_call x1, Pallas kernels, shards(): pl.pallas_call(emb_kernel, out_shape=jax.ShapeDtypeStruct((docs, width),...  1.74 us
    pallas_call x2, Pallas kernels, score(): pl.pallas_call(functools.partial(score_kernel, which=which, after=len(aft...  1.46 us
    pallas_call x1, Pallas kernels, shards(): pl.pallas_call(turn_kernel, out_shape=[jax.ShapeDtypeStruct((docs, width)...  1.41 us
    pallas_call x1, Pallas kernels, shards(): pl.pallas_call(functools.partial(pack_kernel, scale=1.0 / math.sqrt(docs...  1.15 us
    pallas_call x1, Pallas kernels, shards(): pl.pallas_call(functools.partial(targets_kernel, panel=panel, slots=slots...  0.82 us
    pallas_call x1, Pallas kernels, shards(): pl.pallas_call(finish_kernel, out_shape=jax.ShapeDtypeStruct((panel, widt...  0.76 us
  transfers between devices with their start and end apart: 12, of which 5 were waited for; matrix products, arithmetic and copies ran while one was open for 0% of the time, Pallas kernels for 22%

profile of v12, /device:TPU:0, one launch (start us, length us, event | category | flops | bytes accessed | tf_op | source)
XLA Modules:
  0.0 30.2 jit_solution(13318785495111195699)
XLA Ops:
  0.6 0.5 %collective-permute-start.1 = (bf16[512,768]{1,0:T(8,128)(2,1)}, bf16[512,768]{1,0:T(8,128)(2,1)S(1)}, u32[]{:S(2)}, u32[]{:S(2)}) collective-permute-start(bf16[512,768]{1,0:T(8,128)(2,1)} %emb_hbm.1), channel_id=1, source_target_pairs={{0,1},{1,0},{2,3},{3,2},{4,5},{5,4},{6,7},{7,6},{8,9},{9,8},{10,11... | collective-permute-start | bytes 2359304 | tf_op jit(solution)/shard_map/ppermute | solution.py:21
  1.1 1.1 %pack.1 = (bf16[64,768]{1,0:T(8,128)(2,1)S(1)}, f32[64,128]{1,0:T(8,128)S(1)}, bf16[40,512]{1,0:T(8,128)(2,1)S(1)}) custom-call(f32[64,768]{1,0:T(8,128)} %classifier_hbm.1, s32[1,64]{1,0:T(1,128)} %bitcast.9, s32[4,512]{1,0:T(4,128)} %bitcast.6, s32[4,512]{1,0:T(4,128)} %bitcast.7, s32[4,512]{1,0:T(4,128)} %bitcast.8, s32[4,8,512]{2,1,0:T(8,128)} %bitcast.5), custom_call_target="tpu_custom_call" | custom-call | flops 49152 | bytes 376832 | tf_op jit(solution)/shard_map/pack/pallas_call | solution.py:226
  2.3 3.5 %collective-permute-start = (bf16[64,768]{1,0:T(8,128)(2,1)S(1)}, bf16[64,768]{1,0:T(8,128)(2,1)S(1)}, u32[]{:S(2)}, u32[]{:S(2)}) collective-permute-start(bf16[64,768]{1,0:T(8,128)(2,1)S(1)} %get-tuple-element.25.refs_1_), channel_id=1, source_target_pairs={{0,6},{1,7},{2,4},{3,5},{4,2},{5,3},{6,0},{7,1},{8,14},{9,15},{10,... | collective-permute-start | bytes 294920 | tf_op jit(solution)/shard_map/ppermute | solution.py:21
  5.8 0.5 %collective-permute-start.5 = (bf16[64,768]{1,0:T(8,128)(2,1)S(1)}, bf16[64,768]{1,0:T(8,128)(2,1)S(1)}, u32[]{:S(2)}, u32[]{:S(2)}) collective-permute-start(bf16[64,768]{1,0:T(8,128)(2,1)S(1)} %get-tuple-element.25.refs_1_), channel_id=1, source_target_pairs={{0,4},{1,3},{2,6},{3,1},{4,0},{5,7},{6,2},{7,5},{8,12},{9,11},{10,... | collective-permute-start | bytes 294920 | tf_op jit(solution)/shard_map/ppermute | solution.py:21
  6.3 0.1 collective-permute-start.4
  6.5 0.0 collective-permute-start.2
  6.5 0.0 collective-permute-done.1.other_ref.refs_3_
  6.5 1.4 %turn.1 = (bf16[512,768]{1,0:T(8,128)(2,1)S(1)}, bf16[768,512]{1,0:T(8,128)(2,1)S(1)}, bf16[768,512]{1,0:T(8,128)(2,1)S(1)}) custom-call(bf16[512,768]{1,0:T(8,128)(2,1)} %emb_hbm.1, bf16[512,768]{1,0:T(8,128)(2,1)S(1)} %collective-permute-done.1.other_ref.refs_3_), custom_call_target="tpu_custom_call" | custom-call | flops 393216 | bytes 3932160 | tf_op jit(solution)/shard_map/turn/pallas_call | solution.py:254
  7.9 0.0 collective-permute-done.2.index_other_ref
  7.9 0.8 %targets.1 = (bf16[256,512]{1,0:T(8,128)(2,1)S(1)}, bf16[256,512]{1,0:T(8,128)(2,1)S(1)}) custom-call(bf16[40,512]{1,0:T(8,128)(2,1)S(1)} %get-tuple-element.29.index_own_ref, bf16[40,512]{1,0:T(8,128)(2,1)S(1)} %collective-permute-done.2.index_other_ref, bf16[768,512]{1,0:T(8,128)(2,1)S(1)} %get-tuple-element.28.after_ref.refs_5_), custom_call_target="tpu_custom_call" | custom-call | flops 10485760 | bytes 688128 | tf_op jit(solution)/shard_map/targets/pallas_call | solution.py:265
  8.7 0.7 %collective-permute-done.refs_0_ = bf16[64,768]{1,0:T(8,128)(2,1)S(1)} collective-permute-done((bf16[64,768]{1,0:T(8,128)(2,1)S(1)}, bf16[64,768]{1,0:T(8,128)(2,1)S(1)}, u32[]{:S(2)}, u32[]{:S(2)}) %collective-permute-start) | collective-permute-done | bytes 98336 | tf_op jit(solution)/shard_map/ppermute | solution.py:21
  9.5 0.7 %score.2 = (bf16[80,768]{1,0:T(8,128)(2,1)S(1)}, f32[64,768]{1,0:T(8,128)S(1)}, bf16[64,512]{1,0:T(8,128)(2,1)S(1)}, bf16[64,512]{1,0:T(8,128)(2,1)S(1)}, bf16[6...) custom-call(bf16[64,768]{1,0:T(8,128)(2,1)S(1)} %collective-permute-done.refs_0_, ...), custom_call_target="tpu_custom_call" | custom-call | flops 402653184 | bytes 4456448 | tf_op jit(solution)/shard_map/score/pallas_call | solution.py:280
  10.2 2.9 %collective-permute-start.3 = (bf16[80,768]{1,0:T(8,128)(2,1)S(1)}, bf16[80,768]{1,0:T(8,128)(2,1)S(1)}, u32[]{:S(2)}, u32[]{:S(2)}) collective-permute-start(bf16[80,768]{1,0:T(8,128)(2,1)S(1)} %get-tuple-element.33.refs_8_), channel_id=1, source_target_pairs={{0,6},{1,7},{2,4},{3,5},{4,2},{5,3},{6,0},{7,1},{8,14},{9,15},{10,... | collective-permute-start | bytes 368648 | tf_op jit(solution)/shard_map/ppermute | solution.py:21
  13.2 0.0 collective-permute-done.5.refs_1_.refs_3_
  13.2 0.0 collective-permute-done.4.refs_0_.refs_2_
  13.2 0.7 %score.3 = (bf16[64,768]{1,0:T(8,128)(2,1)S(1)}, bf16[64,768]{1,0:T(8,128)(2,1)S(1)}, bf16[64,512]{1,0:T(8,128)(2,1)S(1)}, bf16[64,512]{1,0:T(8,128)(2,1)S(1)}, ...) custom-call(bf16[64,768]{1,0:T(8,128)(2,1)S(1)} %collective-permute-done.4.refs_0_.refs_2_, ...), custom_call_target="tpu_custom_call" | custom-call | flops 402653184 | bytes 4456448 | tf_op jit(solution)/shard_map/score/pallas_call | solution.py:280
  13.9 0.5 %collective-permute-start.6 = (bf16[64,768]{1,0:T(8,128)(2,1)S(1)}, bf16[64,768]{1,0:T(8,128)(2,1)S(1)}, u32[]{:S(2)}, u32[]{:S(2)}) collective-permute-start(bf16[64,768]{1,0:T(8,128)(2,1)S(1)} %get-tuple-element.34), channel_id=1, source_target_pairs={{0,4},{1,3},{2,6},{3,1},{4,0},{5,7},{6,2},{7,5},{8,12},{9,11},{10,... | collective-permute-start | bytes 294920 | tf_op jit(solution)/shard_map/ppermute | solution.py:21
  14.4 0.2 collective-permute-start.7
  14.6 4.0 %collective-permute-done.6 = bf16[64,768]{1,0:T(8,128)(2,1)S(1)} collective-permute-done((bf16[64,768]{1,0:T(8,128)(2,1)S(1)}, bf16[64,768]{1,0:T(8,128)(2,1)S(1)}, u32[]{:S(2)}, u32[]{:S(2)}) %collective-permute-start.6) | collective-permute-done | bytes 98336 | tf_op jit(solution)/shard_map/ppermute | solution.py:21
  18.6 0.4 %collective-permute-done.7 = bf16[64,768]{1,0:T(8,128)(2,1)S(1)} collective-permute-done((bf16[64,768]{1,0:T(8,128)(2,1)S(1)}, bf16[64,768]{1,0:T(8,128)(2,1)S(1)}, u32[]{:S(2)}, u32[]{:S(2)}) %collective-permute-start.7) | collective-permute-done | bytes 98336 | tf_op jit(solution)/shard_map/ppermute | solution.py:21
  19.1 0.0 collective-permute-done.3
  19.1 1.6 %collective-permute-start.8 = (bf16[64,768]{1,0:T(8,128)(2,1)S(1)}, bf16[64,768]{1,0:T(8,128)(2,1)S(1)}, u32[]{:S(2)}, u32[]{:S(2)}) collective-permute-start(bf16[64,768]{1,0:T(8,128)(2,1)S(1)} %fusion), channel_id=1, source_target_pairs={{0,8},{8,0},{16,24},{24,16},{1,9},{9,1},{17,25},{25,17},{2,10},{10... | collective-permute-start | bytes 294920 | tf_op jit(solution)/shard_map/ppermute | solution.py:21
  20.8 0.1 join.1
  20.8 0.1 collective-permute-start.11
  20.9 0.5 %collective-permute-start.10 = (bf16[256,512]{1,0:T(8,128)(2,1)S(1)}, bf16[256,512]{1,0:T(8,128)(2,1)S(1)}, u32[]{:S(2)}, u32[]{:S(2)}) collective-permute-start(bf16[256,512]{1,0:T(8,128)(2,1)S(1)} %get-tuple-element.46), channel_id=1, source_target_pairs={{0,1},{1,0},{2,3},{3,2},{4,5},{5,4},{6,7},{7,6},{8,9},{9,8},{10,11... | collective-permute-start | bytes 786440 | tf_op jit(solution)/shard_map/ppermute | solution.py:21
  21.4 2.4 %collective-permute-done.8 = bf16[64,768]{1,0:T(8,128)(2,1)S(1)} collective-permute-done((bf16[64,768]{1,0:T(8,128)(2,1)S(1)}, bf16[64,768]{1,0:T(8,128)(2,1)S(1)}, u32[]{:S(2)}, u32[]{:S(2)}) %collective-permute-start.8) | collective-permute-done | bytes 98336 | tf_op jit(solution)/shard_map/ppermute | solution.py:21
  23.8 0.1 fusion.1
  23.9 2.6 %collective-permute-start.9 = (bf16[64,768]{1,0:T(8,128)(2,1)S(1)}, bf16[64,768]{1,0:T(8,128)(2,1)S(1)}, u32[]{:S(2)}, u32[]{:S(2)}) collective-permute-start(bf16[64,768]{1,0:T(8,128)(2,1)S(1)} %get-tuple-element.48), channel_id=1, source_target_pairs={{0,16},{8,24},{16,0},{24,8},{1,17},{9,25},{17,1},{25,9},{2,18},{10... | collective-permute-start | bytes 294920 | tf_op jit(solution)/shard_map/ppermute | solution.py:21
  26.5 0.0 collective-permute-done.10.d_other_ref
  26.5 0.0 collective-permute-done.11.c_other_ref
  26.5 1.7 %emb_grad.1.after_hbm = f32[512,768]{1,0:T(8,128)} custom-call(bf16[256,512]{1,0:T(8,128)(2,1)S(1)} %get-tuple-element.45.d_own_ref, bf16[256,512]{1,0:T(8,128)(2,1)S(1)} %collective-permute-done.10.d_other_ref, bf16[256,768]{1,0:T(8,128)(2,1)S(1)} %get-tuple-element.47.c_own_ref, bf16[256,768]{1,0:T(8,128)(2,1)S(1)} %collective-permute-done.11.c_other_ref, ...), custom_call_target="tpu_custom_call" | custom-call | flops 402653184 | bytes 2883584 | tf_op jit(solution)/shard_map/emb_grad/pallas_call | solution.py:341
  28.2 1.2 %collective-permute-done.9.received_ref = bf16[64,768]{1,0:T(8,128)(2,1)S(1)} collective-permute-done((bf16[64,768]{1,0:T(8,128)(2,1)S(1)}, bf16[64,768]{1,0:T(8,128)(2,1)S(1)}, u32[]{:S(2)}, u32[]{:S(2)}) %collective-permute-start.9) | collective-permute-done | bytes 98336 | tf_op jit(solution)/shard_map/ppermute | solution.py:21
  29.4 0.8 %finish.1 = f32[64,768]{1,0:T(8,128)} custom-call(f32[64,768]{1,0:T(8,128)S(1)} %get-tuple-element.49.after_ref.grad_ref, bf16[64,768]{1,0:T(8,128)(2,1)S(1)} %collective-permute-done.9.received_ref, f32[64,128]{1,0:T(8,128)S(1)} %get-tuple-element.36.column_ref, f32[512,768]{1,0:T(8,128)} %emb_grad.1.after_hbm), custom_call_target="tpu_custom_call" | custom-call | flops 49152 | bytes 491520 | tf_op jit(solution)/shard_map/finish/pallas_call | solution.py:351
  (1 shorter events, 0.0 us)
Async XLA Ops:
  0.6 5.8 %collective-permute-start.1 = (bf16[512,768]{1,0:T(8,128)(2,1)}, bf16[512,768]{1,0:T(8,128)(2,1)S(1)}, u32[]{:S(2)}, u32[]{:S(2)}) collective-permute-start(bf16[512,768]{1,0:T(8,128)(2,1)} %emb_hbm.1), channel_id=1, source_target_pairs={{0,1},{1,0},{2,3},{3,2},{4,5},{5,4},{6,7},{7,6},{8,9},{9,8},{10,11... | collective-permute-start | bytes 2359304 | tf_op jit(solution)/shard_map/ppermute | solution.py:21
  2.3 7.2 %collective-permute-start = (bf16[64,768]{1,0:T(8,128)(2,1)S(1)}, bf16[64,768]{1,0:T(8,128)(2,1)S(1)}, u32[]{:S(2)}, u32[]{:S(2)}) collective-permute-start(bf16[64,768]{1,0:T(8,128)(2,1)S(1)} %get-tuple-element.25.refs_1_), channel_id=1, source_target_pairs={{0,6},{1,7},{2,4},{3,5},{4,2},{5,3},{6,0},{7,1},{8,14},{9,15},{10,... | collective-permute-start | bytes 294920 | tf_op jit(solution)/shard_map/ppermute | solution.py:21
  5.8 7.3 %collective-permute-start.5 = (bf16[64,768]{1,0:T(8,128)(2,1)S(1)}, bf16[64,768]{1,0:T(8,128)(2,1)S(1)}, u32[]{:S(2)}, u32[]{:S(2)}) collective-permute-start(bf16[64,768]{1,0:T(8,128)(2,1)S(1)} %get-tuple-element.25.refs_1_), channel_id=1, source_target_pairs={{0,4},{1,3},{2,6},{3,1},{4,0},{5,7},{6,2},{7,5},{8,12},{9,11},{10,... | collective-permute-start | bytes 294920 | tf_op jit(solution)/shard_map/ppermute | solution.py:21
  6.3 6.8 %collective-permute-start.4 = (bf16[64,768]{1,0:T(8,128)(2,1)S(1)}, bf16[64,768]{1,0:T(8,128)(2,1)S(1)}, u32[]{:S(2)}, u32[]{:S(2)}) collective-permute-start(bf16[64,768]{1,0:T(8,128)(2,1)S(1)} %get-tuple-element.25.refs_1_), channel_id=1, source_target_pairs={{0,2},{1,5},{2,0},{3,7},{4,6},{5,1},{6,4},{7,3},{8,10},{9,13},{10,... | collective-permute-start | bytes 294920 | tf_op jit(solution)/shard_map/ppermute | solution.py:21
  6.5 1.4 %collective-permute-start.2 = (bf16[40,512]{1,0:T(8,128)(2,1)S(1)}, bf16[40,512]{1,0:T(8,128)(2,1)S(1)}, u32[]{:S(2)}, u32[]{:S(2)}) collective-permute-start(bf16[40,512]{1,0:T(8,128)(2,1)S(1)} %get-tuple-element.29.index_own_ref), channel_id=1, source_target_pairs={{0,1},{1,0},{2,3},{3,2},{4,5},{5,4},{6,7},{7,6},{8,9},{9,8},{10,11... | collective-permute-start | bytes 122888 | tf_op jit(solution)/shard_map/ppermute | solution.py:21
  10.2 8.8 %collective-permute-start.3 = (bf16[80,768]{1,0:T(8,128)(2,1)S(1)}, bf16[80,768]{1,0:T(8,128)(2,1)S(1)}, u32[]{:S(2)}, u32[]{:S(2)}) collective-permute-start(bf16[80,768]{1,0:T(8,128)(2,1)S(1)} %get-tuple-element.33.refs_8_), channel_id=1, source_target_pairs={{0,6},{1,7},{2,4},{3,5},{4,2},{5,3},{6,0},{7,1},{8,14},{9,15},{10,... | collective-permute-start | bytes 368648 | tf_op jit(solution)/shard_map/ppermute | solution.py:21
  13.9 4.7 %collective-permute-start.6 = (bf16[64,768]{1,0:T(8,128)(2,1)S(1)}, bf16[64,768]{1,0:T(8,128)(2,1)S(1)}, u32[]{:S(2)}, u32[]{:S(2)}) collective-permute-start(bf16[64,768]{1,0:T(8,128)(2,1)S(1)} %get-tuple-element.34), channel_id=1, source_target_pairs={{0,4},{1,3},{2,6},{3,1},{4,0},{5,7},{6,2},{7,5},{8,12},{9,11},{10,... | collective-permute-start | bytes 294920 | tf_op jit(solution)/shard_map/ppermute | solution.py:21
  14.4 4.6 %collective-permute-start.7 = (bf16[64,768]{1,0:T(8,128)(2,1)S(1)}, bf16[64,768]{1,0:T(8,128)(2,1)S(1)}, u32[]{:S(2)}, u32[]{:S(2)}) collective-permute-start(bf16[64,768]{1,0:T(8,128)(2,1)S(1)} %get-tuple-element.35), channel_id=1, source_target_pairs={{0,2},{1,5},{2,0},{3,7},{4,6},{5,1},{6,4},{7,3},{8,10},{9,13},{10,... | collective-permute-start | bytes 294920 | tf_op jit(solution)/shard_map/ppermute | solution.py:21
  19.1 4.7 %collective-permute-start.8 = (bf16[64,768]{1,0:T(8,128)(2,1)S(1)}, bf16[64,768]{1,0:T(8,128)(2,1)S(1)}, u32[]{:S(2)}, u32[]{:S(2)}) collective-permute-start(bf16[64,768]{1,0:T(8,128)(2,1)S(1)} %fusion), channel_id=1, source_target_pairs={{0,8},{8,0},{16,24},{24,16},{1,9},{9,1},{17,25},{25,17},{2,10},{10... | collective-permute-start | bytes 294920 | tf_op jit(solution)/shard_map/ppermute | solution.py:21
  20.8 5.7 %collective-permute-start.11 = (bf16[256,768]{1,0:T(8,128)(2,1)S(1)}, bf16[256,768]{1,0:T(8,128)(2,1)S(1)}, u32[]{:S(2)}, u32[]{:S(2)}) collective-permute-start(bf16[256,768]{1,0:T(8,128)(2,1)S(1)} %get-tuple-element.47.c_own_ref), channel_id=1, source_target_pairs={{0,1},{1,0},{2,3},{3,2},{4,5},{5,4},{6,7},{7,6},{8,9},{9,8},{10,11... | collective-permute-start | bytes 1179656 | tf_op jit(solution)/shard_map/ppermute | solution.py:21
  20.9 5.6 %collective-permute-start.10 = (bf16[256,512]{1,0:T(8,128)(2,1)S(1)}, bf16[256,512]{1,0:T(8,128)(2,1)S(1)}, u32[]{:S(2)}, u32[]{:S(2)}) collective-permute-start(bf16[256,512]{1,0:T(8,128)(2,1)S(1)} %get-tuple-element.46), channel_id=1, source_target_pairs={{0,1},{1,0},{2,3},{3,2},{4,5},{5,4},{6,7},{7,6},{8,9},{9,8},{10,11... | collective-permute-start | bytes 786440 | tf_op jit(solution)/shard_map/ppermute | solution.py:21
  23.9 5.6 %collective-permute-start.9 = (bf16[64,768]{1,0:T(8,128)(2,1)S(1)}, bf16[64,768]{1,0:T(8,128)(2,1)S(1)}, u32[]{:S(2)}, u32[]{:S(2)}) collective-permute-start(bf16[64,768]{1,0:T(8,128)(2,1)S(1)} %get-tuple-element.48), channel_id=1, source_target_pairs={{0,16},{8,24},{16,0},{24,8},{1,17},{9,25},{17,1},{25,9},{2,18},{10... | collective-permute-start | bytes 294920 | tf_op jit(solution)/shard_map/ppermute | solution.py:21

commit v13 on v8

--- a/solution.py
+++ b/solution.py
@@ -139,15 +139,23 @@
 
     for unit in units:
         block = gather(unit, piece_refs)
-        logits = [jnp.dot(block, ref[...], preferred_element_type=F32) for ref in turned_refs]
+        both = jnp.concatenate([ref[...] for ref in turned_refs], 1)
+        logits = jnp.split(jnp.dot(block, both, preferred_element_type=F32), 2, 1)
         dlogits = []
         for x, target_ref in zip(logits, target_refs):
             signed = gather(unit, [target_ref] * count, lambda i: which[i] * each).astype(F32)
             dlogits.append((signed * jax.nn.sigmoid(jnp.where(signed < 0, -x, x))).astype(BF16))
-        grad = jnp.dot(
-            jnp.concatenate(dlogits, 1),
-            jnp.concatenate([ref[...] for ref in emb_refs], 0),
-            preferred_element_type=F32,
+        joined = jnp.concatenate(dlogits, 1)
+        grad = jnp.concatenate(
+            [
+                jnp.dot(
+                    joined,
+                    jnp.concatenate([ref[:, n : n + 256] for ref in emb_refs], 0),
+                    preferred_element_type=F32,
+                )
+                for n in range(0, emb_refs[0].shape[1], 256)
+            ],
+            1,
         )
         off = 0
         for i, start, rows in unit:

time: 30.3 us -> 30.3 us (level)
  no operation moved by 1% of the time
where the time goes in v13:
time: 30.3 us; the launch traced here: 30.1 us
  starting transfers between devices  14.2 us (47%)
  waiting for transfers between devices  7.66 us (25%)
  Pallas kernels  7.37 us (24%)
  between operations  0.72 us (2%)
    ppermute x12, starting transfers between devices, flip(): lax.ppermute(value, axis, [(i, i ^ mask) for i in range(lax.axis_size(axi...  14.2 us
    ppermute x12, waiting for transfers between devices, flip(): lax.ppermute(value, axis, [(i, i ^ mask) for i in range(lax.axis_size(axi...  7.66 us
    pallas_call x1, Pallas kernels, shards(): pl.pallas_call(emb_kernel, out_shape=jax.ShapeDtypeStruct((docs, width),...  1.74 us
    pallas_call x2, Pallas kernels, score(): pl.pallas_call(functools.partial(score_kernel, which=which, after=len(aft...  1.44 us
    pallas_call x1, Pallas kernels, shards(): pl.pallas_call(turn_kernel, out_shape=[jax.ShapeDtypeStruct((docs, width)...  1.41 us
    pallas_call x1, Pallas kernels, shards(): pl.pallas_call(functools.partial(pack_kernel, scale=1.0 / math.sqrt(docs...  1.15 us
    pallas_call x1, Pallas kernels, shards(): pl.pallas_call(functools.partial(targets_kernel, panel=panel, slots=slots...  0.82 us
    pallas_call x1, Pallas kernels, shards(): pl.pallas_call(finish_kernel, out_shape=jax.ShapeDtypeStruct((panel, widt...  0.76 us
  transfers between devices with their start and end apart: 12, of which 5 were waited for; matrix products, arithmetic and copies ran while one was open for 0% of the time, Pallas kernels for 22%

profile of v13, /device:TPU:0, one launch (start us, length us, event | category | flops | bytes accessed | tf_op | source)
XLA Modules:
  0.0 30.1 jit_solution(4409835358556255667)
XLA Ops:
  0.6 0.5 %collective-permute-start.1 = (bf16[512,768]{1,0:T(8,128)(2,1)}, bf16[512,768]{1,0:T(8,128)(2,1)S(1)}, u32[]{:S(2)}, u32[]{:S(2)}) collective-permute-start(bf16[512,768]{1,0:T(8,128)(2,1)} %emb_hbm.1), channel_id=1, source_target_pairs={{0,1},{1,0},{2,3},{3,2},{4,5},{5,4},{6,7},{7,6},{8,9},{9,8},{10,11... | collective-permute-start | bytes 2359304 | tf_op jit(solution)/shard_map/ppermute | solution.py:20
  1.1 1.1 %pack.1 = (bf16[64,768]{1,0:T(8,128)(2,1)S(1)}, f32[64,128]{1,0:T(8,128)S(1)}, bf16[40,512]{1,0:T(8,128)(2,1)S(1)}) custom-call(f32[64,768]{1,0:T(8,128)} %classifier_hbm.1, s32[1,64]{1,0:T(1,128)} %bitcast.9, s32[4,512]{1,0:T(4,128)} %bitcast.6, s32[4,512]{1,0:T(4,128)} %bitcast.7, s32[4,512]{1,0:T(4,128)} %bitcast.8, s32[4,8,512]{2,1,0:T(8,128)} %bitcast.5), custom_call_target="tpu_custom_call" | custom-call | flops 49152 | bytes 376832 | tf_op jit(solution)/shard_map/pack/pallas_call | solution.py:219
  2.3 3.5 %collective-permute-start = (bf16[64,768]{1,0:T(8,128)(2,1)S(1)}, bf16[64,768]{1,0:T(8,128)(2,1)S(1)}, u32[]{:S(2)}, u32[]{:S(2)}) collective-permute-start(bf16[64,768]{1,0:T(8,128)(2,1)S(1)} %get-tuple-element.25.refs_1_), channel_id=1, source_target_pairs={{0,6},{1,7},{2,4},{3,5},{4,2},{5,3},{6,0},{7,1},{8,14},{9,15},{10,... | collective-permute-start | bytes 294920 | tf_op jit(solution)/shard_map/ppermute | solution.py:20
  5.8 0.2 collective-permute-start.2
  6.0 0.5 %collective-permute-start.5 = (bf16[64,768]{1,0:T(8,128)(2,1)S(1)}, bf16[64,768]{1,0:T(8,128)(2,1)S(1)}, u32[]{:S(2)}, u32[]{:S(2)}) collective-permute-start(bf16[64,768]{1,0:T(8,128)(2,1)S(1)} %get-tuple-element.25.refs_1_), channel_id=1, source_target_pairs={{0,4},{1,5},{2,6},{3,7},{4,0},{5,1},{6,2},{7,3},{8,12},{9,13},{10,... | collective-permute-start | bytes 294920 | tf_op jit(solution)/shard_map/ppermute | solution.py:20
  6.5 0.4 %collective-permute-start.4 = (bf16[64,768]{1,0:T(8,128)(2,1)S(1)}, bf16[64,768]{1,0:T(8,128)(2,1)S(1)}, u32[]{:S(2)}, u32[]{:S(2)}) collective-permute-start(bf16[64,768]{1,0:T(8,128)(2,1)S(1)} %get-tuple-element.25.refs_1_), channel_id=1, source_target_pairs={{0,2},{1,3},{2,0},{3,1},{4,6},{5,7},{6,4},{7,5},{8,10},{9,11},{10,... | collective-permute-start | bytes 294920 | tf_op jit(solution)/shard_map/ppermute | solution.py:20
  7.0 0.0 collective-permute-done.1.other_ref.refs_3_
  7.0 1.4 %turn.1 = (bf16[512,768]{1,0:T(8,128)(2,1)S(1)}, bf16[768,512]{1,0:T(8,128)(2,1)S(1)}, bf16[768,512]{1,0:T(8,128)(2,1)S(1)}) custom-call(bf16[512,768]{1,0:T(8,128)(2,1)} %emb_hbm.1, bf16[512,768]{1,0:T(8,128)(2,1)S(1)} %collective-permute-done.1.other_ref.refs_3_), custom_call_target="tpu_custom_call" | custom-call | flops 393216 | bytes 3932160 | tf_op jit(solution)/shard_map/turn/pallas_call | solution.py:247
  8.4 0.0 collective-permute-done.2.index_other_ref
  8.4 0.8 %targets.1 = (bf16[256,512]{1,0:T(8,128)(2,1)S(1)}, bf16[256,512]{1,0:T(8,128)(2,1)S(1)}) custom-call(bf16[40,512]{1,0:T(8,128)(2,1)S(1)} %get-tuple-element.29.index_own_ref, bf16[40,512]{1,0:T(8,128)(2,1)S(1)} %collective-permute-done.2.index_other_ref, bf16[768,512]{1,0:T(8,128)(2,1)S(1)} %get-tuple-element.28.after_ref.refs_5_), custom_call_target="tpu_custom_call" | custom-call | flops 10485760 | bytes 688128 | tf_op jit(solution)/shard_map/targets/pallas_call | solution.py:258
  9.2 0.1 collective-permute-done.refs_0_
  9.3 0.7 %score.2 = (bf16[64,768]{1,0:T(8,128)(2,1)S(1)}, f32[64,768]{1,0:T(8,128)S(1)}, bf16[64,512]{1,0:T(8,128)(2,1)S(1)}, bf16[64,512]{1,0:T(8,128)(2,1)S(1)}, bf16[6...) custom-call(bf16[64,768]{1,0:T(8,128)(2,1)S(1)} %collective-permute-done.refs_0_, ...), custom_call_target="tpu_custom_call" | custom-call | flops 402653184 | bytes 4456448 | tf_op jit(solution)/shard_map/score/pallas_call | solution.py:273
  10.1 3.1 %collective-permute-start.3 = (bf16[65,768]{1,0:T(8,128)(2,1)S(1)}, bf16[65,768]{1,0:T(8,128)(2,1)S(1)}, u32[]{:S(2)}, u32[]{:S(2)}) collective-permute-start(bf16[65,768]{1,0:T(8,128)(2,1)S(1)} %pad_maximum_fusion), channel_id=1, source_target_pairs={{0,6},{1,7},{2,4},{3,5},{4,2},{5,3},{6,0},{7,1},{8,14},{9,15},{10,... | collective-permute-start | bytes 299528 | tf_op jit(solution)/shard_map/ppermute | solution.py:20
  13.2 0.0 collective-permute-done.5.refs_1_.refs_3_
  13.2 0.0 collective-permute-done.4.refs_0_.refs_2_
  13.2 0.7 %score.3 = (bf16[64,768]{1,0:T(8,128)(2,1)S(1)}, bf16[64,768]{1,0:T(8,128)(2,1)S(1)}, bf16[64,512]{1,0:T(8,128)(2,1)S(1)}, bf16[64,512]{1,0:T(8,128)(2,1)S(1)}, ...) custom-call(bf16[64,768]{1,0:T(8,128)(2,1)S(1)} %collective-permute-done.4.refs_0_.refs_2_, ...), custom_call_target="tpu_custom_call" | custom-call | flops 402653184 | bytes 4456448 | tf_op jit(solution)/shard_map/score/pallas_call | solution.py:273
  13.9 0.4 %collective-permute-start.6 = (bf16[64,768]{1,0:T(8,128)(2,1)S(1)}, bf16[64,768]{1,0:T(8,128)(2,1)S(1)}, u32[]{:S(2)}, u32[]{:S(2)}) collective-permute-start(bf16[64,768]{1,0:T(8,128)(2,1)S(1)} %get-tuple-element.34), channel_id=1, source_target_pairs={{0,4},{1,5},{2,6},{3,7},{4,0},{5,1},{6,2},{7,3},{8,12},{9,13},{10,... | collective-permute-start | bytes 294920 | tf_op jit(solution)/shard_map/ppermute | solution.py:20
  14.3 0.5 %collective-permute-start.7 = (bf16[64,768]{1,0:T(8,128)(2,1)S(1)}, bf16[64,768]{1,0:T(8,128)(2,1)S(1)}, u32[]{:S(2)}, u32[]{:S(2)}) collective-permute-start(bf16[64,768]{1,0:T(8,128)(2,1)S(1)} %get-tuple-element.35), channel_id=1, source_target_pairs={{0,2},{1,3},{2,0},{3,1},{4,6},{5,7},{6,4},{7,5},{8,10},{9,11},{10,... | collective-permute-start | bytes 294920 | tf_op jit(solution)/shard_map/ppermute | solution.py:20
  14.8 3.9 %collective-permute-done.6 = bf16[64,768]{1,0:T(8,128)(2,1)S(1)} collective-permute-done((bf16[64,768]{1,0:T(8,128)(2,1)S(1)}, bf16[64,768]{1,0:T(8,128)(2,1)S(1)}, u32[]{:S(2)}, u32[]{:S(2)}) %collective-permute-start.6) | collective-permute-done | bytes 98336 | tf_op jit(solution)/shard_map/ppermute | solution.py:20
  18.6 0.3 %collective-permute-done.7 = bf16[64,768]{1,0:T(8,128)(2,1)S(1)} collective-permute-done((bf16[64,768]{1,0:T(8,128)(2,1)S(1)}, bf16[64,768]{1,0:T(8,128)(2,1)S(1)}, u32[]{:S(2)}, u32[]{:S(2)}) %collective-permute-start.7) | collective-permute-done | bytes 98336 | tf_op jit(solution)/shard_map/ppermute | solution.py:20
  18.9 0.0 collective-permute-done.3
  19.0 1.6 %collective-permute-start.8 = (bf16[64,768]{1,0:T(8,128)(2,1)S(1)}, bf16[64,768]{1,0:T(8,128)(2,1)S(1)}, u32[]{:S(2)}, u32[]{:S(2)}) collective-permute-start(bf16[64,768]{1,0:T(8,128)(2,1)S(1)} %fusion), channel_id=1, source_target_pairs={{0,8},{8,0},{16,24},{24,16},{1,9},{9,1},{17,25},{25,17},{2,10},{10... | collective-permute-start | bytes 294920 | tf_op jit(solution)/shard_map/ppermute | solution.py:20
  20.6 0.1 join.1
  20.7 0.1 collective-permute-start.11
  20.8 0.5 %collective-permute-start.10 = (bf16[256,512]{1,0:T(8,128)(2,1)S(1)}, bf16[256,512]{1,0:T(8,128)(2,1)S(1)}, u32[]{:S(2)}, u32[]{:S(2)}) collective-permute-start(bf16[256,512]{1,0:T(8,128)(2,1)S(1)} %get-tuple-element.46), channel_id=1, source_target_pairs={{0,1},{1,0},{2,3},{3,2},{4,5},{5,4},{6,7},{7,6},{8,9},{9,8},{10,11... | collective-permute-start | bytes 786440 | tf_op jit(solution)/shard_map/ppermute | solution.py:20
  21.3 2.4 %collective-permute-done.8 = bf16[64,768]{1,0:T(8,128)(2,1)S(1)} collective-permute-done((bf16[64,768]{1,0:T(8,128)(2,1)S(1)}, bf16[64,768]{1,0:T(8,128)(2,1)S(1)}, u32[]{:S(2)}, u32[]{:S(2)}) %collective-permute-start.8) | collective-permute-done | bytes 98336 | tf_op jit(solution)/shard_map/ppermute | solution.py:20
  23.7 0.1 fusion.1
  23.7 2.9 %collective-permute-start.9 = (bf16[64,768]{1,0:T(8,128)(2,1)S(1)}, bf16[64,768]{1,0:T(8,128)(2,1)S(1)}, u32[]{:S(2)}, u32[]{:S(2)}) collective-permute-start(bf16[64,768]{1,0:T(8,128)(2,1)S(1)} %get-tuple-element.48), channel_id=1, source_target_pairs={{0,16},{8,24},{16,0},{24,8},{1,17},{9,25},{17,1},{25,9},{2,18},{10... | collective-permute-start | bytes 294920 | tf_op jit(solution)/shard_map/ppermute | solution.py:20
  26.6 0.0 collective-permute-done.10.d_other_ref
  26.6 0.0 collective-permute-done.11.c_other_ref
  26.6 1.7 %emb_grad.1.after_hbm = f32[512,768]{1,0:T(8,128)} custom-call(bf16[256,512]{1,0:T(8,128)(2,1)S(1)} %get-tuple-element.45.d_own_ref, bf16[256,512]{1,0:T(8,128)(2,1)S(1)} %collective-permute-done.10.d_other_ref, bf16[256,768]{1,0:T(8,128)(2,1)S(1)} %get-tuple-element.47.c_own_ref, bf16[256,768]{1,0:T(8,128)(2,1)S(1)} %collective-permute-done.11.c_other_ref, ...), custom_call_target="tpu_custom_call" | custom-call | flops 402653184 | bytes 2883584 | tf_op jit(solution)/shard_map/emb_grad/pallas_call | solution.py:331
  28.3 1.0 %collective-permute-done.9.received_ref = bf16[64,768]{1,0:T(8,128)(2,1)S(1)} collective-permute-done((bf16[64,768]{1,0:T(8,128)(2,1)S(1)}, bf16[64,768]{1,0:T(8,128)(2,1)S(1)}, u32[]{:S(2)}, u32[]{:S(2)}) %collective-permute-start.9) | collective-permute-done | bytes 98336 | tf_op jit(solution)/shard_map/ppermute | solution.py:20
  29.3 0.8 %finish.1 = f32[64,768]{1,0:T(8,128)} custom-call(f32[64,768]{1,0:T(8,128)S(1)} %get-tuple-element.49.after_ref.grad_ref, bf16[64,768]{1,0:T(8,128)(2,1)S(1)} %collective-permute-done.9.received_ref, f32[64,128]{1,0:T(8,128)S(1)} %get-tuple-element.36.column_ref, f32[512,768]{1,0:T(8,128)} %emb_grad.1.after_hbm), custom_call_target="tpu_custom_call" | custom-call | flops 49152 | bytes 491520 | tf_op jit(solution)/shard_map/finish/pallas_call | solution.py:341
  (3 shorter events, 0.1 us)
Async XLA Ops:
  0.6 6.3 %collective-permute-start.1 = (bf16[512,768]{1,0:T(8,128)(2,1)}, bf16[512,768]{1,0:T(8,128)(2,1)S(1)}, u32[]{:S(2)}, u32[]{:S(2)}) collective-permute-start(bf16[512,768]{1,0:T(8,128)(2,1)} %emb_hbm.1), channel_id=1, source_target_pairs={{0,1},{1,0},{2,3},{3,2},{4,5},{5,4},{6,7},{7,6},{8,9},{9,8},{10,11... | collective-permute-start | bytes 2359304 | tf_op jit(solution)/shard_map/ppermute | solution.py:20
  2.3 7.0 %collective-permute-start = (bf16[64,768]{1,0:T(8,128)(2,1)S(1)}, bf16[64,768]{1,0:T(8,128)(2,1)S(1)}, u32[]{:S(2)}, u32[]{:S(2)}) collective-permute-start(bf16[64,768]{1,0:T(8,128)(2,1)S(1)} %get-tuple-element.25.refs_1_), channel_id=1, source_target_pairs={{0,6},{1,7},{2,4},{3,5},{4,2},{5,3},{6,0},{7,1},{8,14},{9,15},{10,... | collective-permute-start | bytes 294920 | tf_op jit(solution)/shard_map/ppermute | solution.py:20
  5.8 2.6 %collective-permute-start.2 = (bf16[40,512]{1,0:T(8,128)(2,1)S(1)}, bf16[40,512]{1,0:T(8,128)(2,1)S(1)}, u32[]{:S(2)}, u32[]{:S(2)}) collective-permute-start(bf16[40,512]{1,0:T(8,128)(2,1)S(1)} %get-tuple-element.29.index_own_ref), channel_id=1, source_target_pairs={{0,1},{1,0},{2,3},{3,2},{4,5},{5,4},{6,7},{7,6},{8,9},{9,8},{10,11... | collective-permute-start | bytes 122888 | tf_op jit(solution)/shard_map/ppermute | solution.py:20
  6.0 7.2 %collective-permute-start.5 = (bf16[64,768]{1,0:T(8,128)(2,1)S(1)}, bf16[64,768]{1,0:T(8,128)(2,1)S(1)}, u32[]{:S(2)}, u32[]{:S(2)}) collective-permute-start(bf16[64,768]{1,0:T(8,128)(2,1)S(1)} %get-tuple-element.25.refs_1_), channel_id=1, source_target_pairs={{0,4},{1,5},{2,6},{3,7},{4,0},{5,1},{6,2},{7,3},{8,12},{9,13},{10,... | collective-permute-start | bytes 294920 | tf_op jit(solution)/shard_map/ppermute | solution.py:20
  6.5 6.7 %collective-permute-start.4 = (bf16[64,768]{1,0:T(8,128)(2,1)S(1)}, bf16[64,768]{1,0:T(8,128)(2,1)S(1)}, u32[]{:S(2)}, u32[]{:S(2)}) collective-permute-start(bf16[64,768]{1,0:T(8,128)(2,1)S(1)} %get-tuple-element.25.refs_1_), channel_id=1, source_target_pairs={{0,2},{1,3},{2,0},{3,1},{4,6},{5,7},{6,4},{7,5},{8,10},{9,11},{10,... | collective-permute-start | bytes 294920 | tf_op jit(solution)/shard_map/ppermute | solution.py:20
  10.1 8.9 %collective-permute-start.3 = (bf16[65,768]{1,0:T(8,128)(2,1)S(1)}, bf16[65,768]{1,0:T(8,128)(2,1)S(1)}, u32[]{:S(2)}, u32[]{:S(2)}) collective-permute-start(bf16[65,768]{1,0:T(8,128)(2,1)S(1)} %pad_maximum_fusion), channel_id=1, source_target_pairs={{0,6},{1,7},{2,4},{3,5},{4,2},{5,3},{6,0},{7,1},{8,14},{9,15},{10,... | collective-permute-start | bytes 299528 | tf_op jit(solution)/shard_map/ppermute | solution.py:20
  13.9 4.7 %collective-permute-start.6 = (bf16[64,768]{1,0:T(8,128)(2,1)S(1)}, bf16[64,768]{1,0:T(8,128)(2,1)S(1)}, u32[]{:S(2)}, u32[]{:S(2)}) collective-permute-start(bf16[64,768]{1,0:T(8,128)(2,1)S(1)} %get-tuple-element.34), channel_id=1, source_target_pairs={{0,4},{1,5},{2,6},{3,7},{4,0},{5,1},{6,2},{7,3},{8,12},{9,13},{10,... | collective-permute-start | bytes 294920 | tf_op jit(solution)/shard_map/ppermute | solution.py:20
  14.3 4.6 %collective-permute-start.7 = (bf16[64,768]{1,0:T(8,128)(2,1)S(1)}, bf16[64,768]{1,0:T(8,128)(2,1)S(1)}, u32[]{:S(2)}, u32[]{:S(2)}) collective-permute-start(bf16[64,768]{1,0:T(8,128)(2,1)S(1)} %get-tuple-element.35), channel_id=1, source_target_pairs={{0,2},{1,3},{2,0},{3,1},{4,6},{5,7},{6,4},{7,5},{8,10},{9,11},{10,... | collective-permute-start | bytes 294920 | tf_op jit(solution)/shard_map/ppermute | solution.py:20
  19.0 4.7 %collective-permute-start.8 = (bf16[64,768]{1,0:T(8,128)(2,1)S(1)}, bf16[64,768]{1,0:T(8,128)(2,1)S(1)}, u32[]{:S(2)}, u32[]{:S(2)}) collective-permute-start(bf16[64,768]{1,0:T(8,128)(2,1)S(1)} %fusion), channel_id=1, source_target_pairs={{0,8},{8,0},{16,24},{24,16},{1,9},{9,1},{17,25},{25,17},{2,10},{10... | collective-permute-start | bytes 294920 | tf_op jit(solution)/shard_map/ppermute | solution.py:20
  20.7 5.9 %collective-permute-start.11 = (bf16[256,768]{1,0:T(8,128)(2,1)S(1)}, bf16[256,768]{1,0:T(8,128)(2,1)S(1)}, u32[]{:S(2)}, u32[]{:S(2)}) collective-permute-start(bf16[256,768]{1,0:T(8,128)(2,1)S(1)} %get-tuple-element.47.c_own_ref), channel_id=1, source_target_pairs={{0,1},{1,0},{2,3},{3,2},{4,5},{5,4},{6,7},{7,6},{8,9},{9,8},{10,11... | collective-permute-start | bytes 1179656 | tf_op jit(solution)/shard_map/ppermute | solution.py:20
  20.8 5.8 %collective-permute-start.10 = (bf16[256,512]{1,0:T(8,128)(2,1)S(1)}, bf16[256,512]{1,0:T(8,128)(2,1)S(1)}, u32[]{:S(2)}, u32[]{:S(2)}) collective-permute-start(bf16[256,512]{1,0:T(8,128)(2,1)S(1)} %get-tuple-element.46), channel_id=1, source_target_pairs={{0,1},{1,0},{2,3},{3,2},{4,5},{5,4},{6,7},{7,6},{8,9},{9,8},{10,11... | collective-permute-start | bytes 786440 | tf_op jit(solution)/shard_map/ppermute | solution.py:20
  23.7 5.6 %collective-permute-start.9 = (bf16[64,768]{1,0:T(8,128)(2,1)S(1)}, bf16[64,768]{1,0:T(8,128)(2,1)S(1)}, u32[]{:S(2)}, u32[]{:S(2)}) collective-permute-start(bf16[64,768]{1,0:T(8,128)(2,1)S(1)} %get-tuple-element.48), channel_id=1, source_target_pairs={{0,16},{8,24},{16,0},{24,8},{1,17},{9,25},{17,1},{25,9},{2,18},{10... | collective-permute-start | bytes 294920 | tf_op jit(solution)/shard_map/ppermute | solution.py:20
